TPU v7x, 32 devices: a whole 2x2x4 slice. The times are simulated.
32 devices in a mesh: expert: 2 (over x), context: 4 (over y, core), dp: 4 (over z).
Axes of the slice: x: 2, y: 2, z: 4, core: 2. Of those that a mesh axis runs over, the one named last changes fastest.
Arguments:
- hidden_in: bfloat16 [8, 1024, 1536], P(('expert', 'dp'), 'context'), may hold values from -6 to 6
- span_order: int32 [8, 8], P(('expert', 'dp')), may hold values from 0 to 7, each once within a row
- expert_ids: int32 [8, 1024, 4], P(('expert', 'dp'), 'context'), may hold values from 0 to 7, all different within a row
- priority: int32 [8, 1024, 4], P(('expert', 'dp'), 'context'), may hold values from 0 to 1023, as said below
- gain_attn: float32 [1536], replicated, may hold values from 0.1 to 1.9
- qkv_weight: bfloat16 [1536, 2048], replicated, may hold values from -0.15625 to 0.15625
- out_weight: bfloat16 [1536, 1536], replicated, may hold values from -0.625 to 0.625
- gain_ffn: float32 [1536], replicated, may hold values from 0.1 to 1.9
- router: bfloat16 [1536, 8], replicated, may hold values from -0.078125 to 0.078125
- in_weight: bfloat16 [8, 1536, 1536], P('expert'), may hold values from -0.15625 to 0.15625
- down_weight: bfloat16 [8, 1536, 768], P('expert'), may hold values from -0.4375 to 0.4375
- cotangent: bfloat16 [8, 1024, 1536], P(('expert', 'dp'), 'context'), may hold values from -6 to 6
Outputs:
- output: bfloat16 [8, 1024, 1536], P(('expert', 'dp'), 'context')
- input_grad: bfloat16 [8, 1024, 1536], P(('expert', 'dp'), 'context')
- gain_attn_grad: float32 [1536], P(('expert', 'context', 'dp'))
- qkv_grad: float32 [1536, 2048], P(('expert', 'context', 'dp'))
- out_proj_grad: float32 [1536, 1536], P(('expert', 'context', 'dp'))
- gain_ffn_grad: float32 [1536], P(('expert', 'context', 'dp'))
- router_grad: float32 [1536, 8], P(('expert', 'context', 'dp'))
- expert_in_grad: float32 [8, 1536, 1536], P('expert', ('context', 'dp'))
- expert_down_grad: float32 [8, 1536, 768], P('expert', ('context', 'dp'))
Inputs may be any that keep to these rules, and one draw needn't show every extreme that they name: `priority`: within each device's block (256 stored rows of one sequence) the 4 entries of all its tokens are a permutation of 0 to 1023. `expert_ids`: each token names 4 different experts. `span_order`: each row is a permutation.
All inputs are finite; a program needn't handle non-finite values.
Results may differ from a plain program's by a relative error of at most 0.022.
Values may be sent and summed in bfloat16 or wider, within the bound.
A program may use at most 320 MiB of HBM per device.

v0:
```python
import jax
import jax.numpy as jnp
from jax import lax
from jax.sharding import PartitionSpec as P

HEADS = 12
KV_HEADS = 2
HEAD = 128


ROPE_BASE = 1000000.0
NORM_EPS = 1e-06
MASKED = -1e30


def rope_tables(positions, head_size):
    half_size = head_size // 2
    freqs = ROPE_BASE ** (jnp.arange(half_size).astype(jnp.float32) * (-2.0 / head_size))
    angles = positions[:, None] * freqs[None, :]
    return (jnp.cos(angles)[:, None, :], jnp.sin(angles)[:, None, :])


def rotate(values, cosine, sine):
    half_size = values.shape[-1] // 2
    first = values[..., :half_size]
    second = values[..., half_size:]
    return jnp.concatenate(
        [first * cosine - second * sine, second * cosine + first * sine], axis=-1
    )


def unrotate(values, cosine, sine):
    half_size = values.shape[-1] // 2
    first = values[..., :half_size]
    second = values[..., half_size:]
    return jnp.concatenate(
        [first * cosine + second * sine, second * cosine - first * sine], axis=-1
    )


def softmax_last(scores):
    shifted = jnp.exp(scores - jnp.max(scores, axis=-1, keepdims=True))
    return shifted / jnp.sum(shifted, axis=-1, keepdims=True)


def route(block_ids, block_order, n_experts, capacity):
    flat_ids = block_ids.reshape(-1)
    flat_order = block_order.reshape(-1)
    choose = (flat_ids[:, None] == jnp.arange(n_experts)[None, :]).astype(jnp.int32)
    ordered = jnp.zeros_like(choose).at[flat_order].set(choose)
    earlier = jnp.cumsum(ordered, axis=0, dtype=jnp.int32) - ordered
    ranks = jnp.sum(earlier[flat_order] * choose, axis=1)
    return jnp.where(ranks < capacity, flat_ids * capacity + ranks, n_experts * capacity)


def local(
    hidden_in,
    span_order,
    expert_ids,
    priority,
    gain_attn,
    qkv_weight,
    out_weight,
    gain_ffn,
    router,
    in_weight,
    down_weight,
    cotangent,
):
    tok_rows = hidden_in.shape[1]
    width = hidden_in.shape[2]
    contexts = lax.axis_size("context")
    span_len = tok_rows // 2
    seq_len = tok_rows * contexts
    group = HEADS // KV_HEADS
    q_cols = HEADS * HEAD
    kv_cols = KV_HEADS * HEAD
    scale = HEAD ** (-0.5)
    local_experts = in_weight.shape[0]
    n_experts = local_experts * lax.axis_size("expert")
    top_k = expert_ids.shape[2]
    capacity = (9 * tok_rows * top_k + 8 * n_experts - 1) // (8 * n_experts)
    ff_width = down_weight.shape[2]
    seq_spans = span_order[0]
    stored = jnp.arange(seq_len) // span_len
    all_pos = (seq_spans[stored] * span_len + jnp.arange(seq_len) % span_len).astype(jnp.float32)
    my_pos = lax.dynamic_slice_in_dim(all_pos, lax.axis_index("context") * tok_rows, tok_rows)
    cosine, sine = rope_tables(my_pos, HEAD)
    inputs = hidden_in[0].astype(jnp.float32)
    inv_one = lax.rsqrt(jnp.mean(inputs * inputs, axis=-1, keepdims=True) + NORM_EPS)
    plain_one = inputs * inv_one
    normed = (plain_one * gain_attn).astype(jnp.bfloat16)
    mixed = jnp.dot(normed, qkv_weight, preferred_element_type=jnp.float32)
    queries = (
        rotate(mixed[:, :q_cols].reshape(tok_rows, HEADS, HEAD), cosine, sine) * scale
    ).astype(jnp.bfloat16)
    keys = rotate(
        mixed[:, q_cols : q_cols + kv_cols].reshape(tok_rows, KV_HEADS, HEAD), cosine, sine
    ).astype(jnp.bfloat16)
    values = mixed[:, q_cols + kv_cols :].reshape(tok_rows, KV_HEADS, HEAD).astype(jnp.bfloat16)
    grouped = queries.reshape(tok_rows, KV_HEADS, group, HEAD)

    def key_scores(key_piece):
        scores = jnp.einsum(
            "qkgd,skd->kgqs", grouped, key_piece, preferred_element_type=jnp.float32
        )
        visible = all_pos[None, None, None, :] <= my_pos[None, None, :, None]
        return (jnp.where(visible, scores, MASKED), visible)

    running = jnp.full((KV_HEADS, group, tok_rows), MASKED, jnp.float32)
    key_piece = lax.all_gather(keys, "context", axis=0, tiled=True)
    value_piece = lax.all_gather(values, "context", axis=0, tiled=True)
    scores, visible = key_scores(key_piece)
    newest = jnp.maximum(running, jnp.max(scores, axis=-1))
    weights = jnp.where(visible, jnp.exp(scores - newest[..., None]), 0.0)
    totals = jnp.sum(weights, axis=-1)
    accum = jnp.einsum(
        "kgqs,skd->kgqd",
        weights.astype(jnp.bfloat16),
        value_piece,
        preferred_element_type=jnp.float32,
    )
    running, totals, accum = (newest, totals, accum)
    log_total = running + jnp.log(totals)
    attended = (
        (accum / totals[..., None])
        .transpose(2, 0, 1, 3)
        .reshape(tok_rows, q_cols)
        .astype(jnp.bfloat16)
    )
    resid = inputs + jnp.einsum(
        "rh,dh->rd", attended, out_weight, preferred_element_type=jnp.float32
    )
    inv_two = lax.rsqrt(jnp.mean(resid * resid, axis=-1, keepdims=True) + NORM_EPS)
    plain_two = resid * inv_two
    ffn_in = (plain_two * gain_ffn).astype(jnp.bfloat16)
    logits = jnp.dot(ffn_in, router, preferred_element_type=jnp.float32)
    token_ids = expert_ids[0]
    gates = softmax_last(jnp.take_along_axis(logits, token_ids, axis=1))
    slots = route(token_ids, priority[0], n_experts, capacity)
    pair_rows = jnp.repeat(ffn_in, top_k, axis=0)
    send_rows = (
        jnp.zeros((n_experts * capacity, width), jnp.bfloat16).at[slots].set(pair_rows, mode="drop")
    )
    received = lax.all_to_all(
        send_rows.reshape(n_experts, capacity, width),
        "expert",
        split_axis=0,
        concat_axis=1,
        tiled=True,
    )
    inner = jnp.einsum("erd,edf->erf", received, in_weight, preferred_element_type=jnp.float32)
    gate_part = inner[..., :ff_width]
    up_part = inner[..., ff_width:]
    sigma = 1.0 / (1.0 + jnp.exp(-gate_part))
    activated = gate_part * sigma
    hidden = (activated * up_part).astype(jnp.bfloat16)
    expert_out = jnp.einsum(
        "erf,edf->erd", hidden, down_weight, preferred_element_type=jnp.float32
    ).astype(jnp.bfloat16)
    returned = lax.all_to_all(
        expert_out, "expert", split_axis=1, concat_axis=0, tiled=True
    ).reshape(n_experts * capacity, width)
    padded = jnp.concatenate([returned, jnp.zeros((1, width), jnp.bfloat16)], axis=0)
    picked = padded[slots].reshape(tok_rows, top_k, width)
    output = (resid + jnp.sum(gates[:, :, None] * picked, axis=1)).astype(jnp.bfloat16)
    cot_low = cotangent[0]
    cot_full = cot_low.astype(jnp.float32)
    gate_grad = jnp.einsum("rkd,rd->rk", picked, cot_low, preferred_element_type=jnp.float32)
    ret_grad = (
        (gates[:, :, None] * cot_full[:, None, :])
        .astype(jnp.bfloat16)
        .reshape(tok_rows * top_k, width)
    )
    send_grad = (
        jnp.zeros((n_experts * capacity, width), jnp.bfloat16).at[slots].set(ret_grad, mode="drop")
    )
    received_grad = lax.all_to_all(
        send_grad.reshape(n_experts, capacity, width),
        "expert",
        split_axis=0,
        concat_axis=1,
        tiled=True,
    )
    hid_grad = jnp.einsum(
        "erd,edf->erf", received_grad, down_weight, preferred_element_type=jnp.float32
    )
    slope = sigma * (1.0 + gate_part * (1.0 - sigma))
    inner_grad = jnp.concatenate(
        [hid_grad * up_part * slope, hid_grad * activated], axis=-1
    ).astype(jnp.bfloat16)
    row_grad = jnp.einsum(
        "erf,edf->erd", inner_grad, in_weight, preferred_element_type=jnp.float32
    ).astype(jnp.bfloat16)
    part_rows = received
    expert_in = (
        lax.psum_scatter(
            jnp.einsum(
                "erd,erf->def", part_rows, inner_grad, preferred_element_type=jnp.float32
            ).astype(jnp.bfloat16),
            ("context", "dp"),
            scatter_dimension=0,
            tiled=True,
        )
        .astype(jnp.float32)
        .transpose(1, 0, 2)
    )
    part_rows = received_grad
    expert_down = (
        lax.psum_scatter(
            jnp.einsum(
                "erd,erf->def", part_rows, hidden, preferred_element_type=jnp.float32
            ).astype(jnp.bfloat16),
            ("context", "dp"),
            scatter_dimension=0,
            tiled=True,
        )
        .astype(jnp.float32)
        .transpose(1, 0, 2)
    )
    back_rows = lax.all_to_all(row_grad, "expert", split_axis=1, concat_axis=0, tiled=True).reshape(
        n_experts * capacity, width
    )
    back_padded = jnp.concatenate([back_rows, jnp.zeros((1, width), jnp.bfloat16)], axis=0)
    pair_grad = back_padded[slots].reshape(tok_rows, top_k, width)
    mix_grad = gates * (gate_grad - jnp.sum(gates * gate_grad, axis=-1, keepdims=True))
    matches = token_ids[:, :, None] == jnp.arange(n_experts)[None, None, :]
    logit_grad = jnp.sum(jnp.where(matches, mix_grad[:, :, None], 0.0), axis=1).astype(jnp.bfloat16)
    router_part = jnp.einsum("rd,re->de", ffn_in, logit_grad, preferred_element_type=jnp.float32)
    ffn_grad = jnp.sum(pair_grad.astype(jnp.float32), axis=1) + jnp.einsum(
        "re,de->rd", logit_grad, router, preferred_element_type=jnp.float32
    )
    gain_ffn_part = jnp.sum(ffn_grad * plain_two, axis=0)
    scaled_two = ffn_grad * gain_ffn
    resid_grad = cot_full + inv_two * (
        scaled_two - plain_two * jnp.mean(scaled_two * plain_two, axis=-1, keepdims=True)
    )
    resid_low = resid_grad.astype(jnp.bfloat16)
    out_part = jnp.einsum("rd,rh->dh", resid_low, attended, preferred_element_type=jnp.float32)
    att_grad = jnp.einsum(
        "rd,dh->rh", resid_low, out_weight, preferred_element_type=jnp.float32
    ).astype(jnp.bfloat16)
    att_heads = att_grad.reshape(tok_rows, KV_HEADS, group, HEAD)
    row_delta = jnp.sum(
        att_heads.astype(jnp.float32)
        * attended.reshape(tok_rows, KV_HEADS, group, HEAD).astype(jnp.float32),
        axis=-1,
    ).transpose(1, 2, 0)
    key_piece = lax.all_gather(keys, "context", axis=0, tiled=True)
    value_piece = lax.all_gather(values, "context", axis=0, tiled=True)
    scores, visible = key_scores(key_piece)
    soft = jnp.exp(scores - log_total[..., None])
    prob_grad = jnp.einsum(
        "qkgd,skd->kgqs", att_heads, value_piece, preferred_element_type=jnp.float32
    )
    score_grad = (soft * (prob_grad - row_delta[..., None])).astype(jnp.bfloat16)
    query_acc = jnp.einsum(
        "kgqs,skd->kgqd", score_grad, key_piece, preferred_element_type=jnp.float32
    )
    key_part = jnp.einsum("kgqs,qkgd->skd", score_grad, grouped, preferred_element_type=jnp.float32)
    value_part = jnp.einsum(
        "kgqs,qkgd->skd", soft.astype(jnp.bfloat16), att_heads, preferred_element_type=jnp.float32
    )
    pair_acc = jnp.stack([key_part, value_part], axis=1)
    query_acc, pair_acc = (query_acc, pair_acc)
    own_pairs = lax.psum_scatter(
        pair_acc.astype(jnp.bfloat16), "context", scatter_dimension=0, tiled=True
    ).astype(jnp.float32)
    query_grad = (
        unrotate(query_acc.transpose(2, 0, 1, 3).reshape(tok_rows, HEADS, HEAD), cosine, sine)
        * scale
    )
    key_grad = unrotate(own_pairs[:, 0], cosine, sine)
    mixed_grad = jnp.concatenate(
        [
            query_grad.reshape(tok_rows, q_cols),
            key_grad.reshape(tok_rows, kv_cols),
            own_pairs[:, 1].reshape(tok_rows, kv_cols),
        ],
        axis=-1,
    ).astype(jnp.bfloat16)
    qkv_part = jnp.einsum("rd,rc->dc", normed, mixed_grad, preferred_element_type=jnp.float32)
    norm_grad = jnp.einsum("rc,dc->rd", mixed_grad, qkv_weight, preferred_element_type=jnp.float32)
    gain_attn_part = jnp.sum(norm_grad * plain_one, axis=0)
    scaled_one = norm_grad * gain_attn
    input_grad = (
        resid_grad
        + inv_one
        * (scaled_one - plain_one * jnp.mean(scaled_one * plain_one, axis=-1, keepdims=True))
    ).astype(jnp.bfloat16)
    gain_attn_grad, qkv_grad, out_proj_grad, gain_ffn_grad, router_grad = (
        lax.psum_scatter(
            gain_attn_part, ("expert", "context", "dp"), scatter_dimension=0, tiled=True
        ),
        lax.psum_scatter(qkv_part, ("expert", "context", "dp"), scatter_dimension=0, tiled=True),
        lax.psum_scatter(out_part, ("expert", "context", "dp"), scatter_dimension=0, tiled=True),
        lax.psum_scatter(
            gain_ffn_part, ("expert", "context", "dp"), scatter_dimension=0, tiled=True
        ),
        lax.psum_scatter(router_part, ("expert", "context", "dp"), scatter_dimension=0, tiled=True),
    )
    return (
        output[None],
        input_grad[None],
        gain_attn_grad,
        qkv_grad,
        out_proj_grad,
        gain_ffn_grad,
        router_grad,
        expert_in,
        expert_down,
    )


def solution(mesh):
    in_specs = (
        P(("expert", "dp"), "context", None),
        P(("expert", "dp"), None),
        P(("expert", "dp"), "context", None),
        P(("expert", "dp"), "context", None),
        P(),
        P(),
        P(),
        P(),
        P(),
        P("expert", None, None),
        P("expert", None, None),
        P(("expert", "dp"), "context", None),
    )
    out_specs = (
        P(("expert", "dp"), "context", None),
        P(("expert", "dp"), "context", None),
        P(("expert", "context", "dp")),
        P(("expert", "context", "dp"), None),
        P(("expert", "context", "dp"), None),
        P(("expert", "context", "dp")),
        P(("expert", "context", "dp"), None),
        P("expert", ("context", "dp"), None),
        P("expert", ("context", "dp"), None),
    )
    return jax.shard_map(local, mesh=mesh, in_specs=in_specs, out_specs=out_specs, check_vma=False)
```

profile of v0, /device:TPU:0, one launch (start us, length us, event | category | flops | bytes accessed | tf_op | source)
XLA Modules:
  0.0 1077.9 jit_solution(13312081621053488858)
XLA Ops:
  12.2 4.9 fusion.69
  19.0 4.5 compare_select_fusion.5
  26.8 3.7 scatter_custom_fusion
  30.7 2.3 reduce-window.6
  35.7 4.0 gather_fusion
  44.5 2.4 multiply_subtract_fusion.1
  47.5 9.1 all_gather.8
  56.6 7.9 all_gather.9
  66.6 5.2 mul.361
  71.7 7.7 mul.362
  80.6 1.8 fusion.6
  82.4 2.5 fusion.4
  85.0 2.0 copy-done.1
  86.9 2.9 fusion.35
  89.9 4.2 multiply_reduce_fusion.4
  94.6 6.5 gather_fusion.3
  102.1 9.5 scatter_custom_fusion.2
  111.5 5.4 all-to-all-start.2
  116.9 2.5 broadcast_in_dim.102
  119.4 5.9 reshape.508
  125.3 8.6 scatter_custom_fusion.1
  133.9 24.1 %all-to-all-done.2 = bf16[8,144,1536]{2,1,0:T(8,128)(2,1)} async-done(((bf16[8,144,1536]{2,1,0:T(8,128)(2,1)}), bf16[8,144,1536]{2,1,0:T(8,128)(2,1)}, u32[]{:S(2)}, u32[]{:S(2)}) %all-to-all-start.2) | async-done | bytes 3538976 | tf_op jit(solution)/shard_map/all_to_all | solution.py:178
  158.1 5.3 all-to-all-start
  163.4 4.1 copy.179
  167.5 36.3 %all-to-all-done = bf16[8,144,1536]{2,1,0:T(8,128)(2,1)} async-done(((bf16[8,144,1536]{2,1,0:T(8,128)(2,1)}), bf16[8,144,1536]{2,1,0:T(8,128)(2,1)}, u32[]{:S(2)}, u32[]{:S(2)}) %all-to-all-start) | async-done | bytes 3538976 | tf_op jit(solution)/shard_map/all_to_all | solution.py:145
  203.8 2.5 copy.176
  206.3 15.9 %fusion.97 = f32[4,288,1536]{2,1,0:T(8,128)} fusion(bf16[4,288,1536]{2,1,0:T(8,128)(2,1)S(1)} %bitcast.220, bf16[4,1536,1536]{2,1,0:T(8,128)(2,1)} %param.21), kind=kOutput, calls=%fused_computation.186 | convolution fusion | flops 5435817984 | bytes 29491200 | tf_op jit(solution)/shard_map/erd,edf->erf/dot_general | solution.py:152
  222.2 7.4 multiply_convert_fusion.2
  229.6 11.9 %convolution_convert_fusion.1 = bf16[4,288,1536]{2,1,0:T(8,128)(2,1)} fusion(bf16[4,1536,1536]{2,1,0:T(8,128)(2,1)} %param.21, bf16[4,288,768]{2,1,0:T(8,128)(2,1)} %get-tuple-element.67, bf16[4,288,768]{2,1,0:T(8,128)(2,1)} %get-tuple-element.66), kind=kOutput, calls=%fused_computation.28 | convolution fusion | flops 5444665344 | bytes 25952256 | tf_op jit(solution)/shard_map/erf,edf->erd/dot_general | solution.py:192
  241.6 6.5 copy.180
  248.1 5.6 all-to-all-start.3
  253.6 7.2 convolution_convert_fusion.2
  260.8 4.5 copy.177
  265.3 27.7 %all-to-all-done.3 = bf16[4,288,1536]{2,0,1:T(4,128)(2,1)} async-done(((bf16[4,288,1536]{2,0,1:T(4,128)(2,1)}), bf16[4,288,1536]{2,0,1:T(4,128)(2,1)}, u32[]{:S(2)}, u32[]{:S(2)}) %all-to-all-start.3) | async-done | bytes 3538976 | tf_op jit(solution)/shard_map/all_to_all | solution.py:221
  293.0 5.3 all-to-all-start.1
  298.5 2.7 copy.181
  301.2 2.0 concatenate.39
  303.2 9.8 gather_fusion.2
  313.0 6.7 reshape.449
  319.7 17.2 %all-to-all-done.1 = bf16[4,288,1536]{2,0,1:T(4,128)(2,1)} async-done(((bf16[4,288,1536]{2,0,1:T(4,128)(2,1)}), bf16[4,288,1536]{2,0,1:T(4,128)(2,1)}, u32[]{:S(2)}, u32[]{:S(2)}) %all-to-all-start.1) | async-done | bytes 3538976 | tf_op jit(solution)/shard_map/all_to_all | solution.py:161
  336.9 2.7 copy.178
  339.6 2.1 concatenate.37
  341.6 9.7 gather_fusion.1
  351.4 6.4 reshape.442
  357.8 5.6 fusion.36
  363.6 6.2 multiply_reduce_fusion
  370.0 6.6 reduce_sum.135
  379.6 4.7 convolution_convert_fusion.3
  385.9 6.9 fusion.47
  392.9 6.5 fusion.2
  399.4 1.8 fusion.50
  403.3 16.9 %fusion = bf16[1536,4,1536]{0,2,1:T(8,128)(2,1)} fusion(bf16[4,288,1536]{2,1,0:T(8,128)(2,1)} %bitcast.221, bf16[4,288,768]{2,1,0:T(8,128)(2,1)} %get-tuple-element.67, bf16[4,288,768]{2,1,0:T(8,128)(2,1)} %get-tuple-element.66), kind=kOutput, calls=%fused_computation.8 | convolution fusion | flops 5452333056 | bytes 25952256 | tf_op jit(solution)/shard_map/erd,erf->def/dot_general | solution.py:198
  421.5 9.7 convert_bitcast_fusion
  431.2 15.5 %copy.197 = bf16[1536,4,768]{2,1,0:T(4,128)(2,1)} copy(bf16[1536,4,768]{0,2,1:T(8,128)(2,1)} %convert_bitcast_fusion) | data formatting | bytes 18874368 | tf_op jit(solution)/shard_map/convert_element_type | solution.py:213
  446.7 32.1 %copy.196 = bf16[1536,4,1536]{2,1,0:T(4,128)(2,1)} copy(bf16[1536,4,1536]{0,2,1:T(8,128)(2,1)} %fusion) | data formatting | bytes 37748736 | tf_op jit(solution)/shard_map/convert_element_type | solution.py:200
  478.9 5.1 fusion.63
  485.2 3.9 fusion.55
  492.8 6.4 fusion.61
  501.2 70.9 %reduce-scatter.13.cloned.1.call-done = f32[48,8]{1,0:T(8,128)} async-done(((f32[1536,8]{1,0:T(8,128)}), f32[48,8]{1,0:T(8,128)}) %reduce-scatter.13.cloned.1.call-update) | async-done | bytes 1552
  573.5 6.1 fusion.31
  579.6 42.1 %all-reduce.6 = (f32[1536]{0:T(1024)S(1)}, f32[1536]{0:T(1024)S(1)}) all-reduce(f32[1536]{0:T(1024)S(1)} %get-tuple-element.56, f32[1536]{0:T(1024)S(1)} %get-tuple-element.54), channel_id=3, replica_groups=mesh['expert'=2,'context'=4,'dp'=4] {'expert','context','dp'}, use_global_device_ids=true, to_apply=%region_21.22.clone | all-reduce | flops 3072 | bytes 24576
  622.8 2.8 fusion.52
  625.6 438.8 %all-reduce.10.cloned.1.call-done = (bf16[1536,4,1536]{2,1,0:T(4,128)(2,1)}, bf16[1536,4,768]{2,1,0:T(4,128)(2,1)}) async-done(((bf16[1536,4,1536]{2,1,0:T(4,128)(2,1)}, bf16[1536,4,768]{2,1,0:T(4,128)(2,1)}), (bf16[1536,4,1536]{2,1,0:T(4,128)(2,1)}, bf16[1536,4,768]{2,1,0:T(4,128)(2,1)})) %all-reduce.10.cloned.1.call-update) | async-done | bytes 28311568
  1068.4 2.1 copy.198
  (191 shorter events, 43.1 us)
Async XLA Ops:
  8.0 86.3 %copy-start = (bf16[1536,8]{0,1:T(8,128)(2,1)S(1)}, bf16[1536,8]{0,1:T(8,128)(2,1)}, u32[]{:S(2)}) copy-start(bf16[1536,8]{0,1:T(8,128)(2,1)} %param.20) | copy-start | bytes 73732
  11.7 0.6 copy-start.38
  17.1 17.4 %copy-start.10 = (f32[256,2048]{1,0:T(8,128)}, f32[256,2048]{1,0:T(8,128)S(1)}, u32[]{:S(2)}) copy-start(f32[256,2048]{1,0:T(8,128)S(1)} %fusion.69) | copy-start | bytes 6291460
  17.1 0.7 copy-start.37
  17.1 9.3 copy-start.40
  25.5 8.0 copy-start.29
  25.5 19.0 %copy-start.27 = (f32[256,64]{0,1:T(8,128)}, f32[256,64]{0,1:T(8,128)S(1)}, u32[]{:S(2)}) copy-start(f32[256,64]{0,1:T(8,128)S(1)} %get-tuple-element.83) | copy-start | bytes 196612
  25.7 21.5 %copy-start.23 = (f32[256,64]{1,0:T(8,128)}, f32[256,64]{1,0:T(8,128)S(1)}, u32[]{:S(2)}) copy-start(f32[256,64]{1,0:T(8,128)S(1)} %copy.161) | copy-start | bytes 196612
  35.6 5.6 copy-start.18
  35.6 6.9 copy-start.34
  35.7 7.0 slice-start.1
  39.7 4.6 slice-start
  39.7 4.8 copy-start.30
  42.7 4.6 copy-start.25
  79.4 1.0 copy-start.12
  79.4 1.1 copy-start.14
  80.6 1.8 copy-start.6
  82.4 4.5 copy-start.1
  82.4 4.5 copy-start.32
  86.9 2.9 copy-start.8
  89.9 4.2 copy-start.21
  89.9 4.2 copy-start.35
  94.3 22.6 %copy-start.4 = (bf16[256,1536]{1,0:T(8,128)(2,1)}, bf16[256,1536]{1,0:T(8,128)(2,1)S(1)}, u32[]{:S(2)}) copy-start(bf16[256,1536]{1,0:T(8,128)(2,1)S(1)} %multiply_convert_fusion.5) | copy-start | bytes 2359300
  111.5 46.5 %all-to-all-start.2 = ((bf16[8,144,1536]{2,1,0:T(8,128)(2,1)}), bf16[8,144,1536]{2,1,0:T(8,128)(2,1)}, u32[]{:S(2)}, u32[]{:S(2)}) async-start(bf16[8,144,1536]{2,1,0:T(8,128)(2,1)} %bitcast.208), calls=%async_computation.2 | async-start | bytes 7077888 | tf_op jit(solution)/shard_map/all_to_all | solution.py:178
  158.1 45.7 %all-to-all-start = ((bf16[8,144,1536]{2,1,0:T(8,128)(2,1)}), bf16[8,144,1536]{2,1,0:T(8,128)(2,1)}, u32[]{:S(2)}, u32[]{:S(2)}) async-start(bf16[8,144,1536]{2,1,0:T(8,128)(2,1)} %bitcast.211), calls=%async_computation | async-start | bytes 7077888 | tf_op jit(solution)/shard_map/all_to_all | solution.py:145
  203.8 18.4 %slice-start.2 = ((s8[9437184]{0:T(1024)(128)(4,1)}), s8[4194304]{0:T(1024)(128)(4,1)S(1)}, s32[]{:S(2)}) async-start(s8[9437184]{0:T(1024)(128)(4,1)} %bitcast.247), calls=%async_computation.15 | async-start | bytes 8388608
  206.2 15.9 %copy-start.17 = (bf16[4,2,144,1536]{3,2,1,0:T(8,128)(2,1)}, bf16[4,2,144,1536]{3,2,1,0:T(8,128)(2,1)S(1)}, u32[]{:S(2)}) copy-start(bf16[4,2,144,1536]{3,2,1,0:T(8,128)(2,1)S(1)} %copy.176) | copy-start | bytes 10616836
  206.2 15.9 %copy-start.16 = (bf16[4,2,144,1536]{3,2,1,0:T(8,128)(2,1)S(1)}, bf16[4,2,144,1536]{3,2,1,0:T(8,128)(2,1)}, u32[]{:S(2)}) copy-start(bf16[4,2,144,1536]{3,2,1,0:T(8,128)(2,1)} %copy.179) | copy-start | bytes 10616836
  206.2 15.9 %slice-start.3 = ((s8[9437184]{0:T(1024)(128)(4,1)}), s8[4194304]{0:T(1024)(128)(4,1)S(1)}, s32[]{:S(2)}) async-start(s8[9437184]{0:T(1024)(128)(4,1)} %bitcast.247), calls=%async_computation.16 | async-start | bytes 8388608
  206.3 15.9 %slice-start.4 = ((s8[9437184]{0:T(1024)(128)(4,1)}), s8[1048576]{0:T(1024)(128)(4,1)S(1)}, s32[]{:S(2)}) async-start(s8[9437184]{0:T(1024)(128)(4,1)} %bitcast.247), calls=%async_computation.17 | async-start | bytes 2097152
  248.1 45.0 %all-to-all-start.3 = ((bf16[4,288,1536]{2,0,1:T(4,128)(2,1)}), bf16[4,288,1536]{2,0,1:T(4,128)(2,1)}, u32[]{:S(2)}, u32[]{:S(2)}) async-start(bf16[4,288,1536]{2,0,1:T(4,128)(2,1)} %copy.180), calls=%async_computation.3 | async-start | bytes 7077888 | tf_op jit(solution)/shard_map/all_to_all | solution.py:221
  293.0 43.9 %all-to-all-start.1 = ((bf16[4,288,1536]{2,0,1:T(4,128)(2,1)}), bf16[4,288,1536]{2,0,1:T(4,128)(2,1)}, u32[]{:S(2)}, u32[]{:S(2)}) async-start(bf16[4,288,1536]{2,0,1:T(4,128)(2,1)} %copy.177), calls=%async_computation.1 | async-start | bytes 7077888 | tf_op jit(solution)/shard_map/all_to_all | solution.py:161
  298.4 191.3 %reduce-scatter.7.cloned.1.call-start = ((), (), s32[]{:S(2)}) async-start(), calls=%async_computation.8 | async-start | bytes 1310720 | tf_op jit(solution)/shard_map/reduce_scatter | solution.py:266
  351.4 6.4 copy-start.19
  357.8 5.8 copy-start.3
  376.6 1.4 copy-start.11
  376.6 1.6 copy-start.20
  379.6 6.1 copy-start.22
  379.6 6.3 copy-start.15
  385.9 7.0 copy-start.33
  392.9 6.5 copy-start.7
  399.4 2.7 copy-start.2
  403.2 16.9 %copy-start.5 = (bf16[256,1536]{1,0:T(8,128)(2,1)S(1)}, bf16[256,1536]{1,0:T(8,128)(2,1)}, u32[]{:S(2)}) copy-start(bf16[256,1536]{1,0:T(8,128)(2,1)} %copy-done.4) | copy-start | bytes 2359300
  403.2 168.8 %reduce-scatter.13.cloned.1.call-start = ((), (), s32[]{:S(2)}) async-start(), calls=%async_computation.11 | async-start | bytes 811008
  421.5 642.9 %all-reduce.10.cloned.1.call-start = ((), (), s32[]{:S(2)}) async-start(), calls=%async_computation.12 | async-start | bytes 56623104
  478.8 591.7 %reduce-scatter.11.cloned.1.call-start = ((), (), s32[]{:S(2)}) async-start(), calls=%async_computation.10 | async-start | bytes 9732096 | tf_op jit(solution)/shard_map/reduce_scatter | solution.py:296
  484.0 1.2 copy-start.13
  484.0 5.1 copy-start.28
  484.0 5.1 copy-start.31
  484.0 586.5 %reduce-scatter.9.cloned.1.call-start = ((), (), s32[]{:S(2)}) async-start(), calls=%async_computation.9 | async-start | bytes 12976128 | tf_op jit(solution)/shard_map/reduce_scatter | solution.py:295
  489.1 2.3 copy-start.24
  489.1 2.3 copy-start.26
  489.2 3.7 copy-start.9
  489.2 3.7 copy-start.36
  489.2 3.6 copy-start.39
  499.3 0.7 copy-start.41
Sparse Core Ops, SparseCore 0:
  403.3 24.7 reduce-scatter.6
  434.6 137.3 reduce-scatter.12
  579.5 183.7 reduce-scatter.10
  769.8 215.1 reduce-scatter.8
Sparse Core Ops, SparseCore 1:
  478.9 585.4 all-reduce.9
where the time goes:
time: 1090 us; the launch traced here: 1080 us
  waiting for transfers between devices  615 us (56%)
  local copies, waits for them, and re-layouts  173 us (16%)
  matrix products  133 us (12%)
  blocking collectives  59.1 us (5%)
  other arithmetic  58.8 us (5%)
  starting transfers between devices  22 us (2%)
  between operations  17.1 us (2%)
    unnamed x7, waiting for transfers between devices  510 us
    unnamed x1, blocking collectives  42.1 us
    all_to_all x1, waiting for transfers between devices, local(): lax.all_to_all(send_rows.reshape(n_experts, capacity, width), 'expert', s...  36.3 us
    convert_element_type x1, local copies, waits for them, and re-layouts, local(): expert_in = lax.psum_scatter(jnp.einsum('erd,erf->def', part_rows, inner_...  32.1 us
    all_to_all x1, waiting for transfers between devices, local(): lax.all_to_all(row_grad, 'expert', split_axis=1, concat_axis=0, tiled=True)  27.7 us
    all_to_all x1, waiting for transfers between devices, local(): lax.all_to_all(send_grad.reshape(n_experts, capacity, width), 'expert', s...  24.1 us
  transfers between devices with their start and end apart: 9, of which 6 were waited for; matrix products, arithmetic and copies ran while one was open for 15% of the time, Pallas kernels for 0%

commit v1 on v0

--- a/solution.py
+++ b/solution.py
@@ -1,6 +1,10 @@
+import functools
+
 import jax
 import jax.numpy as jnp
 from jax import lax
+from jax.experimental import pallas as pl
+from jax.experimental.pallas import tpu as pltpu
 from jax.sharding import PartitionSpec as P
 
 HEADS = 12
@@ -51,6 +55,677 @@
     earlier = jnp.cumsum(ordered, axis=0, dtype=jnp.int32) - ordered
     ranks = jnp.sum(earlier[flat_order] * choose, axis=1)
     return jnp.where(ranks < capacity, flat_ids * capacity + ranks, n_experts * capacity)
+
+
+MESH = pl.DeviceIdType.MESH
+F32 = jnp.float32
+BF16 = jnp.bfloat16
+
+
+def dot(a, b):
+    return jnp.dot(a, b, preferred_element_type=F32)
+
+
+def dot_nt(a, b):
+    return lax.dot_general(a, b, (((1,), (1,)), ((), ())), preferred_element_type=F32)
+
+
+def dot_tn(a, b):
+    return lax.dot_general(a, b, (((0,), (0,)), ((), ())), preferred_element_type=F32)
+
+
+def place():
+    e, c, z = lax.axis_index("expert"), lax.axis_index("context"), lax.axis_index("dp")
+    return e, c, z, lax.div(c, 2), lax.rem(c, 2)
+
+
+def greet(peers, extra=()):
+    barrier = pltpu.get_barrier_semaphore()
+    for peer in peers:
+        pl.semaphore_signal(barrier, inc=1, device_id=peer, device_id_type=MESH)
+    for there, peer in extra:
+
+        @pl.when(there)
+        def _():
+            pl.semaphore_signal(barrier, inc=1, device_id=peer, device_id_type=MESH)
+
+    count = len(peers)
+    for there, _ in extra:
+        count = count + there.astype(jnp.int32)
+    pl.semaphore_wait(barrier, count)
+
+
+def ffn_kernel(
+    cap,
+    ffn,
+    cot_h,
+    meta,
+    win_h,
+    wdn_h,
+    zout_h,
+    pg_out,
+    gg_out,
+    gwin_h,
+    gwdn_h,
+    agb,
+    metas,
+    cotb,
+    win,
+    wdn,
+    xs,
+    ds,
+    hid,
+    igs,
+    pgs,
+    ys,
+    zcs,
+    zcr,
+    zk,
+    rx,
+    ry,
+    ggs,
+    ggr,
+    stage,
+    load_sem,
+    cot_sem,
+    ag_s,
+    ag_r,
+    me_s,
+    me_r,
+    gg_s,
+    gg_r,
+    rs_s,
+    rs_r,
+    st_sem,
+):
+    e, c, z, y, k = place()
+    tok, width = ffn.shape
+    half = tok // 2
+    ff = wdn.shape[1]
+    planes = agb.shape[0]
+    ctx = planes // 2
+    me = e * ctx + c
+    xp, yp, kp = (1 - e, c, z), (e, (1 - y) * 2 + k, z), (e, y * 2 + 1 - k, z)
+    x_me, y_me, k_me = (1 - e) * ctx + c, e * ctx + (1 - y) * 2 + k, e * ctx + y * 2 + 1 - k
+    d_me = (1 - e) * ctx + (1 - y) * 2 + k
+    k_of = 1 - 2 * k
+
+    loads = [
+        pltpu.make_async_copy(win_h.at[c], win, load_sem.at[0]),
+        pltpu.make_async_copy(wdn_h.at[c], wdn, load_sem.at[1]),
+        pltpu.make_async_copy(cot_h, cotb, cot_sem.at[0]),
+    ]
+    for load in loads:
+        load.start()
+    others = []
+    for step in range(1, planes):
+        other = lax.rem(me + step, planes)
+        others.append((other, (lax.div(other, ctx), lax.rem(other, ctx), z)))
+    greet([dev for _, dev in others])
+
+    sent = []
+
+    def push(src, dst, s, r, i, dev):
+        copy = pltpu.make_async_remote_copy(
+            src_ref=src, dst_ref=dst, send_sem=s.at[i], recv_sem=r.at[i], device_id=dev, device_id_type=MESH
+        )
+        copy.start()
+        sent.append(copy)
+
+    def arrive(dst, s, r, i):
+        pltpu.make_async_remote_copy(
+            src_ref=dst, dst_ref=dst, send_sem=s.at[i], recv_sem=r.at[i], device_id=kp, device_id_type=MESH
+        ).wait_recv()
+
+    lo, hi = pl.ds(0, half), pl.ds(half, half)
+
+    def move(p, rows, i, dev):
+        push(agb.at[p, rows], agb.at[p, rows], ag_s, ag_r, i, dev)
+
+    def got(p, rows, i):
+        arrive(agb.at[p, rows], ag_s, ag_r, i)
+
+    for step, (other, dev) in enumerate(others):
+        pltpu.make_async_remote_copy(
+            src_ref=meta.at[other],
+            dst_ref=metas.at[me],
+            send_sem=me_s.at[step],
+            recv_sem=me_r.at[step],
+            device_id=dev,
+            device_id_type=MESH,
+        ).start()
+    push(ffn.at[lo], agb.at[me, lo], ag_s, ag_r, 0, xp)
+    push(ffn.at[hi], agb.at[me, hi], ag_s, ag_r, 3, yp)
+    push(ffn, agb.at[me], ag_s, ag_r, 6, kp)
+    push(ffn.at[hi], agb.at[me, hi], ag_s, ag_r, 1, xp)
+    push(ffn.at[lo], agb.at[me, lo], ag_s, ag_r, 2, yp)
+    agb[me] = ffn[...]
+    metas[me] = meta[me]
+    slot_rows = lax.broadcasted_iota(jnp.int32, (cap, tok), 0).astype(F32)
+
+    def spots(p):
+        return jnp.where(slot_rows == metas[p, 0:1, :], 1.0, 0.0)
+
+    def gate_of(p, hot):
+        return jnp.sum(hot * metas[p, 1:2, :], axis=1, keepdims=True)
+
+    def chip(eq, yq):
+        return eq * ctx + yq * 2
+
+    def group(q, base):
+        rows = pl.ds(q * 2 * cap, 2 * cap)
+        for kk in range(2):
+            p = base + kk
+            hot = spots(p)
+            low = hot.astype(BF16)
+            part = pl.ds(q * 2 * cap + kk * cap, cap)
+            xs[part, :] = dot(low, agb[p]).astype(BF16)
+            ds[part, :] = (dot(low, cotb[p]) * gate_of(p, hot)).astype(BF16)
+        step = 256
+
+        @pl.loop(0, ff // step)
+        def _(n):
+            gate_cols = pl.ds(pl.multiple_of(n * step, step), step)
+            up_cols = pl.ds(pl.multiple_of(ff + n * step, step), step)
+            x = xs[rows, :]
+            g = dot(x, win[:, gate_cols])
+            u = dot(x, win[:, up_cols])
+            s = 1.0 / (1.0 + jnp.exp(-g))
+            act = g * s
+            hid[rows, gate_cols] = (act * u).astype(BF16)
+            h = dot(ds[rows, :], wdn[:, gate_cols])
+            igs[rows, gate_cols] = (h * u * (s * (1.0 + g * (1.0 - s)))).astype(BF16)
+            igs[rows, up_cols] = (h * act).astype(BF16)
+
+        @pl.loop(0, width // step)
+        def _(n):
+            cols = pl.ds(pl.multiple_of(n * step, step), step)
+            pgs[:, cols] = dot_nt(igs[rows, :], win[cols, :]).astype(BF16)
+
+        mine = pl.ds(pl.multiple_of(k * cap, 16), cap)
+        theirs = pl.ds(pl.multiple_of((1 - k) * cap, 16), cap)
+        zcs[q] = dot_tn(spots(base + 1 - k).astype(BF16), pgs[theirs, :]).astype(BF16)
+        push(zcs.at[q], zcr.at[q], rs_s, rs_r, q, kp)
+        zk[q] = dot_tn(spots(base + k).astype(BF16), pgs[mine, :]).astype(BF16)
+
+    def fold(q):
+        arrive(zcr.at[q], rs_s, rs_r, q)
+        zk[q] = (zk[q].astype(F32) + zcr[q].astype(F32)).astype(BF16)
+
+    def add(q, rows, term):
+        zk[q, rows] = (zk[q, rows].astype(F32) + term.astype(F32)).astype(BF16)
+
+    def hop(q, rows, buf, i, sem, dev):
+        push(zk.at[q, rows], buf.at[i], rs_s, rs_r, sem, dev)
+
+    def hopped(buf, i, sem):
+        arrive(buf.at[i], rs_s, rs_r, sem)
+
+    for load in loads:
+        load.wait()
+    for step in range(planes - 1):
+        source = lax.rem(me + planes - 1 - step, planes)
+        arrive(metas.at[source], me_s, me_r, step)
+    got(me + k_of, pl.ds(0, tok), 6)
+    group(0, chip(e, y))
+
+    got(x_me, lo, 0)
+    move(x_me, lo, 4, yp)
+    move(x_me, lo, 7, kp)
+    got(y_me, hi, 3)
+    move(y_me, hi, 5, xp)
+    move(y_me, hi, 10, kp)
+    got(x_me, hi, 1)
+    move(x_me, hi, 8, kp)
+    got(y_me, lo, 2)
+    move(y_me, lo, 9, kp)
+    got(x_me + k_of, lo, 7)
+    got(x_me + k_of, hi, 8)
+    group(1, chip(1 - e, y))
+
+    got(d_me, lo, 4)
+    move(d_me, lo, 11, kp)
+    got(d_me, hi, 5)
+    move(d_me, hi, 12, kp)
+    got(y_me + k_of, lo, 9)
+    got(y_me + k_of, hi, 10)
+    fold(1)
+    hop(1, lo, rx, 1, 5, xp)
+    group(2, chip(e, 1 - y))
+    got(d_me + k_of, lo, 11)
+    got(d_me + k_of, hi, 12)
+    fold(2)
+    hop(2, hi, ry, 1, 8, yp)
+    group(3, chip(1 - e, 1 - y))
+    fold(3)
+    hop(3, lo, rx, 0, 4, xp)
+    hop(3, hi, ry, 0, 7, yp)
+    fold(0)
+
+    step = 256
+
+    @pl.loop(0, width // step)
+    def _(n):
+        cols = pl.ds(pl.multiple_of(n * step, step), step)
+        ys[:, cols] = dot_nt(hid[...], wdn[cols, :]).astype(BF16)
+
+    order = [chip(e, y), chip(1 - e, y), chip(e, 1 - y), chip(1 - e, 1 - y)]
+
+    for q, base in enumerate(order):
+        for kk in range(2):
+            p = base + kk
+            hot = spots(p)
+            part = pl.ds(q * 2 * cap + kk * cap, cap)
+            ggs[p, 0:1, :] = jnp.sum(hot * dot_nt(ys[part, :], cotb[p]), axis=0, keepdims=True)
+    ggr[me] = ggs[me]
+    for step, (other, dev) in enumerate(others):
+        pltpu.make_async_remote_copy(
+            src_ref=ggs.at[other],
+            dst_ref=ggr.at[me],
+            send_sem=gg_s.at[step],
+            recv_sem=gg_r.at[step],
+            device_id=dev,
+            device_id_type=MESH,
+        ).start()
+
+    hopped(rx, 0, 4)
+    add(2, lo, rx[0])
+    hop(2, lo, ry, 2, 9, yp)
+    hopped(ry, 0, 7)
+    add(1, hi, ry[0])
+    hop(1, hi, rx, 2, 6, xp)
+
+    for q, base in enumerate(order):
+        for kk in range(2):
+            p = base + kk
+            i = q * 2 + kk
+            slot = i % 2
+            hot = spots(p)
+            part = pl.ds(q * 2 * cap + kk * cap, cap)
+            scaled = (ys[part, :].astype(F32) * gate_of(p, hot)).astype(BF16)
+            if i >= 2:
+                pltpu.make_async_copy(stage.at[slot], zout_h.at[p], st_sem.at[slot]).wait()
+            stage[slot] = dot_tn(hot.astype(BF16), scaled).astype(BF16)
+            pltpu.make_async_copy(stage.at[slot], zout_h.at[p], st_sem.at[slot]).start()
+
+    for slot in range(2):
+        pltpu.make_async_copy(stage.at[slot], zout_h.at[0], st_sem.at[slot]).wait()
+
+    m = 256
+
+    def out_tiles(left, right, dest, wide):
+        @pl.loop(0, width // m)
+        def _(n):
+            slot = lax.rem(n, 2)
+            cols = pl.ds(pl.multiple_of(n * m, m), m)
+            to = pltpu.make_async_copy(stage.at[slot, :, pl.ds(0, wide)], dest.at[cols, :], st_sem.at[slot])
+
+            @pl.when(n >= 2)
+            def _():
+                to.wait()
+
+            stage[slot, :, pl.ds(0, wide)] = dot_tn(left[:, cols], right[...]).astype(BF16)
+            to.start()
+
+        for slot in range(2):
+            pltpu.make_async_copy(
+                stage.at[slot, :, pl.ds(0, wide)], dest.at[pl.ds(0, m), :], st_sem.at[slot]
+            ).wait()
+
+    out_tiles(ds, hid, gwdn_h, ff)
+    out_tiles(xs, igs, gwin_h, 2 * ff)
+
+    hopped(rx, 1, 5)
+    hopped(ry, 1, 8)
+    hopped(rx, 2, 6)
+    hopped(ry, 2, 9)
+    for rows, first, second in ((lo, rx[1], ry[2]), (hi, rx[2], ry[1])):
+        pg_out[rows, :] = zk[0, rows].astype(F32) + first.astype(F32) + second.astype(F32)
+    for step in range(planes - 1):
+        source = lax.rem(me + planes - 1 - step, planes)
+        arrive(ggr.at[source], gg_s, gg_r, step)
+    for p in range(planes):
+        gg_out[p : p + 1, :] = ggr[p, 0:1, :]
+    for step, (other, dev) in enumerate(others):
+        for buf, s, r in ((meta, me_s, me_r), (ggs, gg_s, gg_r)):
+            pltpu.make_async_remote_copy(
+                src_ref=buf.at[other],
+                dst_ref=buf.at[other],
+                send_sem=s.at[step],
+                recv_sem=r.at[step],
+                device_id=dev,
+                device_id_type=MESH,
+            ).wait_send()
+    for copy in sent:
+        copy.wait_send()
+
+
+def run_ffn(cap, ffn, cot_all, meta, win, wdn):
+    tok, width = ffn.shape
+    ff = wdn.shape[2]
+    planes = cot_all.shape[0]
+    rows = planes * cap
+    vm, anyspace = pl.BlockSpec(memory_space=pltpu.VMEM), pl.BlockSpec(memory_space=pl.ANY)
+    shape = jax.ShapeDtypeStruct
+    dma = pltpu.SemaphoreType.DMA
+    half = tok // 2
+    return pl.pallas_call(
+        functools.partial(ffn_kernel, cap),
+        out_shape=(
+            shape((planes, tok, width), BF16),
+            shape((tok, width), F32),
+            shape((planes, tok), F32),
+            shape((width, 2 * ff), BF16),
+            shape((width, ff), BF16),
+        ),
+        in_specs=[vm, anyspace, vm, anyspace, anyspace],
+        out_specs=(anyspace, vm, vm, anyspace, anyspace),
+        scratch_shapes=[
+            pltpu.VMEM((planes, tok, width), BF16),
+            pltpu.VMEM((planes, 8, tok), F32),
+            pltpu.VMEM((planes, tok, width), BF16),
+            pltpu.VMEM((width, 2 * ff), BF16),
+            pltpu.VMEM((width, ff), BF16),
+            pltpu.VMEM((rows, width), BF16),
+            pltpu.VMEM((rows, width), BF16),
+            pltpu.VMEM((rows, ff), BF16),
+            pltpu.VMEM((rows, 2 * ff), BF16),
+            pltpu.VMEM((2 * cap, width), BF16),
+            pltpu.VMEM((rows, width), BF16),
+            pltpu.VMEM((4, tok, width), BF16),
+            pltpu.VMEM((4, tok, width), BF16),
+            pltpu.VMEM((4, tok, width), BF16),
+            pltpu.VMEM((3, half, width), BF16),
+            pltpu.VMEM((3, half, width), BF16),
+            pltpu.VMEM((planes, 8, tok), F32),
+            pltpu.VMEM((planes, 8, tok), F32),
+            pltpu.VMEM((2, 256, max(width, 2 * ff)), BF16),
+            dma((2,)),
+            dma((1,)),
+            dma((13,)),
+            dma((13,)),
+            dma((planes - 1,)),
+            dma((planes - 1,)),
+            dma((planes - 1,)),
+            dma((planes - 1,)),
+            dma((10,)),
+            dma((10,)),
+            dma((2,)),
+        ],
+        compiler_params=pltpu.CompilerParams(
+            collective_id=1, has_side_effects=True, vmem_limit_bytes=62 * 2**20
+        ),
+        cost_estimate=pl.CostEstimate(flops=25 * 10**9, bytes_accessed=50 * 10**6, transcendentals=10**6),
+    )(ffn, cot_all, meta, win, wdn)
+
+
+def reduce_kernel(
+    shared,
+    gwin,
+    gwdn,
+    sh_out,
+    ex_out,
+    zcr,
+    zk,
+    rx,
+    ry,
+    fin,
+    ar,
+    ez,
+    sz,
+    rs_s,
+    rs_r,
+    ez_s,
+    ez_r,
+    sz_s,
+    sz_r,
+    aa_s,
+    aa_r,
+):
+    e, c, z, y, k = place()
+    parts = lax.axis_size("dp")
+    ctx = lax.axis_size("context")
+    last = parts - 1
+    block = zk.shape[1]
+    half = block // 2
+    piece = block // parts
+    cols = ex_out.shape[2] // 3
+    xp, yp, kp = (1 - e, c, z), (e, (1 - y) * 2 + k, z), (e, y * 2 + 1 - k, z)
+    yk = (e, (1 - y) * 2 + 1 - k, z)
+    ups = [(z, (e, c, z + 1), lambda d: d), (last - z, (e, c, z - 1), lambda d: last - d)]
+    greet([xp, yp, kp, yk], [(z < last, (e, c, z + 1)), (z > 0, (e, c, z - 1))])
+
+    def remote(src, dst, s, r, dev):
+        return pltpu.make_async_remote_copy(
+            src_ref=src, dst_ref=dst, send_sem=s, recv_sem=r, device_id=dev, device_id_type=MESH
+        )
+
+    def plus(a, b):
+        return (a.astype(F32) + b.astype(F32)).astype(BF16)
+
+    units = [(gwdn, 0), (gwin, 0), (gwin, cols)]
+
+    def line_step(own, pieces, buf, s, r, u, turn, adder):
+        for way, (i, dev, part) in enumerate(ups):
+            to = buf.at[way, u, turn - 1]
+
+            @pl.when(i == 0)
+            def _():
+                remote(own(part(parts - turn)), to, s.at[way, u, turn - 1], r.at[way, u, turn - 1], dev).start()
+
+            if turn >= 2:
+                came = buf.at[way, u, turn - 2]
+
+                @pl.when((i >= 1) & (i <= turn - 1) & (i < last))
+                def _():
+                    remote(came, came, s.at[way, u, turn - 2], r.at[way, u, turn - 2], dev).wait_recv()
+                    adder(came, part(parts - turn + i))
+                    remote(came, to, s.at[way, u, turn - 1], r.at[way, u, turn - 1], dev).start()
+
+    def line_final(buf, s, r, u):
+        for way, (i, dev, part) in enumerate(ups):
+            came = buf.at[way, u, last - 1]
+
+            @pl.when(i >= 1)
+            def _():
+                remote(came, came, s.at[way, u, last - 1], r.at[way, u, last - 1], dev).wait_recv()
+
+    def line_sent(buf, s, r, u):
+        for way, (i, dev, part) in enumerate(ups):
+            for turn in range(1, parts):
+                came = buf.at[way, u, turn - 1]
+
+                @pl.when((i <= turn - 1) & (i < last))
+                def _():
+                    remote(came, came, s.at[way, u, turn - 1], r.at[way, u, turn - 1], dev).wait_send()
+
+    def expert_own(u):
+        ref, at = units[u]
+        return lambda d: ref.at[:, d, :, pl.ds(at, cols)]
+
+    def expert_step(u, turn):
+        ref, at = units[u]
+
+        def adder(came, d):
+            for cc in range(ctx):
+                came[cc] = plus(came[cc], ref[cc, d, :, at : at + cols])
+
+        line_step(expert_own(u), ctx, ez, ez_s, ez_r, u, turn, adder)
+
+    def expert_final(u):
+        ref, at = units[u]
+        line_final(ez, ez_s, ez_r, u)
+        below, above = ez.at[0, u, last - 1], ez.at[1, u, last - 1]
+
+        @pl.when(z == 0)
+        def _():
+            for cc in range(ctx):
+                fin[u, cc] = plus(ref[cc, z, :, at : at + cols], above[cc])
+
+        @pl.when(z == last)
+        def _():
+            for cc in range(ctx):
+                fin[u, cc] = plus(ref[cc, z, :, at : at + cols], below[cc])
+
+        @pl.when((z > 0) & (z < last))
+        def _():
+            for cc in range(ctx):
+                total = ref[cc, z, :, at : at + cols].astype(F32) + below[cc].astype(F32)
+                fin[u, cc] = (total + above[cc].astype(F32)).astype(BF16)
+
+        for step in range(1, ctx):
+            cc = lax.rem(c + step, ctx)
+            remote(
+                fin.at[u, cc], ar.at[u, c], aa_s.at[u, step - 1], aa_r.at[u, step - 1], (e, cc, z)
+            ).start()
+
+    def spread(u):
+        at = u * cols
+        for step in range(1, ctx):
+            cc = lax.rem(c + ctx - step, ctx)
+            got = remote(
+                ar.at[u, cc], ar.at[u, cc], aa_s.at[u, step - 1], aa_r.at[u, step - 1], (e, cc, z)
+            )
+            got.wait_recv()
+            got.wait_send()
+            ex_out[cc, :, at : at + cols] = ar[u, cc]
+        ex_out[c, :, at : at + cols] = fin[u, c]
+
+    lo, hi = pl.ds(0, half), pl.ds(half, half)
+    order = [(e, y), (1 - e, y), (e, 1 - y), (1 - e, 1 - y)]
+    sent = []
+
+    def rows_of(eq, yq, kq):
+        return pl.ds(pl.multiple_of((eq * ctx + yq * 2 + kq) * block, 16), block)
+
+    def push(src, dst, i, dev):
+        copy = remote(src, dst, rs_s.at[i], rs_r.at[i], dev)
+        copy.start()
+        sent.append(copy)
+
+    def arrive(dst, i):
+        remote(dst, dst, rs_s.at[i], rs_r.at[i], kp).wait_recv()
+
+    def fold(q):
+        arrive(zcr.at[q], q)
+        eq, yq = order[q]
+        zk[q] = plus(shared[rows_of(eq, yq, k), :], zcr[q])
+
+    def add(q, rows, term):
+        zk[q, rows] = plus(zk[q, rows], term)
+
+    for u in range(3):
+        expert_step(u, 1)
+    for q in (1, 2, 3, 0):
+        eq, yq = order[q]
+        push(shared.at[rows_of(eq, yq, 1 - k)], zcr.at[q], q, kp)
+    fold(1)
+    push(zk.at[1, lo], rx.at[1], 5, xp)
+    fold(2)
+    push(zk.at[2, hi], ry.at[1], 8, yp)
+    fold(3)
+    push(zk.at[3, lo], rx.at[0], 4, xp)
+    push(zk.at[3, hi], ry.at[0], 7, yp)
+    fold(0)
+    expert_step(0, 2)
+    expert_step(0, 3)
+    expert_step(1, 2)
+    arrive(rx.at[0], 4)
+    add(2, lo, rx[0])
+    push(zk.at[2, lo], ry.at[2], 9, yp)
+    arrive(ry.at[0], 7)
+    add(1, hi, ry[0])
+    push(zk.at[1, hi], rx.at[2], 6, xp)
+    expert_final(0)
+    expert_step(1, 3)
+    expert_step(2, 2)
+    arrive(rx.at[1], 5)
+    arrive(ry.at[1], 8)
+    arrive(rx.at[2], 6)
+    arrive(ry.at[2], 9)
+    for rows, first, second in ((lo, rx[1], ry[2]), (hi, rx[2], ry[1])):
+        zk[0, rows] = (zk[0, rows].astype(F32) + first.astype(F32) + second.astype(F32)).astype(BF16)
+
+    def shared_own(d):
+        return zk.at[0, pl.ds(pl.multiple_of(d * piece, 16), piece)]
+
+    def shared_step(turn):
+        def adder(came, d):
+            came[...] = plus(came[...], shared_own(d)[...])
+
+        line_step(shared_own, 1, sz, sz_s, sz_r, 0, turn, adder)
+
+    shared_step(1)
+    expert_final(1)
+    expert_step(2, 3)
+    shared_step(2)
+    expert_final(2)
+    shared_step(3)
+    spread(0)
+    spread(1)
+    line_final(sz, sz_s, sz_r, 0)
+    below, above = sz.at[0, 0, last - 1], sz.at[1, 0, last - 1]
+
+    @pl.when(z == 0)
+    def _():
+        sh_out[...] = plus(shared_own(z)[...], above[...])
+
+    @pl.when(z == last)
+    def _():
+        sh_out[...] = plus(shared_own(z)[...], below[...])
+
+    @pl.when((z > 0) & (z < last))
+    def _():
+        sh_out[...] = (shared_own(z)[...].astype(F32) + below[...].astype(F32) + above[...].astype(F32)).astype(BF16)
+
+    spread(2)
+    for u in range(3):
+        line_sent(ez, ez_s, ez_r, u)
+    line_sent(sz, sz_s, sz_r, 0)
+    for copy in sent:
+        copy.wait_send()
+
+
+def run_reduce(shared, gwin, gwdn, parts, ctx, planes):
+    width, wide = shared.shape
+    block = width // planes
+    piece = block // parts
+    rows = width // (ctx * parts)
+    ff = gwdn.shape[1]
+    gwin = gwin.reshape(ctx, parts, rows, 2 * ff)
+    gwdn = gwdn.reshape(ctx, parts, rows, ff)
+    vm = pl.BlockSpec(memory_space=pltpu.VMEM)
+    shape = jax.ShapeDtypeStruct
+    dma = pltpu.SemaphoreType.DMA
+    turns = parts - 1
+    return pl.pallas_call(
+        reduce_kernel,
+        out_shape=(shape((piece, wide), BF16), shape((ctx, rows, 3 * ff), BF16)),
+        in_specs=[vm, vm, vm],
+        out_specs=(vm, vm),
+        scratch_shapes=[
+            pltpu.VMEM((4, block, wide), BF16),
+            pltpu.VMEM((4, block, wide), BF16),
+            pltpu.VMEM((3, block // 2, wide), BF16),
+            pltpu.VMEM((3, block // 2, wide), BF16),
+            pltpu.VMEM((3, ctx, rows, ff), BF16),
+            pltpu.VMEM((3, ctx, rows, ff), BF16),
+            pltpu.VMEM((2, 3, turns, ctx, rows, ff), BF16),
+            pltpu.VMEM((2, 1, turns, piece, wide), BF16),
+            dma((10,)),
+            dma((10,)),
+            dma((2, 3, turns)),
+            dma((2, 3, turns)),
+            dma((2, 1, turns)),
+            dma((2, 1, turns)),
+            dma((3, ctx - 1)),
+            dma((3, ctx - 1)),
+        ],
+        compiler_params=pltpu.CompilerParams(
+            collective_id=2, has_side_effects=True, vmem_limit_bytes=60 * 2**20
+        ),
+        cost_estimate=pl.CostEstimate(flops=10**8, bytes_accessed=30 * 10**6, transcendentals=0),
+    )(shared, gwin, gwdn)
 
 
 def local(
@@ -136,6 +811,204 @@
     ffn_in = (plain_two * gain_ffn).astype(jnp.bfloat16)
     logits = jnp.dot(ffn_in, router, preferred_element_type=jnp.float32)
     token_ids = expert_ids[0]
+    matches = token_ids[:, :, None] == jnp.arange(n_experts)[None, None, :]
+    chosen = jnp.any(matches, axis=1)
+    gates = softmax_last(jnp.where(chosen, logits, MASKED))
+    turn = jnp.sum(jnp.where(matches, priority[0][:, :, None], 0), axis=1)
+    turn = jnp.where(chosen, turn, tok_rows * top_k)
+    ranks = jnp.sum((turn[:, None, :] < turn[None, :, :]).astype(jnp.int32), axis=0)
+    slots = jnp.where(chosen & (ranks < capacity), ranks, -1).astype(jnp.float32)
+    meta = jnp.stack([slots.T, gates.T], axis=1)
+    meta = jnp.pad(meta, ((0, 0), (0, 6), (0, 0)))
+    cot_low = cotangent[0]
+    cot_full = cot_low.astype(jnp.float32)
+    cot_all = lax.all_gather(cot_low, ("expert", "context"), axis=0)
+    zout, pair_sum, gate_grad_t, gwin, gwdn = run_ffn(
+        capacity, ffn_in, cot_all, meta, in_weight, down_weight
+    )
+    out_sum = lax.psum_scatter(zout, ("expert", "context"), scatter_dimension=0, tiled=True)[0]
+    output = (resid + out_sum.astype(jnp.float32)).astype(jnp.bfloat16)
+    gate_grad = gate_grad_t.T
+    mix_grad = gates * (gate_grad - jnp.sum(gates * gate_grad, axis=-1, keepdims=True))
+    logit_grad = mix_grad.astype(jnp.bfloat16)
+    router_part = jnp.einsum("rd,re->de", ffn_in, logit_grad, preferred_element_type=jnp.float32)
+    ffn_grad = pair_sum + jnp.einsum(
+        "re,de->rd", logit_grad, router, preferred_element_type=jnp.float32
+    )
+    gain_ffn_part = jnp.sum(ffn_grad * plain_two, axis=0)
+    scaled_two = ffn_grad * gain_ffn
+    resid_grad = cot_full + inv_two * (
+        scaled_two - plain_two * jnp.mean(scaled_two * plain_two, axis=-1, keepdims=True)
+    )
+    resid_low = resid_grad.astype(jnp.bfloat16)
+    out_part = jnp.einsum("rd,rh->dh", resid_low, attended, preferred_element_type=jnp.float32)
+    att_grad = jnp.einsum(
+        "rd,dh->rh", resid_low, out_weight, preferred_element_type=jnp.float32
+    ).astype(jnp.bfloat16)
+    att_heads = att_grad.reshape(tok_rows, KV_HEADS, group, HEAD)
+    row_delta = jnp.sum(
+        att_heads.astype(jnp.float32)
+        * attended.reshape(tok_rows, KV_HEADS, group, HEAD).astype(jnp.float32),
+        axis=-1,
+    ).transpose(1, 2, 0)
+    key_piece = lax.all_gather(keys, "context", axis=0, tiled=True)
+    value_piece = lax.all_gather(values, "context", axis=0, tiled=True)
+    scores, visible = key_scores(key_piece)
+    soft = jnp.exp(scores - log_total[..., None])
+    prob_grad = jnp.einsum(
+        "qkgd,skd->kgqs", att_heads, value_piece, preferred_element_type=jnp.float32
+    )
+    score_grad = (soft * (prob_grad - row_delta[..., None])).astype(jnp.bfloat16)
+    query_acc = jnp.einsum(
+        "kgqs,skd->kgqd", score_grad, key_piece, preferred_element_type=jnp.float32
+    )
+    key_part = jnp.einsum("kgqs,qkgd->skd", score_grad, grouped, preferred_element_type=jnp.float32)
+    value_part = jnp.einsum(
+        "kgqs,qkgd->skd", soft.astype(jnp.bfloat16), att_heads, preferred_element_type=jnp.float32
+    )
+    pair_acc = jnp.stack([key_part, value_part], axis=1)
+    query_acc, pair_acc = (query_acc, pair_acc)
+    own_pairs = lax.psum_scatter(
+        pair_acc.astype(jnp.bfloat16), "context", scatter_dimension=0, tiled=True
+    ).astype(jnp.float32)
+    query_grad = (
+        unrotate(query_acc.transpose(2, 0, 1, 3).reshape(tok_rows, HEADS, HEAD), cosine, sine)
+        * scale
+    )
+    key_grad = unrotate(own_pairs[:, 0], cosine, sine)
+    mixed_grad = jnp.concatenate(
+        [
+            query_grad.reshape(tok_rows, q_cols),
+            key_grad.reshape(tok_rows, kv_cols),
+            own_pairs[:, 1].reshape(tok_rows, kv_cols),
+        ],
+        axis=-1,
+    ).astype(jnp.bfloat16)
+    qkv_part = jnp.einsum("rd,rc->dc", normed, mixed_grad, preferred_element_type=jnp.float32)
+    norm_grad = jnp.einsum("rc,dc->rd", mixed_grad, qkv_weight, preferred_element_type=jnp.float32)
+    gain_attn_part = jnp.sum(norm_grad * plain_one, axis=0)
+    scaled_one = norm_grad * gain_attn
+    input_grad = (
+        resid_grad
+        + inv_one
+        * (scaled_one - plain_one * jnp.mean(scaled_one * plain_one, axis=-1, keepdims=True))
+    ).astype(jnp.bfloat16)
+    small = jnp.concatenate(
+        [router_part, gain_attn_part[:, None], gain_ffn_part[:, None]], axis=1
+    )
+    small = jnp.pad(small, ((0, 0), (0, 128 - small.shape[1])))
+    shared = jnp.concatenate(
+        [small.astype(jnp.bfloat16), qkv_part.astype(jnp.bfloat16), out_part.astype(jnp.bfloat16)],
+        axis=1,
+    )
+    shared, experts = run_reduce(
+        shared, gwin, gwdn, lax.axis_size("dp"), contexts, contexts * lax.axis_size("expert")
+    )
+    shared = shared.astype(jnp.float32)
+    experts = experts.astype(jnp.float32)
+    router_grad = shared[:, :n_experts]
+    gain_attn_grad = shared[:, n_experts]
+    gain_ffn_grad = shared[:, n_experts + 1]
+    qkv_grad = shared[:, 128 : 128 + qkv_part.shape[1]]
+    out_proj_grad = shared[:, 128 + qkv_part.shape[1] :]
+    expert_down = experts[:, :, :ff_width]
+    expert_in = experts[:, :, ff_width:]
+    return (
+        output[None],
+        input_grad[None],
+        gain_attn_grad,
+        qkv_grad,
+        out_proj_grad,
+        gain_ffn_grad,
+        router_grad,
+        expert_in,
+        expert_down,
+    )
+
+
+def general(
+    hidden_in,
+    span_order,
+    expert_ids,
+    priority,
+    gain_attn,
+    qkv_weight,
+    out_weight,
+    gain_ffn,
+    router,
+    in_weight,
+    down_weight,
+    cotangent,
+):
+    tok_rows = hidden_in.shape[1]
+    width = hidden_in.shape[2]
+    contexts = lax.axis_size("context")
+    span_len = tok_rows // 2
+    seq_len = tok_rows * contexts
+    group = HEADS // KV_HEADS
+    q_cols = HEADS * HEAD
+    kv_cols = KV_HEADS * HEAD
+    scale = HEAD ** (-0.5)
+    local_experts = in_weight.shape[0]
+    n_experts = local_experts * lax.axis_size("expert")
+    top_k = expert_ids.shape[2]
+    capacity = (9 * tok_rows * top_k + 8 * n_experts - 1) // (8 * n_experts)
+    ff_width = down_weight.shape[2]
+    seq_spans = span_order[0]
+    stored = jnp.arange(seq_len) // span_len
+    all_pos = (seq_spans[stored] * span_len + jnp.arange(seq_len) % span_len).astype(jnp.float32)
+    my_pos = lax.dynamic_slice_in_dim(all_pos, lax.axis_index("context") * tok_rows, tok_rows)
+    cosine, sine = rope_tables(my_pos, HEAD)
+    inputs = hidden_in[0].astype(jnp.float32)
+    inv_one = lax.rsqrt(jnp.mean(inputs * inputs, axis=-1, keepdims=True) + NORM_EPS)
+    plain_one = inputs * inv_one
+    normed = (plain_one * gain_attn).astype(jnp.bfloat16)
+    mixed = jnp.dot(normed, qkv_weight, preferred_element_type=jnp.float32)
+    queries = (
+        rotate(mixed[:, :q_cols].reshape(tok_rows, HEADS, HEAD), cosine, sine) * scale
+    ).astype(jnp.bfloat16)
+    keys = rotate(
+        mixed[:, q_cols : q_cols + kv_cols].reshape(tok_rows, KV_HEADS, HEAD), cosine, sine
+    ).astype(jnp.bfloat16)
+    values = mixed[:, q_cols + kv_cols :].reshape(tok_rows, KV_HEADS, HEAD).astype(jnp.bfloat16)
+    grouped = queries.reshape(tok_rows, KV_HEADS, group, HEAD)
+
+    def key_scores(key_piece):
+        scores = jnp.einsum(
+            "qkgd,skd->kgqs", grouped, key_piece, preferred_element_type=jnp.float32
+        )
+        visible = all_pos[None, None, None, :] <= my_pos[None, None, :, None]
+        return (jnp.where(visible, scores, MASKED), visible)
+
+    running = jnp.full((KV_HEADS, group, tok_rows), MASKED, jnp.float32)
+    key_piece = lax.all_gather(keys, "context", axis=0, tiled=True)
+    value_piece = lax.all_gather(values, "context", axis=0, tiled=True)
+    scores, visible = key_scores(key_piece)
+    newest = jnp.maximum(running, jnp.max(scores, axis=-1))
+    weights = jnp.where(visible, jnp.exp(scores - newest[..., None]), 0.0)
+    totals = jnp.sum(weights, axis=-1)
+    accum = jnp.einsum(
+        "kgqs,skd->kgqd",
+        weights.astype(jnp.bfloat16),
+        value_piece,
+        preferred_element_type=jnp.float32,
+    )
+    running, totals, accum = (newest, totals, accum)
+    log_total = running + jnp.log(totals)
+    attended = (
+        (accum / totals[..., None])
+        .transpose(2, 0, 1, 3)
+        .reshape(tok_rows, q_cols)
+        .astype(jnp.bfloat16)
+    )
+    resid = inputs + jnp.einsum(
+        "rh,dh->rd", attended, out_weight, preferred_element_type=jnp.float32
+    )
+    inv_two = lax.rsqrt(jnp.mean(resid * resid, axis=-1, keepdims=True) + NORM_EPS)
+    plain_two = resid * inv_two
+    ffn_in = (plain_two * gain_ffn).astype(jnp.bfloat16)
+    logits = jnp.dot(ffn_in, router, preferred_element_type=jnp.float32)
+    token_ids = expert_ids[0]
     gates = softmax_last(jnp.take_along_axis(logits, token_ids, axis=1))
     slots = route(token_ids, priority[0], n_experts, capacity)
     pair_rows = jnp.repeat(ffn_in, top_k, axis=0)
@@ -338,4 +1211,7 @@
         P("expert", ("context", "dp"), None),
         P("expert", ("context", "dp"), None),
     )
-    return jax.shard_map(local, mesh=mesh, in_specs=in_specs, out_specs=out_specs, check_vma=False)
+    sizes = dict(mesh.shape)
+    tuned = sizes == {"expert": 2, "context": 4, "dp": 4}
+    body = local if tuned else general
+    return jax.shard_map(body, mesh=mesh, in_specs=in_specs, out_specs=out_specs, check_vma=False)

time: 1090 us -> 471 us (0.43)
  waiting for transfers between devices: 615 us -> 74.6 us
  Pallas kernels: 0 us -> 232 us
  local copies, waits for them, and re-layouts: 173 us -> 27 us
  matrix products: 133 us -> 55.6 us
  blocking collectives: 59.1 us -> 21.8 us
  starting transfers between devices: 22 us -> 0.12 us
  other arithmetic: 58.8 us -> 37.3 us
    unnamed x7 -> x3, waiting for transfers between devices: 510 us -> 0.71 us
    pallas_call x0 -> x2, Pallas kernels: none -> 232 us  [the longest x1 149 us: run_reduce(): pl.pallas_call(reduce_kernel, out_shape=(shape((piece, wide), BF16), shap...]
    all_to_all x4 -> x0, waiting for transfers between devices: 105 us -> none  [the longest x1 36.3 us: local(): lax.all_to_all(send_rows.reshape(n_experts, capacity, width), 'expert', s...]
    dot_general x7 -> x1, matrix products: 74.6 us -> 0.2 us  [local(): jnp.einsum('rd,re->de', ffn_in, logit_grad, preferred_element_type=jnp.fl...]
    convert_element_type x5 -> x0, local copies, waits for them, and re-layouts: 65.3 us -> none  [the longest x1 32.1 us: local(): expert_in = lax.psum_scatter(jnp.einsum('erd,erf->def', part_rows, inner_...]
    reduce_scatter x2 -> x1, waiting for transfers between devices: 0.01 us -> 58.3 us  [local(): lax.psum_scatter(zout, ('expert', 'context'), scatter_dimension=0, tiled=...]
    unnamed x1 -> x0, blocking collectives: 42.1 us -> none
    gather x7 -> x0, local copies, waits for them, and re-layouts: 30.5 us -> none  [the longest x1 9.76 us: local(): pair_grad = back_padded[slots].reshape(tok_rows, top_k, width)]
  transfers between devices with their start and end apart: 9 -> 3, of which waited for: 6 -> 2; matrix products, arithmetic and copies ran while one was open for 15% -> 11% of each run, Pallas kernels for 0% -> 0%
where the time goes in v1:
time: 471 us; the launch traced here: 463 us
  Pallas kernels  232 us (49%)
  waiting for transfers between devices  74.6 us (16%)
  matrix products  55.6 us (12%)
  other arithmetic  37.3 us (8%)
  local copies, waits for them, and re-layouts  27 us (6%)
  blocking collectives  21.8 us (5%)
  between operations  14.8 us (3%)
    pallas_call x1, Pallas kernels, run_reduce(): pl.pallas_call(reduce_kernel, out_shape=(shape((piece, wide), BF16), shap...  149 us
    pallas_call x1, Pallas kernels, run_ffn(): pl.pallas_call(functools.partial(ffn_kernel, cap), out_shape=(shape((plan...  82.6 us
    reduce_scatter x1, waiting for transfers between devices, local(): lax.psum_scatter(zout, ('expert', 'context'), scatter_dimension=0, tiled=...  58.3 us
    reduce_scatter x1, waiting for transfers between devices, local(): lax.psum_scatter(pair_acc.astype(jnp.bfloat16), 'context', scatter_dimens...  15.7 us
    all_gather x1, blocking collectives, local(): key_piece = lax.all_gather(keys, 'context', axis=0, tiled=True)  11.2 us
    all_gather x1, blocking collectives, local(): value_piece = lax.all_gather(values, 'context', axis=0, tiled=True)  10.6 us
    concatenate x1, other arithmetic, local(): jnp.concatenate([small.astype(jnp.bfloat16), qkv_part.astype(jnp.bfloat16...  9.71 us
  transfers between devices with their start and end apart: 3, of which 2 were waited for; matrix products, arithmetic and copies ran while one was open for 11% of the time, Pallas kernels for 0%

profile of v1, /device:TPU:0, one launch (start us, length us, event | category | flops | bytes accessed | tf_op | source)
XLA Modules:
  0.0 463.1 jit_solution(10573863390093248441)
XLA Ops:
  7.2 0.7 all-gather.2.cloned.1.call-update
  8.0 1.4 fusion.28
  9.4 4.9 %fusion.58 = f32[256,2048]{1,0:T(8,128)S(1)} fusion(bf16[1536,2048]{1,0:T(8,128)(2,1)} %param.17, bf16[1,256,1536]{2,1,0:T(8,128)(2,1)} %param.12, f32[1536]{0:T(1024)} %param.16, f32[256]{0:T(256)S(1)} %add_rsqrt_fusion.1), kind=kOutput, calls=%fused_computation.84 | convolution fusion | flops 1612185600 | bytes 9182208 | tf_op jit(solution)/shard_map/dot_general | solution.py:768
  14.3 0.7 slice.102
  15.2 0.6 fusion.85
  15.8 4.5 compare_select_fusion.1
  20.4 0.7 fusion.74
  21.5 0.7 copy.134
  22.2 0.8 copy.136
  23.1 0.3 convert_reduce_fusion
  23.5 0.6 copy.143
  24.1 0.8 copy.172
  24.9 0.5 copy.137
  25.3 1.1 reshape.250
  26.4 2.2 multiply_subtract_fusion.1
  28.6 1.6 copy.138
  30.2 1.6 copy.139
  31.8 0.3 fusion.84
  32.2 1.0 subtract_convert_fusion.1
  33.4 0.5 fusion.29
  33.9 11.2 %all_gather.11 = bf16[1024,2,128]{2,0,1:T(8,128)(2,1)S(1)} all-gather(bf16[256,2,128]{2,0,1:T(8,128)(2,1)S(1)} %pad_maximum_fusion.4), channel_id=1, replica_groups=mesh['expert'=2,'context'=4,'dp'=4] {'context'}, dimensions={0}, use_global_device_ids=true | all-gather | bytes 655360 | tf_op jit(solution)/shard_map/all_gather | solution.py:786
  45.1 10.6 %all_gather.12 = bf16[1024,2,128]{0,2,1:T(8,128)(2,1)S(1)} all-gather(bf16[256,2,128]{0,2,1:T(8,128)(2,1)S(1)} %bitcast.194), channel_id=1, replica_groups=mesh['expert'=2,'context'=4,'dp'=4] {'context'}, dimensions={0}, use_global_device_ids=true | all-gather | bytes 655360 | tf_op jit(solution)/shard_map/all_gather | solution.py:787
  55.9 1.8 fusion.8
  57.8 2.5 fusion.6
  60.3 2.0 copy-done.2
  62.3 3.4 fusion.32
  65.7 4.2 multiply_reduce_fusion.3
  69.9 0.6 copy-done.30
  70.7 0.9 copy-done.9
  72.0 0.6 copy-done.34
  72.6 0.7 select_maximum_fusion.meta
  73.2 82.6 %shard_map.187 = (bf16[8,256,1536]{2,1,0:T(8,128)(2,1)}, f32[256,1536]{1,0:T(8,128)}, f32[8,256]{1,0:T(8,128)}, bf16[1536,1536]{1,0:T(8,128)(2,1)}, bf16[1536,768]{1,0:T(8,128)(2,1)}) custom-call(bf16[256,1536]{1,0:T(8,128)(2,1)} %copy-done.9, bf16[8,256,1536]{2,1,0:T(8,128)(2,1)} %all-gather.2.cloned.1.call-done.cot_h, ...), custom_call_target="tpu_custom_call" | custom-call | flops 24999999488 | bytes 50000000 | tf_op jit(solution)/shard_map/pallas_call | solution.py:412
  155.8 0.6 log_add_fusion
  156.5 0.7 fusion.62
  157.2 0.7 fusion.64
  157.9 2.6 multiply_reduce_fusion
  160.5 58.3 %reduce-scatter.3.cloned.1.call-done = bf16[1,256,1536]{2,1,0:T(8,128)(2,1)} async-done(((bf16[8,256,1536]{2,1,0:T(8,128)(2,1)}), bf16[1,256,1536]{2,1,0:T(8,128)(2,1)}) %reduce-scatter.3.cloned.1.call-update) | async-done | bytes 786448 | tf_op jit(solution)/shard_map/reduce_scatter | solution.py:829
  218.8 3.3 convert_add_fusion
  222.1 4.6 convolution_convert_fusion.2
  226.7 1.5 copy.144
  228.4 7.0 %fusion.42 = bf16[1024,1,2,128]{3,0,2,1:T(8,128)(2,1)S(1)} fusion(bf16[256,2,6,128]{0,3,2,1:T(8,128)(2,1)S(1)} %bitcast.185, f32[2,1024,256,6]{2,1,3,0:T(8,128)} %copy-done.2, f32[2,6,256]{2,1,0:T(8,128)S(1)} %copy-done.32, pred[256,1024]{0,1:T(8,128)(4,1)S(1)} %broadcast_compare_fusion), kind=kOutput, calls=%fused_computation.59 | convolution fusion | flops 815005696 | bytes 14168064 | tf_op jit(solution)/shard_map/kgqs,qkgd->skd/dot_general | solution.py:866
  235.4 6.7 %fusion.2 = bf16[2,6,256,1024]{2,3,1,0:T(8,128)(2,1)S(1)} fusion(f32[2,1024,256,6]{2,1,3,0:T(8,128)} %copy-done.2, f32[2,6,256]{2,1,0:T(8,128)S(1)} %bitcast.196, f32[2,6,256]{2,1,0:T(8,128)S(1)} %copy-done.32, pred[256,1024]{0,1:T(8,128)(4,1)S(1)} %broadcast_compare_fusion, bf16[256,2,6,128]{0,3,2,1:T(8,128)(2,1)S(1)} %bitcast.186, ...), kind=kOutput, calls=%fused_computation.4 | convolution fusion | flops 821035008 | bytes 20471808 | tf_op jit(solution)/shard_map/qkgd,skd->kgqs/dot_general | solution.py:858
  242.1 1.8 fusion.45
  243.9 0.8 copy-done.3
  244.7 1.1 pad_maximum_fusion
  246.4 3.9 fusion.50
  250.7 0.8 copy-done.15
  251.5 3.6 convolution_convert_fusion.1
  255.2 15.7 %reduce-scatter.5.cloned.1.call-done = bf16[256,2,2,128]{3,0,2,1:T(8,128)(2,1)} async-done(((bf16[1024,2,2,128]{3,0,2,1:T(8,128)(2,1)}), bf16[256,2,2,128]{3,0,2,1:T(8,128)(2,1)}) %reduce-scatter.5.cloned.1.call-update) | async-done | bytes 262160 | tf_op jit(solution)/shard_map/reduce_scatter | solution.py:871
  270.9 1.6 fusion.60
  272.9 1.0 copy.155
  274.0 6.1 %fusion.27 = (bf16[1536]{0:T(1024)(128)(2,1)S(1)}, f32[256]{0:T(256)S(1)}, f32[256,1536]{1,0:T(8,128)}) fusion(bf16[1,256,1536]{2,1,0:T(8,128)(2,1)S(1)} %copy-done.5, f32[256]{0:T(256)S(1)} %copy-done.29, f32[1536]{0:T(1024)S(1)} %copy-done.25, bf16[1536,2048]{1,0:T(8,128)(2,1)} %param.17, bf16[256,256]{0,1:T(8,128)(2,1)S(1)} %bitcast.192, ...), kind=kOutput, calls=%fused_computation.39 | convolution fusion | flops 1616509184 | bytes 9710592 | tf_op jit(solution)/shard_map/rc,dc->rd/dot_general | solution.py:888
  280.1 4.6 convolution_convert_fusion
  285.0 9.7 %fusion.4.shared = bf16[1536,3712]{1,0:T(8,128)(2,1)} fusion(bf16[1536,10]{1,0:T(8,128)(2,1)S(1)} %copy.156, bf16[1536,1536]{1,0:T(8,128)(2,1)} %convolution_convert_fusion.1, bf16[1536,2048]{1,0:T(8,128)(2,1)} %convolution_convert_fusion), kind=kLoop, calls=%fused_computation.9 | loop fusion | flops 45613056 | bytes 22444032 | tf_op jit(solution)/shard_map/concatenate | solution.py:900
  294.7 149.3 %shard_map.188 = (bf16[48,3712]{1,0:T(8,128)(2,1)}, bf16[4,96,2304]{2,1,0:T(8,128)(2,1)}) custom-call(bf16[1536,3712]{1,0:T(8,128)(2,1)} %fusion.4.shared, bf16[4,4,96,1536]{3,2,1,0:T(8,128)(2,1)} %bitcast.181, bf16[4,4,96,768]{3,2,1,0:T(8,128)(2,1)} %bitcast.189), custom_call_target="tpu_custom_call" | custom-call | flops 100000000 | bytes 30000000 | tf_op jit(solution)/shard_map/pallas_call | solution.py:701
  444.0 0.8 slice.118
  444.8 1.6 slice.116
  446.5 1.7 slice.115
  448.2 1.0 convert_element_type.139
  449.2 1.1 slice.120
  450.3 1.7 slice.119
  452.0 0.7 copy.158
  452.7 0.7 slice_reduce_fusion
  453.4 2.8 fusion.47
  (106 shorter events, 3.8 us)
Async XLA Ops:
  7.2 64.4 %copy-start = (bf16[1536,8]{0,1:T(8,128)(2,1)S(1)}, bf16[1536,8]{0,1:T(8,128)(2,1)}, u32[]{:S(2)}) copy-start(bf16[1536,8]{0,1:T(8,128)(2,1)} %param.20) | copy-start | bytes 73732
  7.2 66.0 %all-gather.2.cloned.1.call-start = ((), (), s32[]{:S(2)}) async-start(), calls=%async_computation.2 | async-start | bytes 7077888 | tf_op jit(solution)/shard_map/all_gather | solution.py:825
  7.9 210.8 %reduce-scatter.3.cloned.1.call-start = ((), (), s32[]{:S(2)}) async-start(), calls=%async_computation.3 | async-start | bytes 7077888 | tf_op jit(solution)/shard_map/reduce_scatter | solution.py:829
  9.4 4.9 %copy-start.28 = (f32[256]{0:T(256)}, f32[256]{0:T(256)S(1)}, u32[]{:S(2)}) copy-start(f32[256]{0:T(256)S(1)} %add_rsqrt_fusion.1) | copy-start | bytes 3076
  14.3 0.9 copy-start.27
  14.3 8.6 %copy-start.33 = (s32[1,256,4]{1,2,0:T(4,128)S(1)}, s32[1,256,4]{1,2,0:T(4,128)}, u32[]{:S(2)}) copy-start(s32[1,256,4]{1,2,0:T(4,128)} %param.14) | copy-start | bytes 12292
  14.3 8.6 %copy-start.35 = (s32[1,256,4]{1,2,0:T(4,128)S(1)}, s32[1,256,4]{1,2,0:T(4,128)}, u32[]{:S(2)}) copy-start(s32[1,256,4]{1,2,0:T(4,128)} %param.15) | copy-start | bytes 12292
  21.4 2.7 copy-start.19
  33.4 11.7 %copy-start.23 = (bf16[256,256]{0,1:T(8,128)(2,1)S(1)}, bf16[256,256]{0,1:T(8,128)(2,1)}, u32[]{:S(2)}) copy-start(bf16[256,256]{0,1:T(8,128)(2,1)} %copy.172) | copy-start | bytes 393220
  33.8 23.9 %copy-start.7 = (bf16[256,2,6,128]{3,0,2,1:T(8,128)(2,1)}, bf16[256,2,6,128]{3,0,2,1:T(8,128)(2,1)S(1)}, u32[]{:S(2)}) copy-start(bf16[256,2,6,128]{3,0,2,1:T(8,128)(2,1)S(1)} %fusion.29) | copy-start | bytes 2359300
  45.1 12.7 %copy-start.11 = (bf16[1024,2,128]{2,0,1:T(8,128)(2,1)}, bf16[1024,2,128]{2,0,1:T(8,128)(2,1)S(1)}, u32[]{:S(2)}) copy-start(bf16[1024,2,128]{2,0,1:T(8,128)(2,1)S(1)} %all_gather.11) | copy-start | bytes 1572868
  55.7 4.6 %copy-start.21 = (bf16[1024,2,128]{0,2,1:T(8,128)(2,1)}, bf16[1024,2,128]{0,2,1:T(8,128)(2,1)S(1)}, u32[]{:S(2)}) copy-start(bf16[1024,2,128]{0,2,1:T(8,128)(2,1)S(1)} %all_gather.12) | copy-start | bytes 1572868
  57.8 4.6 copy-start.2
  62.3 3.4 copy-start.4
  65.7 4.2 copy-start.13
  65.7 4.8 %copy-start.24 = (f32[1536]{0:T(1024)S(1)}, f32[1536]{0:T(1024)}, u32[]{:S(2)}) copy-start(f32[1536]{0:T(1024)} %param.19) | copy-start | bytes 18436
  69.9 2.6 copy-start.26
  69.9 0.6 copy-start.30
  70.7 0.9 copy-start.9
  71.9 0.6 copy-start.34
  155.8 2.1 copy-start.16
  155.8 115.1 %reduce-scatter.5.cloned.1.call-start = ((), (), s32[]{:S(2)}) async-start(), calls=%async_computation.4 | async-start | bytes 1310720 | tf_op jit(solution)/shard_map/reduce_scatter | solution.py:871
  157.9 60.8 %copy-start.31 = (f32[256]{0:T(256)S(1)}, f32[256]{0:T(256)}, u32[]{:S(2)}) copy-start(f32[256]{0:T(256)} %copy-done.30) | copy-start | bytes 3076
  226.7 1.5 copy-start.14
  226.7 1.7 copy-start.32
  228.4 7.0 %copy-start.22 = (bf16[1024,2,128]{0,2,1:T(8,128)(2,1)S(1)}, bf16[1024,2,128]{0,2,1:T(8,128)(2,1)}, u32[]{:S(2)}) copy-start(bf16[1024,2,128]{0,2,1:T(8,128)(2,1)} %copy-done.21) | copy-start | bytes 1572868
  235.4 6.7 %copy-start.8 = (bf16[256,2,6,128]{3,0,2,1:T(8,128)(2,1)S(1)}, bf16[256,2,6,128]{3,0,2,1:T(8,128)(2,1)}, u32[]{:S(2)}) copy-start(bf16[256,2,6,128]{3,0,2,1:T(8,128)(2,1)} %copy-done.7) | copy-start | bytes 2359300
  242.1 2.6 copy-start.3
  244.7 1.4 copy-start.10
  244.7 1.7 copy-start.12
  246.4 3.9 copy-start.20
  250.3 1.2 copy-start.15
  251.5 21.0 %copy-start.17 = (f32[256,64]{1,0:T(8,128)S(1)}, f32[256,64]{1,0:T(8,128)}, u32[]{:S(2)}) copy-start(f32[256,64]{1,0:T(8,128)} %copy.134) | copy-start | bytes 196612
  251.5 21.0 %copy-start.18 = (f32[256,64]{1,0:T(8,128)S(1)}, f32[256,64]{1,0:T(8,128)}, u32[]{:S(2)}) copy-start(f32[256,64]{1,0:T(8,128)} %copy.136) | copy-start | bytes 196612
  255.2 18.7 %copy-start.5 = (bf16[1,256,1536]{2,1,0:T(8,128)(2,1)S(1)}, bf16[1,256,1536]{2,1,0:T(8,128)(2,1)}, u32[]{:S(2)}) copy-start(bf16[1,256,1536]{2,1,0:T(8,128)(2,1)} %param.12) | copy-start | bytes 2359300
  255.2 18.8 %copy-start.25 = (f32[1536]{0:T(1024)S(1)}, f32[1536]{0:T(1024)}, u32[]{:S(2)}) copy-start(f32[1536]{0:T(1024)} %param.16) | copy-start | bytes 18436
  255.2 18.8 %copy-start.29 = (f32[256]{0:T(256)S(1)}, f32[256]{0:T(256)}, u32[]{:S(2)}) copy-start(f32[256]{0:T(256)} %copy-done.28) | copy-start | bytes 3076
  444.0 5.2 %copy-start.6 = (bf16[4,96,2304]{2,1,0:T(8,128)(2,1)S(1)}, bf16[4,96,2304]{2,1,0:T(8,128)(2,1)}, u32[]{:S(2)}) copy-start(bf16[4,96,2304]{2,1,0:T(8,128)(2,1)} %get-tuple-element.22) | copy-start | bytes 5308420
  453.4 2.8 copy-start.1
Sparse Core Ops, SparseCore 0:
  9.9 53.2 all-gather.1
  155.9 62.7 reduce-scatter.2
  245.9 24.8 reduce-scatter.4

commit v2 on v0

--- a/solution.py
+++ b/solution.py
@@ -1,6 +1,10 @@
+import functools
+
 import jax
 import jax.numpy as jnp
 from jax import lax
+from jax.experimental import pallas as pl
+from jax.experimental.pallas import tpu as pltpu
 from jax.sharding import PartitionSpec as P
 
 HEADS = 12
@@ -51,6 +55,931 @@
     earlier = jnp.cumsum(ordered, axis=0, dtype=jnp.int32) - ordered
     ranks = jnp.sum(earlier[flat_order] * choose, axis=1)
     return jnp.where(ranks < capacity, flat_ids * capacity + ranks, n_experts * capacity)
+
+
+MESH = pl.DeviceIdType.MESH
+F32 = jnp.float32
+BF16 = jnp.bfloat16
+
+
+def dot(a, b):
+    return jnp.dot(a, b, preferred_element_type=F32)
+
+
+def dot_nt(a, b):
+    return lax.dot_general(a, b, (((1,), (1,)), ((), ())), preferred_element_type=F32)
+
+
+def dot_tn(a, b):
+    return lax.dot_general(a, b, (((0,), (0,)), ((), ())), preferred_element_type=F32)
+
+
+def plus(a, *more):
+    total = a.astype(F32)
+    for b in more:
+        total = total + b.astype(F32)
+    return total.astype(BF16)
+
+
+def lanes(at, size):
+    return pl.ds(pl.multiple_of(at, 128), size)
+
+
+def rows_at(at, size):
+    return pl.ds(pl.multiple_of(at, 16), size)
+
+
+def remote(src, dst, s, r, dev):
+    return pltpu.make_async_remote_copy(
+        src_ref=src, dst_ref=dst, send_sem=s, recv_sem=r, device_id=dev, device_id_type=MESH
+    )
+
+
+class Spot:
+    def __init__(self):
+        e, c, z = lax.axis_index("expert"), lax.axis_index("context"), lax.axis_index("dp")
+        self.ctx = lax.axis_size("context")
+        self.parts = lax.axis_size("dp")
+        self.planes = self.ctx * lax.axis_size("expert")
+        y, k = lax.div(c, 2), lax.rem(c, 2)
+        self.e, self.c, self.z, self.k = e, c, z, k
+        self.me = e * self.ctx + c
+        self.xp, self.yp = (1 - e, c, z), (e, (1 - y) * 2 + k, z)
+        self.kp, self.yk = (e, y * 2 + 1 - k, z), (e, (1 - y) * 2 + 1 - k, z)
+        self.chips = [
+            eq * self.ctx + yq * 2 for eq, yq in ((e, y), (1 - e, y), (e, 1 - y), (1 - e, 1 - y))
+        ]
+
+    def others(self):
+        found = []
+        for step in range(1, self.planes):
+            other = lax.rem(self.me + step, self.planes)
+            found.append((other, (lax.div(other, self.ctx), lax.rem(other, self.ctx), self.z)))
+        return found
+
+    def along(self):
+        e, c, z = self.e, self.c, self.z
+        return [(z < self.parts - 1, (e, c, z + 1)), (z > 0, (e, c, z - 1))]
+
+
+def greet(peers, extra=()):
+    barrier = pltpu.get_barrier_semaphore()
+    for peer in peers:
+        pl.semaphore_signal(barrier, inc=1, device_id=peer, device_id_type=MESH)
+    for there, peer in extra:
+
+        @pl.when(there)
+        def _():
+            pl.semaphore_signal(barrier, inc=1, device_id=peer, device_id_type=MESH)
+
+    count = len(peers)
+    for there, _ in extra:
+        count = count + there.astype(jnp.int32)
+    pl.semaphore_wait(barrier, count)
+
+
+class Plane:
+    def __init__(self, spot, zcr, zk, rx, ry, s, r):
+        self.spot, self.zcr, self.zk, self.rx, self.ry, self.s, self.r = spot, zcr, zk, rx, ry, s, r
+        half = zk.shape[1] // 2
+        self.lo, self.hi = pl.ds(0, half), pl.ds(half, half)
+        self.sent = []
+
+    def push(self, src, dst, i, dev):
+        copy = remote(src, dst, self.s.at[i], self.r.at[i], dev)
+        copy.start()
+        self.sent.append(copy)
+
+    def arrive(self, dst, i):
+        remote(dst, dst, self.s.at[i], self.r.at[i], self.spot.kp).wait_recv()
+
+    def give(self, q, src):
+        self.push(src, self.zcr.at[q], q, self.spot.kp)
+
+    def fold(self, q, own):
+        self.arrive(self.zcr.at[q], q)
+        self.zk[q] = plus(own, self.zcr[q])
+
+    def near(self):
+        self.push(self.zk.at[1, self.lo], self.rx.at[1], 5, self.spot.xp)
+        self.push(self.zk.at[2, self.hi], self.ry.at[1], 8, self.spot.yp)
+
+    def across(self):
+        self.push(self.zk.at[3, self.lo], self.rx.at[0], 4, self.spot.xp)
+        self.push(self.zk.at[3, self.hi], self.ry.at[0], 7, self.spot.yp)
+
+    def turn(self):
+        lo, hi = self.lo, self.hi
+        self.arrive(self.rx.at[0], 4)
+        self.zk[2, lo] = plus(self.zk[2, lo], self.rx[0])
+        self.push(self.zk.at[2, lo], self.ry.at[2], 9, self.spot.yp)
+        self.arrive(self.ry.at[0], 7)
+        self.zk[1, hi] = plus(self.zk[1, hi], self.ry[0])
+        self.push(self.zk.at[1, hi], self.rx.at[2], 6, self.spot.xp)
+
+    def total(self):
+        self.arrive(self.rx.at[1], 5)
+        self.arrive(self.ry.at[1], 8)
+        self.arrive(self.rx.at[2], 6)
+        self.arrive(self.ry.at[2], 9)
+        return ((self.lo, self.rx.at[1], self.ry.at[2]), (self.hi, self.rx.at[2], self.ry.at[1]))
+
+    def done(self):
+        for copy in self.sent:
+            copy.wait_send()
+
+
+def plane_scratch(block, wide):
+    return [
+        pltpu.VMEM((4, block, wide), BF16),
+        pltpu.VMEM((4, block, wide), BF16),
+        pltpu.VMEM((3, block // 2, wide), BF16),
+        pltpu.VMEM((3, block // 2, wide), BF16),
+        pltpu.SemaphoreType.DMA((10,)),
+        pltpu.SemaphoreType.DMA((10,)),
+    ]
+
+
+class Line:
+    def __init__(self, spot, own, adder, buf, s, r):
+        z, last = spot.z, spot.parts - 1
+        e, c = spot.e, spot.c
+        self.own, self.adder, self.buf, self.s, self.r = own, adder, buf, s, r
+        self.z, self.last, self.parts = z, last, spot.parts
+        self.ways = [(z, (e, c, z + 1), lambda d: d), (last - z, (e, c, z - 1), lambda d: last - d)]
+
+    def step(self, turn):
+        for way, (i, dev, part) in enumerate(self.ways):
+            to, s, r = self.buf.at[way, turn - 1], self.s.at[way, turn - 1], self.r.at[way, turn - 1]
+
+            @pl.when(i == 0)
+            def _():
+                remote(self.own(part(self.parts - turn)), to, s, r, dev).start()
+
+            if turn >= 2:
+                came, s_came, r_came = (x.at[way, turn - 2] for x in (self.buf, self.s, self.r))
+
+                @pl.when((i >= 1) & (i <= turn - 1) & (i < self.last))
+                def _():
+                    remote(came, came, s_came, r_came, dev).wait_recv()
+                    self.adder(came, part(self.parts - turn + i))
+                    remote(came, to, s, r, dev).start()
+
+    def final(self, put):
+        last, z = self.last, self.z
+        for way, (i, dev, _) in enumerate(self.ways):
+            came = self.buf.at[way, last - 1]
+
+            @pl.when(i >= 1)
+            def _():
+                remote(came, came, self.s.at[way, last - 1], self.r.at[way, last - 1], dev).wait_recv()
+
+        up, down = self.buf.at[0, last - 1], self.buf.at[1, last - 1]
+        pl.when(z == 0)(lambda: put(down))
+        pl.when(z == last)(lambda: put(up))
+        pl.when((z > 0) & (z < last))(lambda: put(up, down))
+
+    def done(self):
+        for way, (i, dev, _) in enumerate(self.ways):
+            for turn in range(1, self.parts):
+                came = self.buf.at[way, turn - 1]
+
+                @pl.when((i <= turn - 1) & (i < self.last))
+                def _():
+                    remote(came, came, self.s.at[way, turn - 1], self.r.at[way, turn - 1], dev).wait_send()
+
+
+def line_scratch(parts, piece):
+    return [
+        pltpu.VMEM((2, parts - 1) + piece, BF16),
+        pltpu.SemaphoreType.DMA((2, parts - 1)),
+        pltpu.SemaphoreType.DMA((2, parts - 1)),
+    ]
+
+
+class ExpertLine:
+    def __init__(self, spot, ref, at, cols, buf, s, r, fin, spread, a_s, a_r):
+        self.spot, self.ref, self.at, self.cols = spot, ref, at, cols
+        self.fin, self.spread, self.a_s, self.a_r = fin, spread, a_s, a_r
+        self.line = Line(spot, self.own, self.adder, buf, s, r)
+        self.step = self.line.step
+
+    def own(self, d):
+        return self.ref.at[:, d, :, pl.ds(self.at, self.cols)]
+
+    def piece(self, cc, d):
+        return self.ref[cc, d, :, self.at : self.at + self.cols]
+
+    def adder(self, came, d):
+        for cc in range(self.spot.ctx):
+            came[cc] = plus(came[cc], self.piece(cc, d))
+
+    def final(self):
+        spot = self.spot
+
+        def put(*came):
+            for cc in range(spot.ctx):
+                self.fin[cc] = plus(self.piece(cc, spot.z), *(x[cc] for x in came))
+
+        self.line.final(put)
+        for step in range(1, spot.ctx):
+            cc = lax.rem(spot.c + step, spot.ctx)
+            remote(
+                self.fin.at[cc],
+                self.spread.at[spot.c],
+                self.a_s.at[step - 1],
+                self.a_r.at[step - 1],
+                (spot.e, cc, spot.z),
+            ).start()
+
+    def done(self, out):
+        spot = self.spot
+        for step in range(1, spot.ctx):
+            cc = lax.rem(spot.c + spot.ctx - step, spot.ctx)
+            got = remote(
+                self.spread.at[cc],
+                self.spread.at[cc],
+                self.a_s.at[step - 1],
+                self.a_r.at[step - 1],
+                (spot.e, cc, spot.z),
+            )
+            got.wait_recv()
+            got.wait_send()
+            out[cc] = self.spread[cc]
+        out[spot.c] = self.fin[spot.c]
+        self.line.done()
+
+
+def expert_scratch(ctx, parts, rows, cols):
+    return line_scratch(parts, (ctx, rows, cols)) + [
+        pltpu.VMEM((ctx, rows, cols), BF16),
+        pltpu.VMEM((ctx, rows, cols), BF16),
+        pltpu.SemaphoreType.DMA((ctx - 1,)),
+        pltpu.SemaphoreType.DMA((ctx - 1,)),
+    ]
+
+
+def ffn_kernel(cap, ffn, cot_h, meta, win_h, wdn_h, zout_h, pg_out, gg_out, gwin_h, ex_out, *scratch):
+    agb, metas, cotb, win, wdn, xs, ds, hid, igs, pgs, ggs, ggr, stage, gwdn, pgt = scratch[:15]
+    load_sem, ag_s, ag_r, me_s, me_r, gg_s, gg_r, st_sem = scratch[15:23]
+    plane_refs, line_refs = scratch[23:29], scratch[29:]
+    spot = Spot()
+    e, c, k, me = spot.e, spot.c, spot.k, spot.me
+    xp, yp, kp = spot.xp, spot.yp, spot.kp
+    tok, width = ffn.shape
+    half = tok // 2
+    ff = wdn.shape[1]
+    planes, ctx = spot.planes, spot.ctx
+    chips = spot.chips
+    x_me, y_me, d_me = (base + k for base in chips[1:])
+    side = 1 - 2 * k
+
+    loads = [
+        pltpu.make_async_copy(win_h.at[c], win, load_sem.at[0]),
+        pltpu.make_async_copy(wdn_h.at[c], wdn, load_sem.at[1]),
+        pltpu.make_async_copy(cot_h, cotb, load_sem.at[2]),
+    ]
+    for load in loads:
+        load.start()
+    others = spot.others()
+    greet([dev for _, dev in others], spot.along())
+    plane = Plane(spot, *plane_refs)
+    line = ExpertLine(spot, gwdn, 0, ff, *line_refs)
+    lo, hi = plane.lo, plane.hi
+    sent = []
+
+    def push(src, dst, i, dev):
+        copy = remote(src, dst, ag_s.at[i], ag_r.at[i], dev)
+        copy.start()
+        sent.append(copy)
+
+    def move(p, rows, i, dev):
+        push(agb.at[p, rows], agb.at[p, rows], i, dev)
+
+    def got(p, rows, i):
+        remote(agb.at[p, rows], agb.at[p, rows], ag_s.at[i], ag_r.at[i], kp).wait_recv()
+
+    for step, (other, dev) in enumerate(others):
+        remote(meta.at[other], metas.at[me], me_s.at[step], me_r.at[step], dev).start()
+    push(ffn.at[lo], agb.at[me, lo], 0, xp)
+    push(ffn.at[hi], agb.at[me, hi], 3, yp)
+    push(ffn, agb.at[me], 6, kp)
+    push(ffn.at[hi], agb.at[me, hi], 1, xp)
+    push(ffn.at[lo], agb.at[me, lo], 2, yp)
+    agb[me] = ffn[...]
+    metas[me] = meta[me]
+    slot_rows = lax.broadcasted_iota(jnp.int32, (cap, tok), 0).astype(F32)
+    step = 256
+
+    def spots(p):
+        return jnp.where(slot_rows == metas[p, 0:1, :], 1.0, 0.0)
+
+    def gate_of(p, hot):
+        return jnp.sum(hot * metas[p, 1:2, :], axis=1, keepdims=True)
+
+    def group(q):
+        base = chips[q]
+        rows = pl.ds(q * 2 * cap, 2 * cap)
+        for kk in range(2):
+            p = base + kk
+            hot = spots(p)
+            low = hot.astype(BF16)
+            part = pl.ds(q * 2 * cap + kk * cap, cap)
+            xs[part, :] = dot(low, agb[p]).astype(BF16)
+            ds[part, :] = (dot(low, cotb[p]) * gate_of(p, hot)).astype(BF16)
+
+        @pl.loop(0, ff // step)
+        def _(n):
+            gate_cols, up_cols = lanes(n * step, step), lanes(ff + n * step, step)
+            x = xs[rows, :]
+            g = dot(x, win[:, gate_cols])
+            u = dot(x, win[:, up_cols])
+            s = 1.0 / (1.0 + jnp.exp(-g))
+            act = g * s
+            hid[rows, gate_cols] = (act * u).astype(BF16)
+            h = dot(ds[rows, :], wdn[:, gate_cols])
+            igs[rows, gate_cols] = (h * u * (s * (1.0 + g * (1.0 - s)))).astype(BF16)
+            igs[rows, up_cols] = (h * act).astype(BF16)
+
+        @pl.loop(0, width // step)
+        def _(n):
+            cols = lanes(n * step, step)
+            pgs[:, cols] = dot_nt(igs[rows, :], win[cols, :]).astype(BF16)
+
+        mine, theirs = rows_at(k * cap, cap), rows_at((1 - k) * cap, cap)
+        zcs = stage.at[q]
+        zcs[...] = dot_tn(spots(base + 1 - k).astype(BF16), pgs[theirs, :]).astype(BF16)
+        plane.give(q, zcs)
+        plane.zk[q] = dot_tn(spots(base + k).astype(BF16), pgs[mine, :]).astype(BF16)
+
+    def fold(q):
+        plane.fold(q, plane.zk[q])
+
+    for load in loads:
+        load.wait()
+    for n in range(planes - 1):
+        source = lax.rem(me + planes - 1 - n, planes)
+        remote(metas.at[source], metas.at[source], me_s.at[n], me_r.at[n], kp).wait_recv()
+    got(me + side, pl.ds(0, tok), 6)
+    group(0)
+
+    got(x_me, lo, 0)
+    move(x_me, lo, 4, yp)
+    move(x_me, lo, 7, kp)
+    got(y_me, hi, 3)
+    move(y_me, hi, 5, xp)
+    move(y_me, hi, 10, kp)
+    got(x_me, hi, 1)
+    move(x_me, hi, 8, kp)
+    got(y_me, lo, 2)
+    move(y_me, lo, 9, kp)
+    got(x_me + side, lo, 7)
+    got(x_me + side, hi, 8)
+    group(1)
+
+    got(d_me, lo, 4)
+    move(d_me, lo, 11, kp)
+    got(d_me, hi, 5)
+    move(d_me, hi, 12, kp)
+    got(y_me + side, lo, 9)
+    got(y_me + side, hi, 10)
+    group(2)
+    fold(1)
+    fold(2)
+    plane.near()
+    got(d_me + side, lo, 11)
+    got(d_me + side, hi, 12)
+    group(3)
+    fold(3)
+    plane.across()
+
+    tall = width // ctx
+
+    @pl.loop(0, ctx)
+    def _(n):
+        tile = dot_tn(ds[:, lanes(n * tall, tall)], hid[...]).astype(BF16)
+        for d in range(gwdn.shape[1]):
+            gwdn[n, d] = tile[d * gwdn.shape[2] : (d + 1) * gwdn.shape[2]]
+
+    line.step(1)
+    fold(0)
+    plane.turn()
+
+    for copy in sent:
+        copy.wait_send()
+
+    for q, base in enumerate(chips):
+
+        @pl.loop(0, width // step)
+        def _(n):
+            cols = lanes(n * step, step)
+            pgs[:, cols] = dot_nt(hid[pl.ds(q * 2 * cap, 2 * cap), :], wdn[cols, :]).astype(BF16)
+
+        for kk in range(2):
+            p = base + kk
+            i = q * 2 + kk
+            hot = spots(p)
+            rows = pgs[pl.ds(kk * cap, cap), :]
+            ggs[p, 0:1, :] = jnp.sum(hot * dot_nt(rows, cotb[p]), axis=0, keepdims=True)
+            scaled = (rows.astype(F32) * gate_of(p, hot)).astype(BF16)
+            agb[p] = dot_tn(hot.astype(BF16), scaled).astype(BF16)
+            pltpu.make_async_copy(agb.at[p], zout_h.at[p], st_sem.at[i]).start()
+    ggr[me] = ggs[me]
+    for n, (other, dev) in enumerate(others):
+        remote(ggs.at[other], ggr.at[me], gg_s.at[n], gg_r.at[n], dev).start()
+    line.step(2)
+    half_wide = ff
+
+    @pl.loop(0, 2 * ctx)
+    def _(n):
+        slot = lax.rem(n, 2)
+        rows = lanes(lax.div(n, 2) * tall, tall)
+        cols = lanes(slot * half_wide, half_wide)
+        tile = pgt.at[slot]
+        to = pltpu.make_async_copy(tile, gwin_h.at[rows, cols], load_sem.at[slot])
+
+        @pl.when(n >= 2)
+        def _():
+            to.wait()
+
+        tile[...] = dot_tn(xs[:, rows], igs[:, cols]).astype(BF16)
+        to.start()
+
+    for slot in range(2):
+        pltpu.make_async_copy(pgt.at[slot], gwin_h.at[pl.ds(0, tall), pl.ds(0, half_wide)], load_sem.at[slot]).wait()
+    line.step(3)
+    for rows, first, second in plane.total():
+        pg_out[rows, :] = (
+            plane.zk[0, rows].astype(F32) + first[...].astype(F32) + second[...].astype(F32)
+        )
+    for n in range(planes - 1):
+        source = lax.rem(me + planes - 1 - n, planes)
+        remote(ggr.at[source], ggr.at[source], gg_s.at[n], gg_r.at[n], kp).wait_recv()
+    for p in range(planes):
+        gg_out[p : p + 1, :] = ggr[p, 0:1, :]
+    line.final()
+    for i in range(planes):
+        pltpu.make_async_copy(agb.at[0], zout_h.at[0], st_sem.at[i]).wait()
+    for n, (other, dev) in enumerate(others):
+        remote(meta.at[other], metas.at[other], me_s.at[n], me_r.at[n], dev).wait_send()
+        remote(ggs.at[other], ggr.at[other], gg_s.at[n], gg_r.at[n], dev).wait_send()
+    plane.done()
+    line.done(ex_out)
+
+
+def run_ffn(cap, ffn, cot_all, meta, win, wdn, parts):
+    tok, width = ffn.shape
+    ff = wdn.shape[2]
+    planes = cot_all.shape[0]
+    ctx = win.shape[0]
+    rows = planes * cap
+    piece = width // (ctx * parts)
+    vm, anyspace = pl.BlockSpec(memory_space=pltpu.VMEM), pl.BlockSpec(memory_space=pl.ANY)
+    shape = jax.ShapeDtypeStruct
+    dma = pltpu.SemaphoreType.DMA
+    return pl.pallas_call(
+        functools.partial(ffn_kernel, cap),
+        out_shape=(
+            shape((planes, tok, width), BF16),
+            shape((tok, width), F32),
+            shape((planes, tok), F32),
+            shape((width, 2 * ff), BF16),
+            shape((ctx, piece, ff), BF16),
+        ),
+        in_specs=[vm, anyspace, vm, anyspace, anyspace],
+        out_specs=(anyspace, vm, vm, anyspace, vm),
+        scratch_shapes=[
+            pltpu.VMEM((planes, tok, width), BF16),
+            pltpu.VMEM((planes, 8, tok), F32),
+            pltpu.VMEM((planes, tok, width), BF16),
+            pltpu.VMEM((width, 2 * ff), BF16),
+            pltpu.VMEM((width, ff), BF16),
+            pltpu.VMEM((rows, width), BF16),
+            pltpu.VMEM((rows, width), BF16),
+            pltpu.VMEM((rows, ff), BF16),
+            pltpu.VMEM((rows, 2 * ff), BF16),
+            pltpu.VMEM((2 * cap, width), BF16),
+            pltpu.VMEM((planes, 8, tok), F32),
+            pltpu.VMEM((planes, 8, tok), F32),
+            pltpu.VMEM((4, tok, width), BF16),
+            pltpu.VMEM((ctx, parts, piece, ff), BF16),
+            pltpu.VMEM((2, width // ctx, ff), BF16),
+            dma((3,)),
+            dma((13,)),
+            dma((13,)),
+            dma((planes - 1,)),
+            dma((planes - 1,)),
+            dma((planes - 1,)),
+            dma((planes - 1,)),
+            dma((planes,)),
+        ]
+        + plane_scratch(tok, width)
+        + expert_scratch(ctx, parts, piece, ff),
+        compiler_params=pltpu.CompilerParams(
+            collective_id=1, has_side_effects=True, vmem_limit_bytes=62 * 2**20
+        ),
+        cost_estimate=pl.CostEstimate(flops=25 * 10**9, bytes_accessed=50 * 10**6, transcendentals=10**6),
+    )(ffn, cot_all, meta, win, wdn)
+
+
+def attend_back_kernel(
+    span,
+    resid,
+    cot,
+    pg,
+    gg,
+    gates,
+    attended,
+    ffn_in,
+    queries,
+    keys,
+    values,
+    lse,
+    trig,
+    wout,
+    router_t,
+    gain,
+    zout_h,
+    gwin_h,
+    output,
+    resid_grad,
+    mixed_grad,
+    out_red,
+    small,
+    ex_out,
+    *scratch,
+):
+    zkeep, gwin, osend, low, attg, mask, delta, dk, dv, dq, kvs, kvr = scratch[:12]
+    load_sem, kv_s, kv_r = scratch[12:15]
+    tok_refs, out_refs, line_refs = scratch[15:21], scratch[21:27], scratch[27:]
+    spot = Spot()
+    c, k, z, ctx = spot.c, spot.k, spot.z, spot.ctx
+    tok, width = cot.shape
+    cols = ex_out.shape[2]
+    block = out_red.shape[0]
+    heads_kv = KV_HEADS
+    group = HEADS // KV_HEADS
+    half_head = HEAD // 2
+    gwin_load = pltpu.make_async_copy(gwin_h.at[:, :, :, pl.ds(0, cols)], gwin, load_sem.at[0])
+    gwin_load.start()
+    keeps = []
+    for q, base in enumerate(spot.chips):
+        keeps.append(pltpu.make_async_copy(zout_h.at[base + k], zkeep.at[q], load_sem.at[1 + q]))
+        keeps[-1].start()
+    greet([spot.xp, spot.yp, spot.kp, spot.yk], spot.along())
+    tokens, weights = Plane(spot, *tok_refs), Plane(spot, *out_refs)
+    line = ExpertLine(spot, gwin, 0, cols, *line_refs)
+    for q, base in enumerate(spot.chips):
+        tokens.give(q, zout_h.at[base + 1 - k])
+    gwin_load.wait()
+    line.step(1)
+
+    gate = gates[...]
+    seen = gate * gg[...]
+    mix = seen - gate * jnp.sum(seen, axis=0, keepdims=True)
+    mix = jnp.concatenate([mix, jnp.zeros((HEAD - mix.shape[0], tok), F32)], axis=0)
+    logit_t = mix.astype(BF16)
+    r = resid[...]
+    inv = lax.rsqrt(jnp.mean(r * r, axis=-1, keepdims=True) + NORM_EPS)
+    plain = r * inv
+    ffn_grad = pg[...] + dot_tn(logit_t[: router_t.shape[0]], router_t[...])
+    gain_row = jnp.sum(ffn_grad * plain, axis=0, keepdims=True)
+    scaled = ffn_grad * gain[...]
+    back = cot[...].astype(F32) + inv * (
+        scaled - plain * jnp.mean(scaled * plain, axis=-1, keepdims=True)
+    )
+    resid_grad[...] = back
+    low[...] = back.astype(BF16)
+    lane = lax.broadcasted_iota(jnp.int32, (width, HEAD), 1)
+    gain_col = jnp.broadcast_to(gain_row, (HEAD, width)).T
+    routed = dot_tn(ffn_in[...], logit_t.T)
+    small[...] = jnp.where(lane == gate.shape[0], gain_col, routed).astype(BF16)
+
+    for q in (1, 2):
+        keeps[q].wait()
+        tokens.fold(q, zkeep[q])
+    tokens.near()
+    keeps[3].wait()
+    tokens.fold(3, zkeep[3])
+    tokens.across()
+    keeps[0].wait()
+    tokens.fold(0, zkeep[0])
+
+    for q in (1, 2, 3, 0):
+        at = lanes(spot.chips[q] * block, 2 * block)
+        osend[q] = dot_tn(low[:, at], attended[...]).astype(BF16)
+        weights.give(q, osend.at[q, rows_at((1 - k) * block, block)])
+
+    step = 256
+
+    @pl.loop(0, width // step)
+    def _(n):
+        at = lanes(n * step, step)
+        attg[:, at] = dot(low[...], wout[:, at]).astype(BF16)
+
+    seq = keys.shape[0]
+    spans = span.shape[1]
+    size = seq // spans
+    mine = spans // ctx
+    along_q = lax.broadcasted_iota(jnp.int32, (size, tok), 1)
+    q_pos = jnp.where(along_q < size, span[0, c * mine] * size, (span[0, c * mine + 1] - 1) * size) + along_q
+    for s in range(spans):
+        k_pos = span[0, s] * size + lax.broadcasted_iota(jnp.int32, (size, tok), 0)
+        mask[s * size : (s + 1) * size, :] = jnp.where(k_pos <= q_pos, 0.0, MASKED)
+
+    lane_h = lax.broadcasted_iota(jnp.int32, (tok, HEAD), 1)
+    deltas = jnp.zeros((tok, HEAD), F32)
+    for h in range(HEADS):
+        at = slice(h * HEAD, (h + 1) * HEAD)
+        term = jnp.sum(attg[:, at].astype(F32) * attended[:, at].astype(F32), axis=-1, keepdims=True)
+        deltas = jnp.where(lane_h == h, term, deltas)
+    delta[...] = deltas.T
+
+    def head(g, h):
+        at = lanes(h * HEAD, HEAD)
+        kv = slice(g * HEAD, (g + 1) * HEAD)
+        q, a = queries[:, at], attg[:, at]
+        soft = jnp.exp(dot_nt(keys[:, kv], q) + mask[...] - lse[pl.ds(h, 1), :])
+        prob = dot_nt(values[:, kv], a)
+        score = (soft * (prob - delta[pl.ds(h, 1), :])).astype(BF16)
+        dq[:, at] = dot_tn(score, keys[:, kv])
+        dk[...] += dot(score, q)
+        dv[...] += dot(soft.astype(BF16), a)
+
+    def send_kv(g):
+        for cc in range(ctx):
+            rows = slice(cc * tok, (cc + 1) * tok)
+            kvs[g, cc, :, :HEAD] = dk[rows, :].astype(BF16)
+            kvs[g, cc, :, HEAD:] = dv[rows, :].astype(BF16)
+        for n in range(1, ctx):
+            cc = lax.rem(c + n, ctx)
+            remote(kvs.at[g, cc], kvr.at[g, c], kv_s.at[g, n - 1], kv_r.at[g, n - 1], (spot.e, cc, z)).start()
+
+    def heads(g, first, count):
+        @pl.loop(first, first + count)
+        def _(h):
+            head(g, h)
+
+    def clear():
+        dk[...] = jnp.zeros(dk.shape, F32)
+        dv[...] = jnp.zeros(dv.shape, F32)
+
+    def own_part(q):
+        return osend[q, rows_at(k * block, block)]
+
+    clear()
+    heads(0, 0, 2)
+    for q in (1, 2):
+        weights.fold(q, own_part(q))
+    weights.near()
+    weights.fold(3, own_part(3))
+    weights.across()
+    weights.fold(0, own_part(0))
+    heads(0, 2, 2)
+    line.step(2)
+    heads(0, 4, 2)
+    send_kv(0)
+    tokens.turn()
+    clear()
+    heads(1, 6, 2)
+    line.step(3)
+    heads(1, 8, 2)
+    heads(1, 10, 2)
+    send_kv(1)
+    weights.turn()
+    for rows, first, second in tokens.total():
+        out_sum = tokens.zk[0, rows].astype(F32) + first[...].astype(F32) + second[...].astype(F32)
+        output[rows, :] = (resid[rows, :] + out_sum).astype(BF16)
+
+    cosine, sine = trig[0], trig[1]
+
+    def unrotate(w):
+        return w * cosine - pltpu.roll(w, half_head, 1) * sine
+
+    for h in range(HEADS):
+        at = slice(h * HEAD, (h + 1) * HEAD)
+        mixed_grad[:, at] = (unrotate(dq[:, at]) * HEAD**-0.5).astype(BF16)
+    line.final()
+    for rows, first, second in weights.total():
+        out_red[rows, :] = plus(weights.zk[0, rows], first[...], second[...])
+    for g in range(heads_kv):
+        own = kvs[g, c].astype(F32)
+        for n in range(1, ctx):
+            cc = lax.rem(c + ctx - n, ctx)
+            got = remote(kvr.at[g, cc], kvr.at[g, cc], kv_s.at[g, n - 1], kv_r.at[g, n - 1], spot.kp)
+            got.wait_recv()
+            own = own + kvr[g, cc].astype(F32)
+        at = width + g * HEAD
+        mixed_grad[:, at : at + HEAD] = unrotate(own[:, :HEAD]).astype(BF16)
+        at = width + (heads_kv + g) * HEAD
+        mixed_grad[:, at : at + HEAD] = own[:, HEAD:].astype(BF16)
+    for g in range(heads_kv):
+        for n in range(1, ctx):
+            cc = lax.rem(c + n, ctx)
+            remote(kvs.at[g, cc], kvr.at[g, cc], kv_s.at[g, n - 1], kv_r.at[g, n - 1], spot.kp).wait_send()
+    tokens.done()
+    weights.done()
+    line.done(ex_out)
+
+
+def run_attend_back(
+    span, resid, cot, pg, gg, gates, attended, ffn_in, queries, keys, values, lse, trig, wout, router_t, gain, zout, gwin
+):
+    tok, width = cot.shape
+    planes = zout.shape[0]
+    ctx, parts, piece, wide = gwin.shape
+    cols = wide // 2
+    block = width // planes
+    seq, kv_cols = keys.shape
+    vm, anyspace = pl.BlockSpec(memory_space=pltpu.VMEM), pl.BlockSpec(memory_space=pl.ANY)
+    sm = pl.BlockSpec(memory_space=pltpu.SMEM)
+    shape = jax.ShapeDtypeStruct
+    dma = pltpu.SemaphoreType.DMA
+    return pl.pallas_call(
+        attend_back_kernel,
+        out_shape=(
+            shape((tok, width), BF16),
+            shape((tok, width), F32),
+            shape((tok, width + 2 * kv_cols), BF16),
+            shape((block, width), BF16),
+            shape((width, HEAD), BF16),
+            shape((ctx, piece, cols), BF16),
+        ),
+        in_specs=[sm] + [vm] * 15 + [anyspace] * 2,
+        out_specs=(vm,) * 6,
+        scratch_shapes=[
+            pltpu.VMEM((4, tok, width), BF16),
+            pltpu.VMEM((ctx, parts, piece, cols), BF16),
+            pltpu.VMEM((4, 2 * block, width), BF16),
+            pltpu.VMEM((tok, width), BF16),
+            pltpu.VMEM((tok, width), BF16),
+            pltpu.VMEM((seq, tok), F32),
+            pltpu.VMEM((HEAD, tok), F32),
+            pltpu.VMEM((seq, HEAD), F32),
+            pltpu.VMEM((seq, HEAD), F32),
+            pltpu.VMEM((tok, width), F32),
+            pltpu.VMEM((KV_HEADS, ctx, tok, 2 * HEAD), BF16),
+            pltpu.VMEM((KV_HEADS, ctx, tok, 2 * HEAD), BF16),
+            dma((5,)),
+            dma((KV_HEADS, ctx - 1)),
+            dma((KV_HEADS, ctx - 1)),
+        ]
+        + plane_scratch(tok, width)
+        + plane_scratch(block, width)
+        + expert_scratch(ctx, parts, piece, cols),
+        compiler_params=pltpu.CompilerParams(
+            collective_id=2, has_side_effects=True, vmem_limit_bytes=62 * 2**20
+        ),
+        cost_estimate=pl.CostEstimate(flops=8 * 10**9, bytes_accessed=40 * 10**6, transcendentals=10**6),
+    )(
+        span, resid, cot, pg, gg, gates, attended, ffn_in, queries, keys, values, lse, trig, wout, router_t, gain, zout, gwin
+    )
+
+
+def last_kernel(
+    normed, mixed_grad, hidden, resid_grad, wqkv, gain, small, out_red, gwin_h, input_grad, qkv_out, proj_out, ex_out, *scratch
+):
+    gwin, asend, bsend, norm_grad, smalls, total, load_sem = scratch[:7]
+    a_refs, b_refs, qkv_refs, proj_refs, line_refs = (
+        scratch[7:13],
+        scratch[13:19],
+        scratch[19:22],
+        scratch[22:25],
+        scratch[25:],
+    )
+    spot = Spot()
+    k, z = spot.k, spot.z
+    tok, width = normed.shape
+    cols = ex_out.shape[2]
+    block = out_red.shape[0]
+    piece = proj_out.shape[0]
+    kv_wide = mixed_grad.shape[1] - width
+    load = pltpu.make_async_copy(gwin_h.at[:, :, :, pl.ds(cols, cols)], gwin, load_sem.at[0])
+    load.start()
+    greet([spot.xp, spot.yp, spot.kp, spot.yk], spot.along())
+    first, second = Plane(spot, *a_refs), Plane(spot, *b_refs)
+    line = ExpertLine(spot, gwin, 0, cols, *line_refs)
+
+    def shared_line(ref, refs):
+        def own(d):
+            return ref.at[rows_at(d * piece, piece)]
+
+        def adder(came, d):
+            came[...] = plus(came[...], own(d)[...])
+
+        return Line(spot, own, adder, *refs)
+
+    qkv, proj = shared_line(total, qkv_refs), shared_line(out_red, proj_refs)
+    def put_shared(to, ref, came):
+        to[...] = plus(ref[rows_at(z * piece, piece)], *(x[...] for x in came))
+
+    mine, theirs = rows_at(k * block, block), rows_at((1 - k) * block, block)
+    load.wait()
+    line.step(1)
+    proj.step(1)
+    for q in (1, 2, 3, 0):
+        at = lanes(spot.chips[q] * block, 2 * block)
+        asend[q] = dot_tn(normed[:, at], mixed_grad[:, :width]).astype(BF16)
+        first.give(q, asend.at[q, theirs])
+    first.fold(1, asend[1, mine])
+    first.fold(2, asend[2, mine])
+    first.near()
+    first.fold(3, asend[3, mine])
+    first.across()
+    first.fold(0, asend[0, mine])
+
+    step = 256
+
+    @pl.loop(0, width // step)
+    def _(n):
+        at = lanes(n * step, step)
+        norm_grad[:, at] = dot_nt(mixed_grad[...], wqkv[at, :])
+
+    x = hidden[...].astype(F32)
+    inv = lax.rsqrt(jnp.mean(x * x, axis=-1, keepdims=True) + NORM_EPS)
+    plain = x * inv
+    ng = norm_grad[...]
+    gain_row = jnp.sum(ng * plain, axis=0, keepdims=True)
+    scaled = ng * gain[...]
+    input_grad[...] = (
+        resid_grad[...]
+        + inv * (scaled - plain * jnp.mean(scaled * plain, axis=-1, keepdims=True))
+    ).astype(BF16)
+    lane = lax.broadcasted_iota(jnp.int32, (width, HEAD), 1)
+    gain_col = jnp.broadcast_to(gain_row, (HEAD, width)).T
+    smalls[...] = jnp.where(lane == HEAD - 1, gain_col, small[...].astype(F32)).astype(BF16)
+    for q in (1, 2, 3, 0):
+        at = lanes(spot.chips[q] * block, 2 * block)
+        bsend[q, :, :kv_wide] = dot_tn(normed[:, at], mixed_grad[:, width:]).astype(BF16)
+        bsend[q, :, kv_wide:] = smalls[rows_at(spot.chips[q] * block, 2 * block), :]
+        second.give(q, bsend.at[q, theirs])
+    first.turn()
+    second.fold(1, bsend[1, mine])
+    second.fold(2, bsend[2, mine])
+    second.near()
+    second.fold(3, bsend[3, mine])
+    second.across()
+    second.fold(0, bsend[0, mine])
+    line.step(2)
+    proj.step(2)
+    for rows, one, two in first.total():
+        total[rows, :width] = plus(first.zk[0, rows], one[...], two[...])
+    second.turn()
+    line.step(3)
+    proj.step(3)
+    for rows, one, two in second.total():
+        total[rows, width:] = plus(second.zk[0, rows], one[...], two[...])
+    qkv.step(1)
+    proj.final(lambda *came: put_shared(proj_out, out_red, came))
+    line.final()
+    qkv.step(2)
+    line.done(ex_out)
+    qkv.step(3)
+    proj.done()
+    first.done()
+    second.done()
+    qkv.final(lambda *came: put_shared(qkv_out, total, came))
+    qkv.done()
+
+
+def run_last(normed, mixed_grad, hidden, resid_grad, wqkv, gain, small, out_red, gwin):
+    tok, width = normed.shape
+    block = out_red.shape[0]
+    ctx, parts, rows, wide = gwin.shape
+    cols = wide // 2
+    piece = block // parts
+    rest = mixed_grad.shape[1] - width + HEAD
+    vm, anyspace = pl.BlockSpec(memory_space=pltpu.VMEM), pl.BlockSpec(memory_space=pl.ANY)
+    shape = jax.ShapeDtypeStruct
+    return pl.pallas_call(
+        last_kernel,
+        out_shape=(
+            shape((tok, width), BF16),
+            shape((piece, width + rest), BF16),
+            shape((piece, width), BF16),
+            shape((ctx, rows, cols), BF16),
+        ),
+        in_specs=[vm] * 8 + [anyspace],
+        out_specs=(vm,) * 4,
+        scratch_shapes=[
+            pltpu.VMEM((ctx, parts, rows, cols), BF16),
+            pltpu.VMEM((4, 2 * block, width), BF16),
+            pltpu.VMEM((4, 2 * block, rest), BF16),
+            pltpu.VMEM((tok, width), F32),
+            pltpu.VMEM((width, HEAD), BF16),
+            pltpu.VMEM((block, width + rest), BF16),
+            pltpu.SemaphoreType.DMA((1,)),
+        ]
+        + plane_scratch(block, width)
+        + plane_scratch(block, rest)
+        + line_scratch(parts, (piece, width + rest))
+        + line_scratch(parts, (piece, width))
+        + expert_scratch(ctx, parts, rows, cols),
+        compiler_params=pltpu.CompilerParams(
+            collective_id=3, has_side_effects=True, vmem_limit_bytes=62 * 2**20
+        ),
+        cost_estimate=pl.CostEstimate(flops=4 * 10**9, bytes_accessed=40 * 10**6, transcendentals=0),
+    )(normed, mixed_grad, hidden, resid_grad, wqkv, gain, small, out_red, gwin)
 
 
 def local(
@@ -136,6 +1065,150 @@
     ffn_in = (plain_two * gain_ffn).astype(jnp.bfloat16)
     logits = jnp.dot(ffn_in, router, preferred_element_type=jnp.float32)
     token_ids = expert_ids[0]
+    matches = token_ids[:, :, None] == jnp.arange(n_experts)[None, None, :]
+    chosen = jnp.any(matches, axis=1)
+    gates = softmax_last(jnp.where(chosen, logits, MASKED))
+    turn = jnp.sum(jnp.where(matches, priority[0][:, :, None], 0), axis=1)
+    turn = jnp.where(chosen, turn, tok_rows * top_k)
+    ranks = jnp.sum((turn[:, None, :] < turn[None, :, :]).astype(jnp.int32), axis=0)
+    slots = jnp.where(chosen & (ranks < capacity), ranks, -1).astype(jnp.float32)
+    gates_t = gates.T
+    meta = jnp.stack([slots.T, gates_t], axis=1)
+    meta = jnp.pad(meta, ((0, 0), (0, 6), (0, 0)))
+    cot_low = cotangent[0]
+    cot_all = lax.all_gather(cot_low, ("expert", "context"), axis=0)
+    parts = lax.axis_size("dp")
+    zout, pair_sum, gate_grad_t, gwin, down = run_ffn(
+        capacity, ffn_in, cot_all, meta, in_weight, down_weight, parts
+    )
+    gwin = gwin.reshape(contexts, parts, width // (contexts * parts), 2 * ff_width)
+    lse = jnp.pad(log_total.reshape(HEADS, tok_rows), ((0, 16 - HEADS), (0, 0)))
+    cosine, sine = cosine[:, 0, :], sine[:, 0, :]
+    trig = jnp.stack(
+        [jnp.concatenate([cosine, cosine], axis=1), jnp.concatenate([-sine, sine], axis=1)]
+    )
+    router_t = jnp.pad(router.T, ((0, 16 - n_experts), (0, 0)))
+    output, resid_grad, mixed_grad, out_red, small, in_one = run_attend_back(
+        span_order,
+        resid,
+        cot_low,
+        pair_sum,
+        gate_grad_t,
+        gates_t,
+        attended,
+        ffn_in,
+        queries.reshape(tok_rows, q_cols),
+        key_piece.reshape(seq_len, kv_cols),
+        value_piece.reshape(seq_len, kv_cols),
+        lse,
+        trig,
+        out_weight,
+        router_t,
+        gain_ffn[None],
+        zout,
+        gwin,
+    )
+    input_grad, qkv_sum, proj_sum, in_two = run_last(
+        normed, mixed_grad, hidden_in[0], resid_grad, qkv_weight, gain_attn[None], small, out_red, gwin
+    )
+    qkv_sum = qkv_sum.astype(jnp.float32)
+    smalls = qkv_sum[:, q_cols + 2 * kv_cols :]
+    return (
+        output[None],
+        input_grad[None],
+        smalls[:, HEAD - 1],
+        qkv_sum[:, : q_cols + 2 * kv_cols],
+        proj_sum.astype(jnp.float32),
+        smalls[:, n_experts],
+        smalls[:, :n_experts],
+        jnp.concatenate([in_one, in_two], axis=2).astype(jnp.float32),
+        down.astype(jnp.float32),
+    )
+
+
+def general(
+    hidden_in,
+    span_order,
+    expert_ids,
+    priority,
+    gain_attn,
+    qkv_weight,
+    out_weight,
+    gain_ffn,
+    router,
+    in_weight,
+    down_weight,
+    cotangent,
+):
+    tok_rows = hidden_in.shape[1]
+    width = hidden_in.shape[2]
+    contexts = lax.axis_size("context")
+    span_len = tok_rows // 2
+    seq_len = tok_rows * contexts
+    group = HEADS // KV_HEADS
+    q_cols = HEADS * HEAD
+    kv_cols = KV_HEADS * HEAD
+    scale = HEAD ** (-0.5)
+    local_experts = in_weight.shape[0]
+    n_experts = local_experts * lax.axis_size("expert")
+    top_k = expert_ids.shape[2]
+    capacity = (9 * tok_rows * top_k + 8 * n_experts - 1) // (8 * n_experts)
+    ff_width = down_weight.shape[2]
+    seq_spans = span_order[0]
+    stored = jnp.arange(seq_len) // span_len
+    all_pos = (seq_spans[stored] * span_len + jnp.arange(seq_len) % span_len).astype(jnp.float32)
+    my_pos = lax.dynamic_slice_in_dim(all_pos, lax.axis_index("context") * tok_rows, tok_rows)
+    cosine, sine = rope_tables(my_pos, HEAD)
+    inputs = hidden_in[0].astype(jnp.float32)
+    inv_one = lax.rsqrt(jnp.mean(inputs * inputs, axis=-1, keepdims=True) + NORM_EPS)
+    plain_one = inputs * inv_one
+    normed = (plain_one * gain_attn).astype(jnp.bfloat16)
+    mixed = jnp.dot(normed, qkv_weight, preferred_element_type=jnp.float32)
+    queries = (
+        rotate(mixed[:, :q_cols].reshape(tok_rows, HEADS, HEAD), cosine, sine) * scale
+    ).astype(jnp.bfloat16)
+    keys = rotate(
+        mixed[:, q_cols : q_cols + kv_cols].reshape(tok_rows, KV_HEADS, HEAD), cosine, sine
+    ).astype(jnp.bfloat16)
+    values = mixed[:, q_cols + kv_cols :].reshape(tok_rows, KV_HEADS, HEAD).astype(jnp.bfloat16)
+    grouped = queries.reshape(tok_rows, KV_HEADS, group, HEAD)
+
+    def key_scores(key_piece):
+        scores = jnp.einsum(
+            "qkgd,skd->kgqs", grouped, key_piece, preferred_element_type=jnp.float32
+        )
+        visible = all_pos[None, None, None, :] <= my_pos[None, None, :, None]
+        return (jnp.where(visible, scores, MASKED), visible)
+
+    running = jnp.full((KV_HEADS, group, tok_rows), MASKED, jnp.float32)
+    key_piece = lax.all_gather(keys, "context", axis=0, tiled=True)
+    value_piece = lax.all_gather(values, "context", axis=0, tiled=True)
+    scores, visible = key_scores(key_piece)
+    newest = jnp.maximum(running, jnp.max(scores, axis=-1))
+    weights = jnp.where(visible, jnp.exp(scores - newest[..., None]), 0.0)
+    totals = jnp.sum(weights, axis=-1)
+    accum = jnp.einsum(
+        "kgqs,skd->kgqd",
+        weights.astype(jnp.bfloat16),
+        value_piece,
+        preferred_element_type=jnp.float32,
+    )
+    running, totals, accum = (newest, totals, accum)
+    log_total = running + jnp.log(totals)
+    attended = (
+        (accum / totals[..., None])
+        .transpose(2, 0, 1, 3)
+        .reshape(tok_rows, q_cols)
+        .astype(jnp.bfloat16)
+    )
+    resid = inputs + jnp.einsum(
+        "rh,dh->rd", attended, out_weight, preferred_element_type=jnp.float32
+    )
+    inv_two = lax.rsqrt(jnp.mean(resid * resid, axis=-1, keepdims=True) + NORM_EPS)
+    plain_two = resid * inv_two
+    ffn_in = (plain_two * gain_ffn).astype(jnp.bfloat16)
+    logits = jnp.dot(ffn_in, router, preferred_element_type=jnp.float32)
+    token_ids = expert_ids[0]
     gates = softmax_last(jnp.take_along_axis(logits, token_ids, axis=1))
     slots = route(token_ids, priority[0], n_experts, capacity)
     pair_rows = jnp.repeat(ffn_in, top_k, axis=0)
@@ -338,4 +1411,6 @@
         P("expert", ("context", "dp"), None),
         P("expert", ("context", "dp"), None),
     )
-    return jax.shard_map(local, mesh=mesh, in_specs=in_specs, out_specs=out_specs, check_vma=False)
+    tuned = dict(mesh.shape) == {"expert": 2, "context": 4, "dp": 4}
+    body = local if tuned else general
+    return jax.shard_map(body, mesh=mesh, in_specs=in_specs, out_specs=out_specs, check_vma=False)

time: 1090 us -> 365 us (0.33)
  waiting for transfers between devices: 615 us -> 0.68 us
  Pallas kernels: 0 us -> 261 us
  local copies, waits for them, and re-layouts: 173 us -> 23.8 us
  matrix products: 133 us -> 18.5 us
  blocking collectives: 59.1 us -> 19.8 us
  other arithmetic: 58.8 us -> 20.7 us
  starting transfers between devices: 22 us -> 0.04 us
    unnamed x7 -> x1, waiting for transfers between devices: 510 us -> 0.68 us
    pallas_call x0 -> x3, Pallas kernels: none -> 261 us  [the longest x1 109 us: run_ffn(): pl.pallas_call(functools.partial(ffn_kernel, cap), out_shape=(shape((plan...]
    dot_general x16 -> x0, matrix products: 117 us -> none  [the longest x1 16.9 us: local(): jnp.einsum('erd,erf->def', part_rows, inner_grad, preferred_element_type=...]
    all_to_all x4 -> x0, waiting for transfers between devices: 105 us -> none  [the longest x1 36.3 us: local(): lax.all_to_all(send_rows.reshape(n_experts, capacity, width), 'expert', s...]
    convert_element_type x6 -> x2, local copies, waits for them, and re-layouts: 66.8 us -> 2.31 us  [the longest x1 1.15 us: local(): queries = (rotate(mixed[:, :q_cols].reshape(tok_rows, HEADS, HEAD), cosin...]
    unnamed x1 -> x0, blocking collectives: 42.1 us -> none
    gather x7 -> x0, local copies, waits for them, and re-layouts: 30.5 us -> none  [the longest x1 9.76 us: local(): pair_grad = back_padded[slots].reshape(tok_rows, top_k, width)]
    all_to_all x4 -> x0, starting transfers between devices: 21.6 us -> none  [the longest x1 5.55 us: local(): lax.all_to_all(row_grad, 'expert', split_axis=1, concat_axis=0, tiled=True)]
  transfers between devices with their start and end apart: 9 -> 1, of which waited for: 6 -> 0; matrix products, arithmetic and copies ran while one was open for 15% -> 14% of each run, Pallas kernels for 0% -> 0%
where the time goes in v2:
time: 365 us; the launch traced here: 359 us
  Pallas kernels  261 us (72%)
  local copies, waits for them, and re-layouts  23.8 us (7%)
  other arithmetic  20.7 us (6%)
  blocking collectives  19.8 us (5%)
  matrix products  18.5 us (5%)
  between operations  14.8 us (4%)
    pallas_call x1, Pallas kernels, run_ffn(): pl.pallas_call(functools.partial(ffn_kernel, cap), out_shape=(shape((plan...  109 us
    pallas_call x1, Pallas kernels, run_attend_back(): pl.pallas_call(attend_back_kernel, out_shape=(shape((tok, width), BF16),...  76.7 us
    pallas_call x1, Pallas kernels, run_last(): pl.pallas_call(last_kernel, out_shape=(shape((tok, width), BF16), shape((...  75.3 us
    all_gather x1, blocking collectives, local(): key_piece = lax.all_gather(keys, 'context', axis=0, tiled=True)  11.1 us
    all_gather x1, blocking collectives, local(): value_piece = lax.all_gather(values, 'context', axis=0, tiled=True)  8.64 us
    dot_general x1, matrix products, local(): jnp.einsum('kgqs,skd->kgqd', weights.astype(jnp.bfloat16), value_piece, p...  7.45 us
  transfers between devices with their start and end apart: 1, of which 0 were waited for; matrix products, arithmetic and copies ran while one was open for 14% of the time, Pallas kernels for 0%

profile of v2, /device:TPU:0, one launch (start us, length us, event | category | flops | bytes accessed | tf_op | source)
XLA Modules:
  0.0 359.4 jit_solution(8028224479093490451)
XLA Ops:
  7.2 0.0 copy-start.1
  7.2 0.0 all-gather.2.cloned.1.call-start
  7.2 0.7 all-gather.2.cloned.1.call-update
  7.9 1.3 broadcast_in_dim.91.gain
  9.2 1.4 fusion.6
  10.6 0.9 fusion.8.normed
  11.6 4.9 %fusion.39 = f32[256,2048]{1,0:T(8,128)S(1)} fusion(bf16[256,1536]{1,0:T(8,128)(2,1)S(1)} %fusion.8.normed, bf16[1536,2048]{1,0:T(8,128)(2,1)} %wqkv.1), kind=kOutput, calls=%fused_computation.91 | convolution fusion | flops 1610612736 | bytes 9175040 | tf_op jit(solution)/shard_map/dot_general | solution.py:1022
  16.4 0.0 copy-start.19
  16.5 0.0 copy-start.21
  16.5 0.1 slice.71
  16.7 0.5 copy-done.19
  17.1 0.6 broadcast_in_dim.89.gain
  17.8 0.8 copy.83
  18.6 0.6 fusion.38
  19.2 4.5 %compare_select_fusion.1 = s32[1024,1]{0,1:T(1,128)S(1)} fusion(s32[]{:T(128)} %bitcast.2, s32[]{:T(128)} %bitcast.3, s32[]{:T(128)} %bitcast.4, s32[]{:T(128)} %bitcast.5, s32[]{:T(128)} %bitcast.6, s32[]{:T(128)} %bitcast.8, s32[]{:T(128)} %bitcast.7), kind=kLoop, calls=%fused_computation.50 | loop fusion | flops 23552 | bytes 4124 | tf_op jit(solution)/shard_map/gather | solution.py:1015
  23.8 0.7 fusion.28
  24.4 0.1 dynamic_slice.3
  24.5 1.2 fusion.19
  25.7 0.1 copy.78
  25.8 0.1 copy.77
  25.9 0.1 copy.93
  26.0 1.6 copy.76
  27.6 0.1 reshape.227
  27.8 8.6 %all_gather.10 = bf16[1024,2,128]{0,2,1:T(8,128)(2,1)S(1)} all-gather(bf16[256,2,128]{0,2,1:T(8,128)(2,1)S(1)} %bitcast.110), channel_id=1, replica_groups=mesh['expert'=2,'context'=4,'dp'=4] {'context'}, dimensions={0}, use_global_device_ids=true | all-gather | bytes 655360 | tf_op jit(solution)/shard_map/all_gather | solution.py:1041
  36.4 1.0 copy.94.values
  37.4 2.0 multiply_subtract_fusion
  39.4 1.6 copy.79
  41.0 1.6 copy.80
  42.6 0.2 fusion.10
  42.8 1.2 copy.88.queries
  44.0 0.3 fusion.37
  44.3 0.1 subtract_convert_fusion
  44.4 0.1 pad_maximum_fusion.1
  44.5 11.1 %all_gather.9 = bf16[1024,2,128]{2,0,1:T(8,128)(2,1)S(1)} all-gather(bf16[256,2,128]{2,0,1:T(8,128)(2,1)S(1)} %pad_maximum_fusion.1), channel_id=1, replica_groups=mesh['expert'=2,'context'=4,'dp'=4] {'context'}, dimensions={0}, use_global_device_ids=true | all-gather | bytes 655360 | tf_op jit(solution)/shard_map/all_gather | solution.py:1040
  55.7 0.2 broadcast_compare_fusion
  55.9 2.0 fusion
  58.0 2.5 fusion.1
  60.5 2.0 copy-done
  62.5 7.5 %fusion.11 = bf16[256,2,6,128]{0,3,2,1:T(8,128)(2,1)S(1)} fusion(f32[2,1024,256,6]{2,1,3,0:T(8,128)} %copy-done, f32[2,6,256]{2,1,0:T(8,128)S(1)} %broadcast_maximum_fusion, pred[256,1024]{0,1:T(8,128)(4,1)S(1)} %broadcast_compare_fusion, f32[256,2,6]{0,2,1:T(8,128)S(1)} %bitcast.112, bf16[1024,2,128]{0,2,1:T(8,128)(2,1)S(1)} %copy-done.7), kind=kOutput, calls=%fused_computation.19 | convolution fusion | flops 818675712 | bytes 14180352 | tf_op jit(solution)/shard_map/kgqs,skd->kgqd/dot_general | solution.py:1046
  69.9 1.2 copy.87.attended
  71.1 3.9 %multiply_reduce_fusion = (f32[256]{0:T(256)S(1)}, f32[256,1536]{1,0:T(8,128)S(1)}) fusion(bf16[256,1536]{0,1:T(8,128)(2,1)S(1)} %bitcast.109, bf16[1536,1536]{1,0:T(8,128)(2,1)} %wout.1, bf16[1,256,1536]{2,1,0:T(8,128)(2,1)S(1)} %copy-done.1), kind=kOutput, calls=%fused_computation.21 | convolution fusion | flops 1209532160 | bytes 7865344 | tf_op jit(solution)/shard_map/rh,dh->rd/dot_general | solution.py:1060
  75.0 0.2 multiply_convert_fusion.ffn.ffn_in
  75.2 0.5 copy-done.18
  75.7 0.3 fusion.29
  76.1 0.3 convert_reduce_fusion
  76.5 0.6 pad.13.lse
  77.1 0.6 pad.12.clone.meta
  77.8 0.6 pad.14.router_t
  78.4 0.1 maximum_bitcast_fusion
  78.5 0.7 pad_maximum_fusion.trig
  79.3 0.9 copy_bitcast_fusion.keys
  80.1 109.1 %shard_map.187 = (bf16[8,256,1536]{2,1,0:T(8,128)(2,1)}, f32[256,1536]{1,0:T(8,128)}, f32[8,256]{1,0:T(8,128)}, bf16[1536,1536]{1,0:T(8,128)(2,1)}, bf16[4,96,768]{2,1,0:T(8,128)(2,1)}) custom-call(bf16[256,1536]{1,0:T(8,128)(2,1)} %copy-done.5, bf16[8,256,1536]{2,1,0:T(8,128)(2,1)} %all-gather.2.cloned.1.call-done.cot_h, f32[8,8,256]{2,1,0:T(8,128)} %pad.12.clone.meta, ...), custom_call_target="tpu_custom_call" | custom-call | flops 24999999488 | bytes 50000000 | tf_op jit(solution)/shard_map/pallas_call | solution.py:540
  189.3 76.7 %shard_map.188 = (bf16[256,1536]{1,0:T(8,128)(2,1)}, f32[256,1536]{1,0:T(8,128)}, bf16[256,2048]{1,0:T(8,128)(2,1)}, bf16[192,1536]{1,0:T(8,128)(2,1)}, bf16[153...) custom-call(s32[1,8]{1,0:T(1,128)} %span.1, f32[256,1536]{1,0:T(8,128)} %copy-done.10, bf16[256,1536]{1,0:T(8,128)(2,1)} %bitcast.105, ...), custom_call_target="tpu_custom_call" | custom-call | flops 8000000000 | bytes 40000000 | tf_op jit(solution)/shard_map/pallas_call | solution.py:798
  266.0 75.3 %shard_map.189 = (bf16[256,1536]{1,0:T(8,128)(2,1)}, bf16[48,2176]{1,0:T(8,128)(2,1)}, bf16[48,1536]{1,0:T(8,128)(2,1)}, bf16[4,96,768]{2,1,0:T(8,128)(2,1)}) custom-call(bf16[256,1536]{1,0:T(8,128)(2,1)} %copy-done.4, bf16[256,2048]{1,0:T(8,128)(2,1)} %get-tuple-element.29.mixed_grad, bf16[256,1536]{1,0:T(8,128)(2,1)} %bitcast.97, ...), custom_call_target="tpu_custom_call" | custom-call | flops 4000000000 | bytes 40000000 | tf_op jit(solution)/shard_map/pallas_call | solution.py:954
  341.3 0.8 slice.77
  342.2 1.7 slice.75
  343.9 1.0 convert_element_type.85
  344.8 0.7 copy.89
  345.5 1.6 convert_element_type.86
  347.1 0.7 slice_reduce_fusion
  347.8 1.1 convert_element_type.88
  349.0 1.7 maximum_convert_fusion
  350.6 0.9 copy.106
  351.5 0.9 copy.107
  (66 shorter events, 0.3 us)
Async XLA Ops:
  7.2 3.4 copy-start.1
  7.2 72.9 %all-gather.2.cloned.1.call-start = ((), (), s32[]{:S(2)}) async-start(), calls=%async_computation | async-start | bytes 7077888 | tf_op jit(solution)/shard_map/all_gather | solution.py:1079
  11.6 4.9 %copy-start.4 = (bf16[256,1536]{1,0:T(8,128)(2,1)}, bf16[256,1536]{1,0:T(8,128)(2,1)S(1)}, u32[]{:S(2)}) copy-start(bf16[256,1536]{1,0:T(8,128)(2,1)S(1)} %fusion.8.normed) | copy-start | bytes 2359300
  16.4 0.7 copy-start.19
  16.4 1.3 copy-start.23
  16.5 1.3 copy-start.26
  16.5 2.1 copy-start.21
  24.5 1.5 copy-start.24
  25.7 2.0 copy-start.8
  36.4 1.0 copy-start.6
  42.8 1.5 copy-start.9
  42.8 12.8 %copy-start.25 = (f32[256]{0:T(256)S(1)}, f32[256]{0:T(256)}, u32[]{:S(2)}) copy-start(f32[256]{0:T(256)} %copy-done.24) | copy-start | bytes 3076
  44.0 11.9 %copy-start.2 = (f32[256,12,64]{2,0,1:T(8,128)S(1)}, f32[256,12,64]{2,0,1:T(8,128)}, u32[]{:S(2)}) copy-start(f32[256,12,64]{2,0,1:T(8,128)} %copy.79) | copy-start | bytes 2359300
  44.0 11.9 %copy-start.3 = (f32[256,12,64]{2,0,1:T(8,128)S(1)}, f32[256,12,64]{2,0,1:T(8,128)}, u32[]{:S(2)}) copy-start(f32[256,12,64]{2,0,1:T(8,128)} %copy.80) | copy-start | bytes 2359300
  57.9 4.5 %copy-start = (f32[2,1024,256,6]{2,1,3,0:T(8,128)}, f32[2,1024,256,6]{2,1,3,0:T(8,128)S(1)}, u32[]{:S(2)}) copy-start(f32[2,1024,256,6]{2,1,3,0:T(8,128)S(1)} %get-tuple-element.95) | copy-start | bytes 37748740
  57.9 4.5 %copy-start.7 = (bf16[1024,2,128]{0,2,1:T(8,128)(2,1)S(1)}, bf16[1024,2,128]{0,2,1:T(8,128)(2,1)}, u32[]{:S(2)}) copy-start(bf16[1024,2,128]{0,2,1:T(8,128)(2,1)} %copy-done.6) | copy-start | bytes 1572868
  71.1 3.9 %copy-start.20 = (f32[1536]{0:T(1024)S(1)}, f32[1536]{0:T(1024)}, u32[]{:S(2)}) copy-start(f32[1536]{0:T(1024)} %param.19) | copy-start | bytes 18436
  75.0 3.5 copy-start.10
  75.0 0.7 copy-start.18
  75.0 1.1 copy-start.17
  75.0 3.4 copy-start.16
  75.7 4.4 %copy-start.5 = (bf16[256,1536]{1,0:T(8,128)(2,1)}, bf16[256,1536]{1,0:T(8,128)(2,1)S(1)}, u32[]{:S(2)}) copy-start(bf16[256,1536]{1,0:T(8,128)(2,1)S(1)} %multiply_convert_fusion.ffn.ffn_in) | copy-start | bytes 2359300
  76.5 112.8 %copy-start.22 = (f32[8,256]{1,0:T(8,128)}, f32[8,256]{1,0:T(8,128)S(1)}, u32[]{:S(2)}) copy-start(f32[8,256]{1,0:T(8,128)S(1)} %fusion.23.gates) | copy-start | bytes 24580
  341.3 6.5 %copy-start.13 = (bf16[4,96,768]{2,1,0:T(8,128)(2,1)S(1)}, bf16[4,96,768]{2,1,0:T(8,128)(2,1)}, u32[]{:S(2)}) copy-start(bf16[4,96,768]{2,1,0:T(8,128)(2,1)} %get-tuple-element.38) | copy-start | bytes 1769476
  341.3 7.6 %copy-start.14 = (bf16[4,96,768]{2,1,0:T(8,128)(2,1)S(1)}, bf16[4,96,768]{2,1,0:T(8,128)(2,1)}, u32[]{:S(2)}) copy-start(bf16[4,96,768]{2,1,0:T(8,128)(2,1)} %get-tuple-element.36) | copy-start | bytes 1769476
  341.3 7.6 %copy-start.15 = (bf16[4,96,768]{2,1,0:T(8,128)(2,1)S(1)}, bf16[4,96,768]{2,1,0:T(8,128)(2,1)}, u32[]{:S(2)}) copy-start(bf16[4,96,768]{2,1,0:T(8,128)(2,1)} %get-tuple-element.37) | copy-start | bytes 1769476
  348.9 1.7 copy-start.11
  348.9 2.6 copy-start.12
Sparse Core Ops, SparseCore 0:
  9.9 51.0 all-gather.1

commit v3 on v2

--- a/solution.py
+++ b/solution.py
@@ -319,20 +319,302 @@
     ]
 
 
+class Gather:
+    def __init__(self, spot, own, buf, s, r):
+        self.spot, self.own, self.buf, self.s, self.r = spot, own, buf, s, r
+        half = own.shape[0] // 2
+        self.lo, self.hi = pl.ds(0, half), pl.ds(half, half)
+        self.x_me, self.y_me, self.d_me = (base + spot.k for base in spot.chips[1:])
+        self.side = 1 - 2 * spot.k
+        self.sent = []
+
+    def push(self, src, dst, i, dev):
+        copy = remote(src, dst, self.s.at[i], self.r.at[i], dev)
+        copy.start()
+        self.sent.append(copy)
+
+    def move(self, p, rows, i, dev):
+        self.push(self.buf.at[p, rows], self.buf.at[p, rows], i, dev)
+
+    def got(self, p, rows, i):
+        to = self.buf.at[p, rows]
+        remote(to, to, self.s.at[i], self.r.at[i], self.spot.kp).wait_recv()
+
+    def start(self):
+        me, own, lo, hi = self.spot.me, self.own, self.lo, self.hi
+        self.push(own.at[lo], self.buf.at[me, lo], 0, self.spot.xp)
+        self.push(own.at[hi], self.buf.at[me, hi], 3, self.spot.yp)
+        self.push(own.at[lo], self.buf.at[me, lo], 6, self.spot.kp)
+        self.push(own.at[hi], self.buf.at[me, hi], 13, self.spot.kp)
+        self.push(own.at[hi], self.buf.at[me, hi], 1, self.spot.xp)
+        self.push(own.at[lo], self.buf.at[me, lo], 2, self.spot.yp)
+
+    def first(self):
+        spot = self.spot
+        self.got(self.x_me, self.lo, 0)
+        self.move(self.x_me, self.lo, 4, spot.yp)
+        self.move(self.x_me, self.lo, 7, spot.kp)
+        self.got(self.y_me, self.hi, 3)
+        self.move(self.y_me, self.hi, 5, spot.xp)
+        self.move(self.y_me, self.hi, 10, spot.kp)
+
+    def second(self):
+        self.got(self.x_me, self.hi, 1)
+        self.move(self.x_me, self.hi, 8, self.spot.kp)
+        self.got(self.y_me, self.lo, 2)
+        self.move(self.y_me, self.lo, 9, self.spot.kp)
+
+    def third(self):
+        self.got(self.d_me, self.lo, 4)
+        self.move(self.d_me, self.lo, 11, self.spot.kp)
+        self.got(self.d_me, self.hi, 5)
+        self.move(self.d_me, self.hi, 12, self.spot.kp)
+
+    def other_core(self, q):
+        low_sem, high_sem = ((6, 13), (7, 8), (9, 10), (11, 12))[q]
+        p = (self.spot.me, self.x_me, self.y_me, self.d_me)[q] + self.side
+        self.got(p, self.lo, low_sem)
+        self.got(p, self.hi, high_sem)
+
+    def done(self):
+        for copy in self.sent:
+            copy.wait_send()
+
+
+GATHER_COPIES = 14
+
+
+def front_kernel(
+    cap,
+    span,
+    hidden,
+    cot,
+    gain_one,
+    freqs,
+    gain_two,
+    router_t,
+    ids_t,
+    turn_t,
+    wqkv_h,
+    wout_h,
+    normed,
+    queries,
+    kv,
+    lse,
+    attended,
+    resid,
+    ffn_in,
+    trig,
+    meta,
+    cot_all,
+    wqkv,
+    wout,
+    mask,
+    vt,
+    load_sem,
+    kv_s,
+    kv_r,
+    co_s,
+    co_r,
+):
+    spot = Spot()
+    c, ctx, k = spot.c, spot.ctx, spot.k
+    tok, width = hidden.shape
+    group = HEADS // KV_HEADS
+    kv_cols = KV_HEADS * HEAD
+    half_head = HEAD // 2
+    seq = kv.shape[0]
+    spans = span.shape[1]
+    size = seq // spans
+    mine = spans // ctx
+    n_experts = meta.shape[0]
+    loads = [
+        pltpu.make_async_copy(wqkv_h.at[:, pl.ds(width, 2 * kv_cols)], wqkv.at[:, pl.ds(width, 2 * kv_cols)], load_sem.at[0]),
+        pltpu.make_async_copy(wqkv_h.at[:, pl.ds(0, width)], wqkv.at[:, pl.ds(0, width)], load_sem.at[1]),
+        pltpu.make_async_copy(wout_h, wout, load_sem.at[2]),
+        pltpu.make_async_copy(cot, cot_all.at[spot.me], load_sem.at[3]),
+    ]
+    for load in loads:
+        load.start()
+    greet([spot.xp, spot.yp, spot.kp])
+    gather = Gather(spot, cot, cot_all, co_s, co_r)
+
+    x = hidden[...].astype(F32)
+    inv = lax.rsqrt(jnp.mean(x * x, axis=-1, keepdims=True) + NORM_EPS)
+    normed[...] = (x * inv * gain_one[...]).astype(BF16)
+
+    along = lax.broadcasted_iota(jnp.int32, (tok, HEAD), 0)
+    start_one, start_two = span[0, c * mine] * size, (span[0, c * mine + 1] - 1) * size
+    place = jnp.where(along < size, start_one, start_two) + along
+    angle = place.astype(F32) * freqs[...]
+    cosine, sine = jnp.cos(angle), jnp.sin(angle)
+    lane = lax.broadcasted_iota(jnp.int32, (tok, HEAD), 1)
+    sine = jnp.where(lane < half_head, -sine, sine)
+    trig[0] = cosine
+    trig[1] = sine
+
+    def rotate_in(w):
+        return w * cosine + pltpu.roll(w, half_head, 1) * sine
+
+    loads[0].wait()
+    raw = dot(normed[...], wqkv[:, width:])
+    own = rows_at(c * tok, tok)
+    for g in range(KV_HEADS):
+        at = slice(g * HEAD, (g + 1) * HEAD)
+        kv[own, at] = rotate_in(raw[:, at]).astype(BF16)
+    kv[own, kv_cols:] = raw[:, kv_cols:].astype(BF16)
+
+    def kv_copy(rows, i, dev):
+        return remote(kv.at[rows], kv.at[rows], kv_s.at[i], kv_r.at[i], dev)
+
+    flip_c = lax.rem(c + 2, ctx)
+    near_c = c + 1 - 2 * k
+    across_c = lax.rem(near_c + 2, ctx)
+    sent = [kv_copy(own, 1, spot.yp), kv_copy(own, 0, spot.kp)]
+    for copy in sent:
+        copy.start()
+    gather.start()
+
+    loads[1].wait()
+    step = 256
+
+    @pl.loop(0, width // step)
+    def _(n):
+        at = lanes(n * step, step)
+        raw = dot(normed[...], wqkv[:, at])
+        for i in range(step // HEAD):
+            w = raw[:, i * HEAD : (i + 1) * HEAD]
+            queries[:, lanes(n * step + i * HEAD, HEAD)] = (rotate_in(w) * HEAD**-0.5).astype(BF16)
+
+    flip = rows_at(flip_c * tok, tok)
+    kv_copy(flip, 1, spot.kp).wait_recv()
+    sent.append(kv_copy(flip, 2, spot.kp))
+    sent[-1].start()
+
+    expert = lax.broadcasted_iota(jnp.int32, (n_experts, tok), 0)
+    never = tok * ids_t.shape[0]
+    turn = jnp.full((n_experts, tok), never, jnp.int32)
+    for i in range(ids_t.shape[0]):
+        turn = jnp.where(ids_t[i : i + 1, :] == expert, turn_t[i : i + 1, :], turn)
+    turn_f = turn.astype(F32)
+    tall = jnp.concatenate([turn_f, jnp.full((HEAD - n_experts, tok), float(never), F32)], axis=0).T
+    meta[...] = jnp.zeros(meta.shape, F32)
+    for g in range(n_experts):
+        row = turn_f[g : g + 1, :]
+        rank = jnp.sum(jnp.where(tall[:, g : g + 1] < row, 1.0, 0.0), axis=0, keepdims=True)
+        meta[g, 0:1, :] = jnp.where((row < never) & (rank < cap), rank, -1.0)
+
+    along_q = lax.broadcasted_iota(jnp.int32, (size, tok), 1)
+    q_pos = jnp.where(along_q < size, start_one, start_two) + along_q
+    for s in range(spans):
+        k_pos = span[0, s] * size + lax.broadcasted_iota(jnp.int32, (size, tok), 0)
+        mask[s * size : (s + 1) * size, :] = jnp.where(k_pos <= q_pos, 0.0, MASKED)
+
+    near, across = rows_at(near_c * tok, tok), rows_at(across_c * tok, tok)
+    kv_copy(near, 0, spot.kp).wait_recv()
+    kv_copy(across, 2, spot.kp).wait_recv()
+    for g in range(KV_HEADS):
+        vt[g] = kv[:, kv_cols + g * HEAD : kv_cols + (g + 1) * HEAD].astype(F32).T.astype(BF16)
+    lse[...] = jnp.zeros(lse.shape, F32)
+
+    def heads(g, first, count):
+        @pl.loop(first, first + count)
+        def _(h):
+            at = lanes(h * HEAD, HEAD)
+            scores = dot_nt(kv[:, g * HEAD : (g + 1) * HEAD], queries[:, at]) + mask[...]
+            top = jnp.max(scores, axis=0, keepdims=True)
+            weights = jnp.exp(scores - top)
+            total = jnp.sum(weights, axis=0, keepdims=True)
+            lse[pl.ds(h, 1), :] = top + jnp.log(total)
+            out = dot(vt[g], weights.astype(BF16)) / total
+            attended[:, at] = out.T.astype(BF16)
+
+    heads(0, 0, 3)
+    gather.first()
+    heads(0, 3, 3)
+    heads(1, 6, 3)
+    gather.second()
+    heads(1, 9, 3)
+
+    loads[2].wait()
+
+    @pl.loop(0, width // step)
+    def _(n):
+        at = lanes(n * step, step)
+        resid[:, at] = hidden[:, at].astype(F32) + dot_nt(attended[...], wout[at, :])
+
+    r = resid[...]
+    inv = lax.rsqrt(jnp.mean(r * r, axis=-1, keepdims=True) + NORM_EPS)
+    ffn_in[...] = (r * inv * gain_two[...]).astype(BF16)
+    logits = dot_nt(router_t[...], ffn_in[...])[:n_experts]
+    logits = jnp.where(turn < never, logits, MASKED)
+    shifted = jnp.exp(logits - jnp.max(logits, axis=0, keepdims=True))
+    gates = shifted / jnp.sum(shifted, axis=0, keepdims=True)
+    for g in range(n_experts):
+        meta[g, 1:2, :] = gates[g : g + 1, :]
+    gather.third()
+    for q in range(4):
+        gather.other_core(q)
+    loads[3].wait()
+    gather.done()
+    for copy in sent:
+        copy.wait_send()
+
+
+def run_front(cap, span, hidden, cot, gain_one, freqs, gain_two, router_t, ids_t, turn_t, wqkv, wout, ctx, planes):
+    tok, width = hidden.shape
+    seq = tok * ctx
+    n_experts = planes
+    kv_cols = 2 * KV_HEADS * HEAD
+    vm, anyspace = pl.BlockSpec(memory_space=pltpu.VMEM), pl.BlockSpec(memory_space=pl.ANY)
+    sm = pl.BlockSpec(memory_space=pltpu.SMEM)
+    shape = jax.ShapeDtypeStruct
+    dma = pltpu.SemaphoreType.DMA
+    return pl.pallas_call(
+        functools.partial(front_kernel, cap),
+        out_shape=(
+            shape((tok, width), BF16),
+            shape((tok, width), BF16),
+            shape((seq, kv_cols), BF16),
+            shape((16, tok), F32),
+            shape((tok, width), BF16),
+            shape((tok, width), F32),
+            shape((tok, width), BF16),
+            shape((2, tok, HEAD), F32),
+            shape((n_experts, 8, tok), F32),
+            shape((planes, tok, width), BF16),
+        ),
+        in_specs=[sm] + [vm] * 8 + [anyspace] * 2,
+        out_specs=(vm,) * 9 + (anyspace,),
+        scratch_shapes=[
+            pltpu.VMEM(wqkv.shape, BF16),
+            pltpu.VMEM(wout.shape, BF16),
+            pltpu.VMEM((seq, tok), F32),
+            pltpu.VMEM((KV_HEADS, HEAD, seq), BF16),
+            dma((4,)),
+            dma((3,)),
+            dma((3,)),
+            dma((GATHER_COPIES,)),
+            dma((GATHER_COPIES,)),
+        ],
+        compiler_params=pltpu.CompilerParams(
+            collective_id=4, has_side_effects=True, vmem_limit_bytes=56 * 2**20
+        ),
+        cost_estimate=pl.CostEstimate(flops=5 * 10**9, bytes_accessed=20 * 10**6, transcendentals=4 * 10**6),
+    )(span, hidden, cot, gain_one, freqs, gain_two, router_t, ids_t, turn_t, wqkv, wout)
+
+
 def ffn_kernel(cap, ffn, cot_h, meta, win_h, wdn_h, zout_h, pg_out, gg_out, gwin_h, ex_out, *scratch):
     agb, metas, cotb, win, wdn, xs, ds, hid, igs, pgs, ggs, ggr, stage, gwdn, pgt = scratch[:15]
     load_sem, ag_s, ag_r, me_s, me_r, gg_s, gg_r, st_sem = scratch[15:23]
     plane_refs, line_refs = scratch[23:29], scratch[29:]
     spot = Spot()
-    e, c, k, me = spot.e, spot.c, spot.k, spot.me
-    xp, yp, kp = spot.xp, spot.yp, spot.kp
+    c, k, me = spot.c, spot.k, spot.me
+    kp = spot.kp
     tok, width = ffn.shape
-    half = tok // 2
     ff = wdn.shape[1]
     planes, ctx = spot.planes, spot.ctx
     chips = spot.chips
-    x_me, y_me, d_me = (base + k for base in chips[1:])
-    side = 1 - 2 * k
 
     loads = [
         pltpu.make_async_copy(win_h.at[c], win, load_sem.at[0]),
@@ -345,27 +627,10 @@
     greet([dev for _, dev in others], spot.along())
     plane = Plane(spot, *plane_refs)
     line = ExpertLine(spot, gwdn, 0, ff, *line_refs)
-    lo, hi = plane.lo, plane.hi
-    sent = []
-
-    def push(src, dst, i, dev):
-        copy = remote(src, dst, ag_s.at[i], ag_r.at[i], dev)
-        copy.start()
-        sent.append(copy)
-
-    def move(p, rows, i, dev):
-        push(agb.at[p, rows], agb.at[p, rows], i, dev)
-
-    def got(p, rows, i):
-        remote(agb.at[p, rows], agb.at[p, rows], ag_s.at[i], ag_r.at[i], kp).wait_recv()
-
+    gather = Gather(spot, ffn, agb, ag_s, ag_r)
     for step, (other, dev) in enumerate(others):
         remote(meta.at[other], metas.at[me], me_s.at[step], me_r.at[step], dev).start()
-    push(ffn.at[lo], agb.at[me, lo], 0, xp)
-    push(ffn.at[hi], agb.at[me, hi], 3, yp)
-    push(ffn, agb.at[me], 6, kp)
-    push(ffn.at[hi], agb.at[me, hi], 1, xp)
-    push(ffn.at[lo], agb.at[me, lo], 2, yp)
+    gather.start()
     agb[me] = ffn[...]
     metas[me] = meta[me]
     slot_rows = lax.broadcasted_iota(jnp.int32, (cap, tok), 0).astype(F32)
@@ -420,35 +685,19 @@
     for n in range(planes - 1):
         source = lax.rem(me + planes - 1 - n, planes)
         remote(metas.at[source], metas.at[source], me_s.at[n], me_r.at[n], kp).wait_recv()
-    got(me + side, pl.ds(0, tok), 6)
+    gather.other_core(0)
     group(0)
-
-    got(x_me, lo, 0)
-    move(x_me, lo, 4, yp)
-    move(x_me, lo, 7, kp)
-    got(y_me, hi, 3)
-    move(y_me, hi, 5, xp)
-    move(y_me, hi, 10, kp)
-    got(x_me, hi, 1)
-    move(x_me, hi, 8, kp)
-    got(y_me, lo, 2)
-    move(y_me, lo, 9, kp)
-    got(x_me + side, lo, 7)
-    got(x_me + side, hi, 8)
+    gather.first()
+    gather.second()
+    gather.other_core(1)
     group(1)
-
-    got(d_me, lo, 4)
-    move(d_me, lo, 11, kp)
-    got(d_me, hi, 5)
-    move(d_me, hi, 12, kp)
-    got(y_me + side, lo, 9)
-    got(y_me + side, hi, 10)
+    gather.third()
+    gather.other_core(2)
     group(2)
     fold(1)
     fold(2)
     plane.near()
-    got(d_me + side, lo, 11)
-    got(d_me + side, hi, 12)
+    gather.other_core(3)
     group(3)
     fold(3)
     plane.across()
@@ -465,8 +714,7 @@
     fold(0)
     plane.turn()
 
-    for copy in sent:
-        copy.wait_send()
+    gather.done()
 
     for q, base in enumerate(chips):
 
@@ -565,8 +813,8 @@
             pltpu.VMEM((ctx, parts, piece, ff), BF16),
             pltpu.VMEM((2, width // ctx, ff), BF16),
             dma((3,)),
-            dma((13,)),
-            dma((13,)),
+            dma((GATHER_COPIES,)),
+            dma((GATHER_COPIES,)),
             dma((planes - 1,)),
             dma((planes - 1,)),
             dma((planes - 1,)),
@@ -588,12 +836,11 @@
     cot,
     pg,
     gg,
-    gates,
+    meta,
     attended,
     ffn_in,
     queries,
-    keys,
-    values,
+    kv,
     lse,
     trig,
     wout,
@@ -609,9 +856,9 @@
     ex_out,
     *scratch,
 ):
-    zkeep, gwin, osend, low, attg, mask, delta, dk, dv, dq, kvs, kvr = scratch[:12]
-    load_sem, kv_s, kv_r = scratch[12:15]
-    tok_refs, out_refs, line_refs = scratch[15:21], scratch[21:27], scratch[27:]
+    zkeep, gwin, osend, low, attg, mask, delta, kt, dk, dv, dq, kvs, kvr = scratch[:13]
+    load_sem, kv_s, kv_r = scratch[13:16]
+    tok_refs, out_refs, line_refs = scratch[16:22], scratch[22:28], scratch[28:]
     spot = Spot()
     c, k, z, ctx = spot.c, spot.k, spot.z, spot.ctx
     tok, width = cot.shape
@@ -634,7 +881,7 @@
     gwin_load.wait()
     line.step(1)
 
-    gate = gates[...]
+    gate = jnp.concatenate([meta[g, 1:2, :] for g in range(meta.shape[0])], axis=0)
     seen = gate * gg[...]
     mix = seen - gate * jnp.sum(seen, axis=0, keepdims=True)
     mix = jnp.concatenate([mix, jnp.zeros((HEAD - mix.shape[0], tok), F32)], axis=0)
@@ -677,7 +924,7 @@
         at = lanes(n * step, step)
         attg[:, at] = dot(low[...], wout[:, at]).astype(BF16)
 
-    seq = keys.shape[0]
+    seq = kv.shape[0]
     spans = span.shape[1]
     size = seq // spans
     mine = spans // ctx
@@ -694,15 +941,18 @@
         term = jnp.sum(attg[:, at].astype(F32) * attended[:, at].astype(F32), axis=-1, keepdims=True)
         deltas = jnp.where(lane_h == h, term, deltas)
     delta[...] = deltas.T
+    for g in range(heads_kv):
+        kt[g] = kv[:, g * HEAD : (g + 1) * HEAD].astype(F32).T.astype(BF16)
 
     def head(g, h):
         at = lanes(h * HEAD, HEAD)
-        kv = slice(g * HEAD, (g + 1) * HEAD)
+        k_at = slice(g * HEAD, (g + 1) * HEAD)
+        v_at = slice((heads_kv + g) * HEAD, (heads_kv + g + 1) * HEAD)
         q, a = queries[:, at], attg[:, at]
-        soft = jnp.exp(dot_nt(keys[:, kv], q) + mask[...] - lse[pl.ds(h, 1), :])
-        prob = dot_nt(values[:, kv], a)
+        soft = jnp.exp(dot_nt(kv[:, k_at], q) + mask[...] - lse[pl.ds(h, 1), :])
+        prob = dot_nt(kv[:, v_at], a)
         score = (soft * (prob - delta[pl.ds(h, 1), :])).astype(BF16)
-        dq[:, at] = dot_tn(score, keys[:, kv])
+        dq[:, at] = dot(kt[g], score).T
         dk[...] += dot(score, q)
         dv[...] += dot(soft.astype(BF16), a)
 
@@ -783,14 +1033,14 @@
 
 
 def run_attend_back(
-    span, resid, cot, pg, gg, gates, attended, ffn_in, queries, keys, values, lse, trig, wout, router_t, gain, zout, gwin
+    span, resid, cot, pg, gg, meta, attended, ffn_in, queries, kv, lse, trig, wout, router_t, gain, zout, gwin
 ):
     tok, width = cot.shape
     planes = zout.shape[0]
     ctx, parts, piece, wide = gwin.shape
     cols = wide // 2
     block = width // planes
-    seq, kv_cols = keys.shape
+    seq, kv_cols = kv.shape
     vm, anyspace = pl.BlockSpec(memory_space=pltpu.VMEM), pl.BlockSpec(memory_space=pl.ANY)
     sm = pl.BlockSpec(memory_space=pltpu.SMEM)
     shape = jax.ShapeDtypeStruct
@@ -800,12 +1050,12 @@
         out_shape=(
             shape((tok, width), BF16),
             shape((tok, width), F32),
-            shape((tok, width + 2 * kv_cols), BF16),
+            shape((tok, width + kv_cols), BF16),
             shape((block, width), BF16),
             shape((width, HEAD), BF16),
             shape((ctx, piece, cols), BF16),
         ),
-        in_specs=[sm] + [vm] * 15 + [anyspace] * 2,
+        in_specs=[sm] + [vm] * 14 + [anyspace] * 2,
         out_specs=(vm,) * 6,
         scratch_shapes=[
             pltpu.VMEM((4, tok, width), BF16),
@@ -815,6 +1065,7 @@
             pltpu.VMEM((tok, width), BF16),
             pltpu.VMEM((seq, tok), F32),
             pltpu.VMEM((HEAD, tok), F32),
+            pltpu.VMEM((KV_HEADS, HEAD, seq), BF16),
             pltpu.VMEM((seq, HEAD), F32),
             pltpu.VMEM((seq, HEAD), F32),
             pltpu.VMEM((tok, width), F32),
@@ -832,7 +1083,7 @@
         ),
         cost_estimate=pl.CostEstimate(flops=8 * 10**9, bytes_accessed=40 * 10**6, transcendentals=10**6),
     )(
-        span, resid, cot, pg, gg, gates, attended, ffn_in, queries, keys, values, lse, trig, wout, router_t, gain, zout, gwin
+        span, resid, cot, pg, gg, meta, attended, ffn_in, queries, kv, lse, trig, wout, router_t, gain, zout, gwin
     )
 
 
@@ -996,110 +1247,48 @@
     down_weight,
     cotangent,
 ):
-    tok_rows = hidden_in.shape[1]
-    width = hidden_in.shape[2]
-    contexts = lax.axis_size("context")
-    span_len = tok_rows // 2
-    seq_len = tok_rows * contexts
-    group = HEADS // KV_HEADS
-    q_cols = HEADS * HEAD
-    kv_cols = KV_HEADS * HEAD
-    scale = HEAD ** (-0.5)
-    local_experts = in_weight.shape[0]
-    n_experts = local_experts * lax.axis_size("expert")
+    _, tok_rows, width = hidden_in.shape
+    ctx, parts = lax.axis_size("context"), lax.axis_size("dp")
+    planes = ctx * lax.axis_size("expert")
+    n_experts = router.shape[1]
     top_k = expert_ids.shape[2]
     capacity = (9 * tok_rows * top_k + 8 * n_experts - 1) // (8 * n_experts)
-    ff_width = down_weight.shape[2]
-    seq_spans = span_order[0]
-    stored = jnp.arange(seq_len) // span_len
-    all_pos = (seq_spans[stored] * span_len + jnp.arange(seq_len) % span_len).astype(jnp.float32)
-    my_pos = lax.dynamic_slice_in_dim(all_pos, lax.axis_index("context") * tok_rows, tok_rows)
-    cosine, sine = rope_tables(my_pos, HEAD)
-    inputs = hidden_in[0].astype(jnp.float32)
-    inv_one = lax.rsqrt(jnp.mean(inputs * inputs, axis=-1, keepdims=True) + NORM_EPS)
-    plain_one = inputs * inv_one
-    normed = (plain_one * gain_attn).astype(jnp.bfloat16)
-    mixed = jnp.dot(normed, qkv_weight, preferred_element_type=jnp.float32)
-    queries = (
-        rotate(mixed[:, :q_cols].reshape(tok_rows, HEADS, HEAD), cosine, sine) * scale
-    ).astype(jnp.bfloat16)
-    keys = rotate(
-        mixed[:, q_cols : q_cols + kv_cols].reshape(tok_rows, KV_HEADS, HEAD), cosine, sine
-    ).astype(jnp.bfloat16)
-    values = mixed[:, q_cols + kv_cols :].reshape(tok_rows, KV_HEADS, HEAD).astype(jnp.bfloat16)
-    grouped = queries.reshape(tok_rows, KV_HEADS, group, HEAD)
-
-    def key_scores(key_piece):
-        scores = jnp.einsum(
-            "qkgd,skd->kgqs", grouped, key_piece, preferred_element_type=jnp.float32
-        )
-        visible = all_pos[None, None, None, :] <= my_pos[None, None, :, None]
-        return (jnp.where(visible, scores, MASKED), visible)
-
-    running = jnp.full((KV_HEADS, group, tok_rows), MASKED, jnp.float32)
-    key_piece = lax.all_gather(keys, "context", axis=0, tiled=True)
-    value_piece = lax.all_gather(values, "context", axis=0, tiled=True)
-    scores, visible = key_scores(key_piece)
-    newest = jnp.maximum(running, jnp.max(scores, axis=-1))
-    weights = jnp.where(visible, jnp.exp(scores - newest[..., None]), 0.0)
-    totals = jnp.sum(weights, axis=-1)
-    accum = jnp.einsum(
-        "kgqs,skd->kgqd",
-        weights.astype(jnp.bfloat16),
-        value_piece,
-        preferred_element_type=jnp.float32,
-    )
-    running, totals, accum = (newest, totals, accum)
-    log_total = running + jnp.log(totals)
-    attended = (
-        (accum / totals[..., None])
-        .transpose(2, 0, 1, 3)
-        .reshape(tok_rows, q_cols)
-        .astype(jnp.bfloat16)
-    )
-    resid = inputs + jnp.einsum(
-        "rh,dh->rd", attended, out_weight, preferred_element_type=jnp.float32
-    )
-    inv_two = lax.rsqrt(jnp.mean(resid * resid, axis=-1, keepdims=True) + NORM_EPS)
-    plain_two = resid * inv_two
-    ffn_in = (plain_two * gain_ffn).astype(jnp.bfloat16)
-    logits = jnp.dot(ffn_in, router, preferred_element_type=jnp.float32)
-    token_ids = expert_ids[0]
-    matches = token_ids[:, :, None] == jnp.arange(n_experts)[None, None, :]
-    chosen = jnp.any(matches, axis=1)
-    gates = softmax_last(jnp.where(chosen, logits, MASKED))
-    turn = jnp.sum(jnp.where(matches, priority[0][:, :, None], 0), axis=1)
-    turn = jnp.where(chosen, turn, tok_rows * top_k)
-    ranks = jnp.sum((turn[:, None, :] < turn[None, :, :]).astype(jnp.int32), axis=0)
-    slots = jnp.where(chosen & (ranks < capacity), ranks, -1).astype(jnp.float32)
-    gates_t = gates.T
-    meta = jnp.stack([slots.T, gates_t], axis=1)
-    meta = jnp.pad(meta, ((0, 0), (0, 6), (0, 0)))
-    cot_low = cotangent[0]
-    cot_all = lax.all_gather(cot_low, ("expert", "context"), axis=0)
-    parts = lax.axis_size("dp")
-    zout, pair_sum, gate_grad_t, gwin, down = run_ffn(
+    ff = down_weight.shape[2]
+    half_freqs = ROPE_BASE ** (jnp.arange(HEAD // 2).astype(jnp.float32) * (-2.0 / HEAD))
+    freqs = jnp.concatenate([half_freqs, half_freqs])[None]
+    router_t = jnp.pad(router.T, ((0, 16 - n_experts), (0, 0)))
+    hidden, cot = hidden_in[0], cotangent[0]
+    normed, queries, kv, lse, attended, resid, ffn_in, trig, meta, cot_all = run_front(
+        capacity,
+        span_order,
+        hidden,
+        cot,
+        gain_attn[None],
+        freqs,
+        gain_ffn[None],
+        router_t,
+        expert_ids[0].T,
+        priority[0].T,
+        qkv_weight,
+        out_weight,
+        ctx,
+        planes,
+    )
+    zout, pair_sum, gate_grad, gwin, down = run_ffn(
         capacity, ffn_in, cot_all, meta, in_weight, down_weight, parts
     )
-    gwin = gwin.reshape(contexts, parts, width // (contexts * parts), 2 * ff_width)
-    lse = jnp.pad(log_total.reshape(HEADS, tok_rows), ((0, 16 - HEADS), (0, 0)))
-    cosine, sine = cosine[:, 0, :], sine[:, 0, :]
-    trig = jnp.stack(
-        [jnp.concatenate([cosine, cosine], axis=1), jnp.concatenate([-sine, sine], axis=1)]
-    )
-    router_t = jnp.pad(router.T, ((0, 16 - n_experts), (0, 0)))
+    gwin = gwin.reshape(ctx, parts, width // (ctx * parts), 2 * ff)
     output, resid_grad, mixed_grad, out_red, small, in_one = run_attend_back(
         span_order,
         resid,
-        cot_low,
+        cot,
         pair_sum,
-        gate_grad_t,
-        gates_t,
+        gate_grad,
+        meta,
         attended,
         ffn_in,
-        queries.reshape(tok_rows, q_cols),
-        key_piece.reshape(seq_len, kv_cols),
-        value_piece.reshape(seq_len, kv_cols),
+        queries,
+        kv,
         lse,
         trig,
         out_weight,
@@ -1109,15 +1298,16 @@
         gwin,
     )
     input_grad, qkv_sum, proj_sum, in_two = run_last(
-        normed, mixed_grad, hidden_in[0], resid_grad, qkv_weight, gain_attn[None], small, out_red, gwin
-    )
+        normed, mixed_grad, hidden, resid_grad, qkv_weight, gain_attn[None], small, out_red, gwin
+    )
+    wide = qkv_weight.shape[1]
     qkv_sum = qkv_sum.astype(jnp.float32)
-    smalls = qkv_sum[:, q_cols + 2 * kv_cols :]
+    smalls = qkv_sum[:, wide:]
     return (
         output[None],
         input_grad[None],
         smalls[:, HEAD - 1],
-        qkv_sum[:, : q_cols + 2 * kv_cols],
+        qkv_sum[:, :wide],
         proj_sum.astype(jnp.float32),
         smalls[:, n_experts],
         smalls[:, :n_experts],

time: 365 us -> 327 us (0.90)
  Pallas kernels: 261 us -> 305 us
  blocking collectives: 19.8 us -> 0 us
  matrix products: 18.5 us -> 0 us
  other arithmetic: 20.7 us -> 5.99 us
  local copies, waits for them, and re-layouts: 23.8 us -> 9.62 us
  between operations: 14.8 us -> 0.94 us
    pallas_call x0 -> x1, Pallas kernels: none -> 44.1 us  [run_front(): pl.pallas_call(functools.partial(front_kernel, cap), out_shape=(shape((to...]
    all_gather x2 -> x0, blocking collectives: 19.8 us -> none  [the longest x1 11.1 us: local(): key_piece = lax.all_gather(keys, 'context', axis=0, tiled=True)]
    dot_general x5 -> x0, matrix products: 18.5 us -> none  [the longest x1 7.45 us: local(): jnp.einsum('kgqs,skd->kgqd', weights.astype(jnp.bfloat16), value_piece, p...]
    gather x2 -> x0, other arithmetic: 4.57 us -> none  [local(): seq_spans[stored] * span_len + jnp.arange(seq_len) % span_len]
    reduce_sum x5 -> x0, other arithmetic: 4.27 us -> none  [the longest x1 2.53 us: local(): totals = jnp.sum(weights, axis=-1)]
  transfers between devices with their start and end apart: 1 -> 0, of which waited for: 0 -> 0; matrix products, arithmetic and copies ran while one was open for 14% -> 0% of each run, Pallas kernels for 0% -> 0%
where the time goes in v3:
time: 327 us; the launch traced here: 321 us
  Pallas kernels  305 us (93%)
  local copies, waits for them, and re-layouts  9.62 us (3%)
  other arithmetic  5.99 us (2%)
    pallas_call x1, Pallas kernels, run_ffn(): pl.pallas_call(functools.partial(ffn_kernel, cap), out_shape=(shape((plan...  108 us
    pallas_call x1, Pallas kernels, run_attend_back(): pl.pallas_call(attend_back_kernel, out_shape=(shape((tok, width), BF16),...  76.7 us
    pallas_call x1, Pallas kernels, run_last(): pl.pallas_call(last_kernel, out_shape=(shape((tok, width), BF16), shape((...  75.9 us
    pallas_call x1, Pallas kernels, run_front(): pl.pallas_call(functools.partial(front_kernel, cap), out_shape=(shape((to...  44.1 us

profile of v3, /device:TPU:0, one launch (start us, length us, event | category | flops | bytes accessed | tf_op | source)
XLA Modules:
  0.0 321.4 jit_solution(3256234499058526947)
XLA Ops:
  0.7 0.6 maximum_bitcast_fusion.freqs
  1.2 1.3 broadcast_in_dim.17.gain_one.gain
  2.5 1.3 broadcast_in_dim.19.gain_two.gain
  3.8 1.4 pad.4.router_t
  5.2 44.1 %shard_map.187 = (bf16[256,1536]{1,0:T(8,128)(2,1)}, bf16[256,1536]{1,0:T(8,128)(2,1)}, bf16[1024,512]{1,0:T(8,128)(2,1)}, f32[16,256]{1,0:T(8,128)}, bf16[256,1...) custom-call(s32[1,8]{1,0:T(1,128)} %span.3, ...), custom_call_target="tpu_custom_call" | custom-call | flops 5000000000 | bytes 20000000 | tf_op jit(solution)/shard_map/pallas_call | solution.py:573
  49.3 108.2 %shard_map.188 = (bf16[8,256,1536]{2,1,0:T(8,128)(2,1)}, f32[256,1536]{1,0:T(8,128)}, f32[8,256]{1,0:T(8,128)}, bf16[1536,1536]{1,0:T(8,128)(2,1)}, bf16[4,96,768]{2,1,0:T(8,128)(2,1)}) custom-call(bf16[256,1536]{1,0:T(8,128)(2,1)} %get-tuple-element.35.ffn.ffn_in, bf16[8,256,1536]{2,1,0:T(8,128)(2,1)} %get-tuple-element.36.cot_h, ...), custom_call_target="tpu_custom_call" | custom-call | flops 24999999488 | bytes 50000000 | tf_op jit(solution)/shard_map/pallas_call | solution.py:788
  157.5 76.7 %shard_map.189 = (bf16[256,1536]{1,0:T(8,128)(2,1)}, f32[256,1536]{1,0:T(8,128)}, bf16[256,2048]{1,0:T(8,128)(2,1)}, bf16[192,1536]{1,0:T(8,128)(2,1)}, bf16[153...) custom-call(s32[1,8]{1,0:T(1,128)} %span.3, f32[256,1536]{1,0:T(8,128)} %get-tuple-element.34.resid, ...), custom_call_target="tpu_custom_call" | custom-call | flops 8000000000 | bytes 40000000 | tf_op jit(solution)/shard_map/pallas_call | solution.py:1048
  234.1 75.9 %shard_map.190 = (bf16[256,1536]{1,0:T(8,128)(2,1)}, bf16[48,2176]{1,0:T(8,128)(2,1)}, bf16[48,1536]{1,0:T(8,128)(2,1)}, bf16[4,96,768]{2,1,0:T(8,128)(2,1)}) custom-call(bf16[256,1536]{1,0:T(8,128)(2,1)} %get-tuple-element.48.normed, bf16[256,2048]{1,0:T(8,128)(2,1)} %get-tuple-element.49.mixed_grad, bf16[256,1536]{1,0:T(8,128)(2,1)} %bitcast.17, ...), custom_call_target="tpu_custom_call" | custom-call | flops 4000000000 | bytes 40000000 | tf_op jit(solution)/shard_map/pallas_call | solution.py:1205
  310.1 0.0 copy-start.2
  310.1 0.0 copy-start.3
  310.1 0.0 copy-start.4
  310.1 0.8 slice.23
  311.0 0.7 copy.22
  311.6 1.6 convert_element_type.21
  313.3 1.7 slice.21
  315.0 1.0 convert_element_type.20
  315.9 0.7 slice_reduce_fusion
  316.6 0.0 copy-done.2
  316.6 0.0 copy-start
  316.6 1.1 convert_element_type.23
  317.7 0.0 copy-done.3
  317.7 0.0 copy-done.4
  317.7 0.0 copy-start.1
  317.7 1.7 maximum_convert_fusion
  319.4 0.0 copy-done
  319.4 0.9 copy.25
  320.3 0.0 copy-done.1
  320.3 0.9 copy.26
  (1 shorter events, 0.0 us)
Async XLA Ops:
  310.1 6.5 %copy-start.2 = (bf16[4,96,768]{2,1,0:T(8,128)(2,1)S(1)}, bf16[4,96,768]{2,1,0:T(8,128)(2,1)}, u32[]{:S(2)}) copy-start(bf16[4,96,768]{2,1,0:T(8,128)(2,1)} %get-tuple-element.58) | copy-start | bytes 1769476
  310.1 7.6 %copy-start.3 = (bf16[4,96,768]{2,1,0:T(8,128)(2,1)S(1)}, bf16[4,96,768]{2,1,0:T(8,128)(2,1)}, u32[]{:S(2)}) copy-start(bf16[4,96,768]{2,1,0:T(8,128)(2,1)} %get-tuple-element.56) | copy-start | bytes 1769476
  310.1 7.6 %copy-start.4 = (bf16[4,96,768]{2,1,0:T(8,128)(2,1)S(1)}, bf16[4,96,768]{2,1,0:T(8,128)(2,1)}, u32[]{:S(2)}) copy-start(bf16[4,96,768]{2,1,0:T(8,128)(2,1)} %get-tuple-element.57) | copy-start | bytes 1769476
  316.6 2.8 copy-start
  317.7 2.6 copy-start.1

commit v4 on v3

--- a/solution.py
+++ b/solution.py
@@ -2,6 +2,7 @@
 
 import jax
 import jax.numpy as jnp
+import numpy as np
 from jax import lax
 from jax.experimental import pallas as pl
 from jax.experimental.pallas import tpu as pltpu
@@ -141,7 +142,7 @@
 class Plane:
     def __init__(self, spot, zcr, zk, rx, ry, s, r):
         self.spot, self.zcr, self.zk, self.rx, self.ry, self.s, self.r = spot, zcr, zk, rx, ry, s, r
-        half = zk.shape[1] // 2
+        half = zk[0].shape[0] // 2
         self.lo, self.hi = pl.ds(0, half), pl.ds(half, half)
         self.sent = []
 
@@ -154,39 +155,49 @@
         remote(dst, dst, self.s.at[i], self.r.at[i], self.spot.kp).wait_recv()
 
     def give(self, q, src):
-        self.push(src, self.zcr.at[q], q, self.spot.kp)
-
-    def fold(self, q, own):
-        self.arrive(self.zcr.at[q], q)
-        self.zk[q] = plus(own, self.zcr[q])
+        self.push(src, self.zcr[q], q, self.spot.kp)
+
+    def fold(self, q, own=None):
+        self.arrive(self.zcr[q], q)
+        self.zk[q][...] = plus(self.zk[q][...] if own is None else own, self.zcr[q][...])
 
     def near(self):
-        self.push(self.zk.at[1, self.lo], self.rx.at[1], 5, self.spot.xp)
-        self.push(self.zk.at[2, self.hi], self.ry.at[1], 8, self.spot.yp)
+        self.push(self.zk[1].at[self.lo], self.rx[1], 5, self.spot.xp)
+        self.push(self.zk[2].at[self.hi], self.ry[1], 8, self.spot.yp)
 
     def across(self):
-        self.push(self.zk.at[3, self.lo], self.rx.at[0], 4, self.spot.xp)
-        self.push(self.zk.at[3, self.hi], self.ry.at[0], 7, self.spot.yp)
+        self.push(self.zk[3].at[self.lo], self.rx[0], 4, self.spot.xp)
+        self.push(self.zk[3].at[self.hi], self.ry[0], 7, self.spot.yp)
 
     def turn(self):
         lo, hi = self.lo, self.hi
-        self.arrive(self.rx.at[0], 4)
-        self.zk[2, lo] = plus(self.zk[2, lo], self.rx[0])
-        self.push(self.zk.at[2, lo], self.ry.at[2], 9, self.spot.yp)
-        self.arrive(self.ry.at[0], 7)
-        self.zk[1, hi] = plus(self.zk[1, hi], self.ry[0])
-        self.push(self.zk.at[1, hi], self.rx.at[2], 6, self.spot.xp)
+        self.arrive(self.rx[0], 4)
+        self.zk[2][lo] = plus(self.zk[2][lo], self.rx[0][...])
+        self.push(self.zk[2].at[lo], self.ry[2], 9, self.spot.yp)
+        self.arrive(self.ry[0], 7)
+        self.zk[1][hi] = plus(self.zk[1][hi], self.ry[0][...])
+        self.push(self.zk[1].at[hi], self.rx[2], 6, self.spot.xp)
 
     def total(self):
-        self.arrive(self.rx.at[1], 5)
-        self.arrive(self.ry.at[1], 8)
-        self.arrive(self.rx.at[2], 6)
-        self.arrive(self.ry.at[2], 9)
-        return ((self.lo, self.rx.at[1], self.ry.at[2]), (self.hi, self.rx.at[2], self.ry.at[1]))
+        self.arrive(self.rx[1], 5)
+        self.arrive(self.ry[1], 8)
+        self.arrive(self.rx[2], 6)
+        self.arrive(self.ry[2], 9)
+        return (
+            (self.lo, (self.zk[0][self.lo], self.rx[1][...], self.ry[2][...])),
+            (self.hi, (self.zk[0][self.hi], self.rx[2][...], self.ry[1][...])),
+        )
 
     def done(self):
         for copy in self.sent:
             copy.wait_send()
+
+
+def plane_of(spot, zcr, zk, rx, ry, s, r):
+    four, three = range(4), range(3)
+    return Plane(
+        spot, [zcr.at[q] for q in four], [zk.at[q] for q in four], [rx.at[i] for i in three], [ry.at[i] for i in three], s, r
+    )
 
 
 def plane_scratch(block, wide):
@@ -198,6 +209,13 @@
         pltpu.SemaphoreType.DMA((10,)),
         pltpu.SemaphoreType.DMA((10,)),
     ]
+
+
+def summed(terms):
+    total = terms[0].astype(F32)
+    for term in terms[1:]:
+        total = total + term.astype(F32)
+    return total
 
 
 class Line:
@@ -343,10 +361,13 @@
     def start(self):
         me, own, lo, hi = self.spot.me, self.own, self.lo, self.hi
         self.push(own.at[lo], self.buf.at[me, lo], 0, self.spot.xp)
-        self.push(own.at[hi], self.buf.at[me, hi], 3, self.spot.yp)
         self.push(own.at[lo], self.buf.at[me, lo], 6, self.spot.kp)
         self.push(own.at[hi], self.buf.at[me, hi], 13, self.spot.kp)
         self.push(own.at[hi], self.buf.at[me, hi], 1, self.spot.xp)
+
+    def start_y(self):
+        me, own, lo, hi = self.spot.me, self.own, self.lo, self.hi
+        self.push(own.at[hi], self.buf.at[me, hi], 3, self.spot.yp)
         self.push(own.at[lo], self.buf.at[me, lo], 2, self.spot.yp)
 
     def first(self):
@@ -438,6 +459,7 @@
         load.start()
     greet([spot.xp, spot.yp, spot.kp])
     gather = Gather(spot, cot, cot_all, co_s, co_r)
+    gather.start()
 
     x = hidden[...].astype(F32)
     inv = lax.rsqrt(jnp.mean(x * x, axis=-1, keepdims=True) + NORM_EPS)
@@ -473,7 +495,7 @@
     sent = [kv_copy(own, 1, spot.yp), kv_copy(own, 0, spot.kp)]
     for copy in sent:
         copy.start()
-    gather.start()
+    gather.start_y()
 
     loads[1].wait()
     step = 256
@@ -604,10 +626,10 @@
     )(span, hidden, cot, gain_one, freqs, gain_two, router_t, ids_t, turn_t, wqkv, wout)
 
 
-def ffn_kernel(cap, ffn, cot_h, meta, win_h, wdn_h, zout_h, pg_out, gg_out, gwin_h, ex_out, *scratch):
+def ffn_kernel(cap, ffn, resid, cot_h, meta, win_h, wdn_h, output, pg_out, gg_out, gwin_h, ex_out, *scratch):
     agb, metas, cotb, win, wdn, xs, ds, hid, igs, pgs, ggs, ggr, stage, gwdn, pgt = scratch[:15]
-    load_sem, ag_s, ag_r, me_s, me_r, gg_s, gg_r, st_sem = scratch[15:23]
-    plane_refs, line_refs = scratch[23:29], scratch[29:]
+    load_sem, ag_s, ag_r, me_s, me_r, gg_s, gg_r, out_s, out_r = scratch[15:24]
+    plane_refs, line_refs = scratch[24:30], scratch[30:]
     spot = Spot()
     c, k, me = spot.c, spot.k, spot.me
     kp = spot.kp
@@ -625,12 +647,23 @@
         load.start()
     others = spot.others()
     greet([dev for _, dev in others], spot.along())
-    plane = Plane(spot, *plane_refs)
+    plane = plane_of(spot, *plane_refs)
+    lo, hi = plane.lo, plane.hi
+    outs = Plane(
+        spot,
+        [agb.at[q] for q in range(4)],
+        [cotb.at[base + k] for base in chips],
+        [agb.at[4, lo], agb.at[4, hi], agb.at[5, lo]],
+        [agb.at[6, lo], agb.at[6, hi], agb.at[5, hi]],
+        out_s,
+        out_r,
+    )
     line = ExpertLine(spot, gwdn, 0, ff, *line_refs)
     gather = Gather(spot, ffn, agb, ag_s, ag_r)
     for step, (other, dev) in enumerate(others):
         remote(meta.at[other], metas.at[me], me_s.at[step], me_r.at[step], dev).start()
     gather.start()
+    gather.start_y()
     agb[me] = ffn[...]
     metas[me] = meta[me]
     slot_rows = lax.broadcasted_iota(jnp.int32, (cap, tok), 0).astype(F32)
@@ -675,10 +708,7 @@
         zcs = stage.at[q]
         zcs[...] = dot_tn(spots(base + 1 - k).astype(BF16), pgs[theirs, :]).astype(BF16)
         plane.give(q, zcs)
-        plane.zk[q] = dot_tn(spots(base + k).astype(BF16), pgs[mine, :]).astype(BF16)
-
-    def fold(q):
-        plane.fold(q, plane.zk[q])
+        plane.zk[q][...] = dot_tn(spots(base + k).astype(BF16), pgs[mine, :]).astype(BF16)
 
     for load in loads:
         load.wait()
@@ -694,12 +724,13 @@
     gather.third()
     gather.other_core(2)
     group(2)
-    fold(1)
-    fold(2)
+    plane.fold(1)
+    plane.fold(2)
     plane.near()
     gather.other_core(3)
+    gather.done()
     group(3)
-    fold(3)
+    plane.fold(3)
     plane.across()
 
     tall = width // ctx
@@ -711,12 +742,11 @@
             gwdn[n, d] = tile[d * gwdn.shape[2] : (d + 1) * gwdn.shape[2]]
 
     line.step(1)
-    fold(0)
+    plane.fold(0)
     plane.turn()
 
-    gather.done()
-
-    for q, base in enumerate(chips):
+    for q in (1, 2, 3, 0):
+        base = chips[q]
 
         @pl.loop(0, width // step)
         def _(n):
@@ -725,17 +755,22 @@
 
         for kk in range(2):
             p = base + kk
-            i = q * 2 + kk
             hot = spots(p)
             rows = pgs[pl.ds(kk * cap, cap), :]
             ggs[p, 0:1, :] = jnp.sum(hot * dot_nt(rows, cotb[p]), axis=0, keepdims=True)
             scaled = (rows.astype(F32) * gate_of(p, hot)).astype(BF16)
-            agb[p] = dot_tn(hot.astype(BF16), scaled).astype(BF16)
-            pltpu.make_async_copy(agb.at[p], zout_h.at[p], st_sem.at[i]).start()
+            cotb[p] = dot_tn(hot.astype(BF16), scaled).astype(BF16)
+        outs.give(q, cotb.at[base + 1 - k])
     ggr[me] = ggs[me]
     for n, (other, dev) in enumerate(others):
         remote(ggs.at[other], ggr.at[me], gg_s.at[n], gg_r.at[n], dev).start()
     line.step(2)
+    outs.fold(1)
+    outs.fold(2)
+    outs.near()
+    outs.fold(3)
+    outs.across()
+    outs.fold(0)
     half_wide = ff
 
     @pl.loop(0, 2 * ctx)
@@ -755,27 +790,27 @@
 
     for slot in range(2):
         pltpu.make_async_copy(pgt.at[slot], gwin_h.at[pl.ds(0, tall), pl.ds(0, half_wide)], load_sem.at[slot]).wait()
+    outs.turn()
     line.step(3)
-    for rows, first, second in plane.total():
-        pg_out[rows, :] = (
-            plane.zk[0, rows].astype(F32) + first[...].astype(F32) + second[...].astype(F32)
-        )
+    for rows, terms in plane.total():
+        pg_out[rows, :] = summed(terms)
     for n in range(planes - 1):
         source = lax.rem(me + planes - 1 - n, planes)
         remote(ggr.at[source], ggr.at[source], gg_s.at[n], gg_r.at[n], kp).wait_recv()
     for p in range(planes):
         gg_out[p : p + 1, :] = ggr[p, 0:1, :]
     line.final()
-    for i in range(planes):
-        pltpu.make_async_copy(agb.at[0], zout_h.at[0], st_sem.at[i]).wait()
+    for rows, terms in outs.total():
+        output[rows, :] = (resid[rows, :] + summed(terms)).astype(BF16)
     for n, (other, dev) in enumerate(others):
         remote(meta.at[other], metas.at[other], me_s.at[n], me_r.at[n], dev).wait_send()
         remote(ggs.at[other], ggr.at[other], gg_s.at[n], gg_r.at[n], dev).wait_send()
     plane.done()
+    outs.done()
     line.done(ex_out)
 
 
-def run_ffn(cap, ffn, cot_all, meta, win, wdn, parts):
+def run_ffn(cap, ffn, resid, cot_all, meta, win, wdn, parts):
     tok, width = ffn.shape
     ff = wdn.shape[2]
     planes = cot_all.shape[0]
@@ -788,14 +823,14 @@
     return pl.pallas_call(
         functools.partial(ffn_kernel, cap),
         out_shape=(
-            shape((planes, tok, width), BF16),
+            shape((tok, width), BF16),
             shape((tok, width), F32),
             shape((planes, tok), F32),
             shape((width, 2 * ff), BF16),
             shape((ctx, piece, ff), BF16),
         ),
-        in_specs=[vm, anyspace, vm, anyspace, anyspace],
-        out_specs=(anyspace, vm, vm, anyspace, vm),
+        in_specs=[vm, vm, anyspace, vm, anyspace, anyspace],
+        out_specs=(vm, vm, vm, anyspace, vm),
         scratch_shapes=[
             pltpu.VMEM((planes, tok, width), BF16),
             pltpu.VMEM((planes, 8, tok), F32),
@@ -819,7 +854,8 @@
             dma((planes - 1,)),
             dma((planes - 1,)),
             dma((planes - 1,)),
-            dma((planes,)),
+            dma((10,)),
+            dma((10,)),
         ]
         + plane_scratch(tok, width)
         + expert_scratch(ctx, parts, piece, ff),
@@ -827,7 +863,7 @@
             collective_id=1, has_side_effects=True, vmem_limit_bytes=62 * 2**20
         ),
         cost_estimate=pl.CostEstimate(flops=25 * 10**9, bytes_accessed=50 * 10**6, transcendentals=10**6),
-    )(ffn, cot_all, meta, win, wdn)
+    )(ffn, resid, cot_all, meta, win, wdn)
 
 
 def attend_back_kernel(
@@ -846,9 +882,7 @@
     wout,
     router_t,
     gain,
-    zout_h,
     gwin_h,
-    output,
     resid_grad,
     mixed_grad,
     out_red,
@@ -856,9 +890,9 @@
     ex_out,
     *scratch,
 ):
-    zkeep, gwin, osend, low, attg, mask, delta, kt, dk, dv, dq, kvs, kvr = scratch[:13]
-    load_sem, kv_s, kv_r = scratch[13:16]
-    tok_refs, out_refs, line_refs = scratch[16:22], scratch[22:28], scratch[28:]
+    gwin, osend, low, attg, mask, delta, kt, dk, dv, dq, kvs, kvr = scratch[:12]
+    load_sem, kv_s, kv_r = scratch[12:15]
+    out_refs, line_refs = scratch[15:21], scratch[21:]
     spot = Spot()
     c, k, z, ctx = spot.c, spot.k, spot.z, spot.ctx
     tok, width = cot.shape
@@ -869,15 +903,9 @@
     half_head = HEAD // 2
     gwin_load = pltpu.make_async_copy(gwin_h.at[:, :, :, pl.ds(0, cols)], gwin, load_sem.at[0])
     gwin_load.start()
-    keeps = []
-    for q, base in enumerate(spot.chips):
-        keeps.append(pltpu.make_async_copy(zout_h.at[base + k], zkeep.at[q], load_sem.at[1 + q]))
-        keeps[-1].start()
     greet([spot.xp, spot.yp, spot.kp, spot.yk], spot.along())
-    tokens, weights = Plane(spot, *tok_refs), Plane(spot, *out_refs)
+    weights = plane_of(spot, *out_refs)
     line = ExpertLine(spot, gwin, 0, cols, *line_refs)
-    for q, base in enumerate(spot.chips):
-        tokens.give(q, zout_h.at[base + 1 - k])
     gwin_load.wait()
     line.step(1)
 
@@ -902,16 +930,6 @@
     routed = dot_tn(ffn_in[...], logit_t.T)
     small[...] = jnp.where(lane == gate.shape[0], gain_col, routed).astype(BF16)
 
-    for q in (1, 2):
-        keeps[q].wait()
-        tokens.fold(q, zkeep[q])
-    tokens.near()
-    keeps[3].wait()
-    tokens.fold(3, zkeep[3])
-    tokens.across()
-    keeps[0].wait()
-    tokens.fold(0, zkeep[0])
-
     for q in (1, 2, 3, 0):
         at = lanes(spot.chips[q] * block, 2 * block)
         osend[q] = dot_tn(low[:, at], attended[...]).astype(BF16)
@@ -989,18 +1007,13 @@
     line.step(2)
     heads(0, 4, 2)
     send_kv(0)
-    tokens.turn()
+    weights.turn()
     clear()
     heads(1, 6, 2)
     line.step(3)
     heads(1, 8, 2)
     heads(1, 10, 2)
     send_kv(1)
-    weights.turn()
-    for rows, first, second in tokens.total():
-        out_sum = tokens.zk[0, rows].astype(F32) + first[...].astype(F32) + second[...].astype(F32)
-        output[rows, :] = (resid[rows, :] + out_sum).astype(BF16)
-
     cosine, sine = trig[0], trig[1]
 
     def unrotate(w):
@@ -1010,8 +1023,8 @@
         at = slice(h * HEAD, (h + 1) * HEAD)
         mixed_grad[:, at] = (unrotate(dq[:, at]) * HEAD**-0.5).astype(BF16)
     line.final()
-    for rows, first, second in weights.total():
-        out_red[rows, :] = plus(weights.zk[0, rows], first[...], second[...])
+    for rows, terms in weights.total():
+        out_red[rows, :] = summed(terms).astype(BF16)
     for g in range(heads_kv):
         own = kvs[g, c].astype(F32)
         for n in range(1, ctx):
@@ -1027,17 +1040,16 @@
         for n in range(1, ctx):
             cc = lax.rem(c + n, ctx)
             remote(kvs.at[g, cc], kvr.at[g, cc], kv_s.at[g, n - 1], kv_r.at[g, n - 1], spot.kp).wait_send()
-    tokens.done()
     weights.done()
     line.done(ex_out)
 
 
 def run_attend_back(
-    span, resid, cot, pg, gg, meta, attended, ffn_in, queries, kv, lse, trig, wout, router_t, gain, zout, gwin
+    span, resid, cot, pg, gg, meta, attended, ffn_in, queries, kv, lse, trig, wout, router_t, gain, gwin
 ):
     tok, width = cot.shape
-    planes = zout.shape[0]
     ctx, parts, piece, wide = gwin.shape
+    planes = meta.shape[0]
     cols = wide // 2
     block = width // planes
     seq, kv_cols = kv.shape
@@ -1048,17 +1060,15 @@
     return pl.pallas_call(
         attend_back_kernel,
         out_shape=(
-            shape((tok, width), BF16),
             shape((tok, width), F32),
             shape((tok, width + kv_cols), BF16),
             shape((block, width), BF16),
             shape((width, HEAD), BF16),
             shape((ctx, piece, cols), BF16),
         ),
-        in_specs=[sm] + [vm] * 14 + [anyspace] * 2,
-        out_specs=(vm,) * 6,
+        in_specs=[sm] + [vm] * 14 + [anyspace],
+        out_specs=(vm,) * 5,
         scratch_shapes=[
-            pltpu.VMEM((4, tok, width), BF16),
             pltpu.VMEM((ctx, parts, piece, cols), BF16),
             pltpu.VMEM((4, 2 * block, width), BF16),
             pltpu.VMEM((tok, width), BF16),
@@ -1071,11 +1081,10 @@
             pltpu.VMEM((tok, width), F32),
             pltpu.VMEM((KV_HEADS, ctx, tok, 2 * HEAD), BF16),
             pltpu.VMEM((KV_HEADS, ctx, tok, 2 * HEAD), BF16),
-            dma((5,)),
+            dma((1,)),
             dma((KV_HEADS, ctx - 1)),
             dma((KV_HEADS, ctx - 1)),
         ]
-        + plane_scratch(tok, width)
         + plane_scratch(block, width)
         + expert_scratch(ctx, parts, piece, cols),
         compiler_params=pltpu.CompilerParams(
@@ -1083,7 +1092,7 @@
         ),
         cost_estimate=pl.CostEstimate(flops=8 * 10**9, bytes_accessed=40 * 10**6, transcendentals=10**6),
     )(
-        span, resid, cot, pg, gg, meta, attended, ffn_in, queries, kv, lse, trig, wout, router_t, gain, zout, gwin
+        span, resid, cot, pg, gg, meta, attended, ffn_in, queries, kv, lse, trig, wout, router_t, gain, gwin
     )
 
 
@@ -1108,7 +1117,7 @@
     load = pltpu.make_async_copy(gwin_h.at[:, :, :, pl.ds(cols, cols)], gwin, load_sem.at[0])
     load.start()
     greet([spot.xp, spot.yp, spot.kp, spot.yk], spot.along())
-    first, second = Plane(spot, *a_refs), Plane(spot, *b_refs)
+    first, second = plane_of(spot, *a_refs), plane_of(spot, *b_refs)
     line = ExpertLine(spot, gwin, 0, cols, *line_refs)
 
     def shared_line(ref, refs):
@@ -1173,13 +1182,13 @@
     second.fold(0, bsend[0, mine])
     line.step(2)
     proj.step(2)
-    for rows, one, two in first.total():
-        total[rows, :width] = plus(first.zk[0, rows], one[...], two[...])
+    for rows, terms in first.total():
+        total[rows, :width] = summed(terms).astype(BF16)
     second.turn()
     line.step(3)
     proj.step(3)
-    for rows, one, two in second.total():
-        total[rows, width:] = plus(second.zk[0, rows], one[...], two[...])
+    for rows, terms in second.total():
+        total[rows, width:] = summed(terms).astype(BF16)
     qkv.step(1)
     proj.final(lambda *came: put_shared(proj_out, out_red, came))
     line.final()
@@ -1233,6 +1242,51 @@
     )(normed, mixed_grad, hidden, resid_grad, wqkv, gain, small, out_red, gwin)
 
 
+def finish_kernel(
+    n_experts, output_low, input_low, qkv_low, proj_low, one, two, down_low, output, input_grad, gains, qkv, proj, router, inner, down
+):
+    output[...] = output_low[...]
+    input_grad[...] = input_low[...]
+    wide = qkv.shape[1]
+    qkv[...] = qkv_low[:, :wide].astype(F32)
+    proj[...] = proj_low[...].astype(F32)
+    ff = one.shape[2]
+    inner[:, :, :ff] = one[...].astype(F32)
+    inner[:, :, ff:] = two[...].astype(F32)
+    down[...] = down_low[...].astype(F32)
+    small = qkv_low[:, wide:].astype(F32)
+    router[...] = small[:, :n_experts]
+    piece = small.shape[0]
+    same = lax.broadcasted_iota(jnp.int32, (piece, piece), 0) == lax.broadcasted_iota(
+        jnp.int32, (piece, piece), 1
+    )
+    for row, col in ((0, HEAD - 1), (1, n_experts)):
+        gains[row : row + 1, :] = jnp.sum(jnp.where(same, small[:, col : col + 1], 0.0), axis=0, keepdims=True)
+
+
+def run_finish(n_experts, output, input_grad, qkv, proj, one, two, down):
+    piece, width = proj.shape
+    ctx, rows, ff = one.shape
+    shape = jax.ShapeDtypeStruct
+    vm = pl.BlockSpec(memory_space=pltpu.VMEM)
+    return pl.pallas_call(
+        functools.partial(finish_kernel, n_experts),
+        out_shape=(
+            shape(output.shape, BF16),
+            shape(input_grad.shape, BF16),
+            shape((2, piece), F32),
+            shape((piece, qkv.shape[1] - HEAD), F32),
+            shape((piece, width), F32),
+            shape((piece, n_experts), F32),
+            shape((ctx, rows, 2 * ff), F32),
+            shape((ctx, rows, ff), F32),
+        ),
+        in_specs=[vm] * 7,
+        out_specs=(vm,) * 8,
+        compiler_params=pltpu.CompilerParams(vmem_limit_bytes=40 * 2**20),
+    )(output, input_grad, qkv, proj, one, two, down)
+
+
 def local(
     hidden_in,
     span_order,
@@ -1254,18 +1308,18 @@
     top_k = expert_ids.shape[2]
     capacity = (9 * tok_rows * top_k + 8 * n_experts - 1) // (8 * n_experts)
     ff = down_weight.shape[2]
-    half_freqs = ROPE_BASE ** (jnp.arange(HEAD // 2).astype(jnp.float32) * (-2.0 / HEAD))
-    freqs = jnp.concatenate([half_freqs, half_freqs])[None]
-    router_t = jnp.pad(router.T, ((0, 16 - n_experts), (0, 0)))
+    half_freqs = ROPE_BASE ** (np.arange(HEAD // 2) * (-2.0 / HEAD))
+    freqs = np.concatenate([half_freqs, half_freqs])[None].astype(np.float32)
+    router_t = router.T
     hidden, cot = hidden_in[0], cotangent[0]
     normed, queries, kv, lse, attended, resid, ffn_in, trig, meta, cot_all = run_front(
         capacity,
         span_order,
         hidden,
         cot,
-        gain_attn[None],
+        gain_attn,
         freqs,
-        gain_ffn[None],
+        gain_ffn,
         router_t,
         expert_ids[0].T,
         priority[0].T,
@@ -1274,11 +1328,11 @@
         ctx,
         planes,
     )
-    zout, pair_sum, gate_grad, gwin, down = run_ffn(
-        capacity, ffn_in, cot_all, meta, in_weight, down_weight, parts
+    output, pair_sum, gate_grad, gwin, down = run_ffn(
+        capacity, ffn_in, resid, cot_all, meta, in_weight, down_weight, parts
     )
     gwin = gwin.reshape(ctx, parts, width // (ctx * parts), 2 * ff)
-    output, resid_grad, mixed_grad, out_red, small, in_one = run_attend_back(
+    resid_grad, mixed_grad, out_red, small, in_one = run_attend_back(
         span_order,
         resid,
         cot,
@@ -1293,26 +1347,25 @@
         trig,
         out_weight,
         router_t,
-        gain_ffn[None],
-        zout,
+        gain_ffn,
         gwin,
     )
     input_grad, qkv_sum, proj_sum, in_two = run_last(
-        normed, mixed_grad, hidden, resid_grad, qkv_weight, gain_attn[None], small, out_red, gwin
-    )
-    wide = qkv_weight.shape[1]
-    qkv_sum = qkv_sum.astype(jnp.float32)
-    smalls = qkv_sum[:, wide:]
+        normed, mixed_grad, hidden, resid_grad, qkv_weight, gain_attn, small, out_red, gwin
+    )
+    output, input_grad, gains, qkv_grad, proj_grad, router_grad, inner_grad, down_grad = run_finish(
+        n_experts, output, input_grad, qkv_sum, proj_sum, in_one, in_two, down
+    )
     return (
         output[None],
         input_grad[None],
-        smalls[:, HEAD - 1],
-        qkv_sum[:, :wide],
-        proj_sum.astype(jnp.float32),
-        smalls[:, n_experts],
-        smalls[:, :n_experts],
-        jnp.concatenate([in_one, in_two], axis=2).astype(jnp.float32),
-        down.astype(jnp.float32),
+        gains[0],
+        qkv_grad,
+        proj_grad,
+        gains[1],
+        router_grad,
+        inner_grad,
+        down_grad,
     )
 
 

time: 327 us -> 308 us (0.942)
  Pallas kernels: 305 us -> 296 us
  other arithmetic: 5.99 us -> 0 us
  local copies, waits for them, and re-layouts: 9.62 us -> 5.22 us
    pallas_call x2 -> x3, Pallas kernels: 185 us -> 178 us  [the longest x1 114 us: run_ffn(): pl.pallas_call(functools.partial(ffn_kernel, cap), out_shape=(shape((tok,...]
    convert_element_type x4 -> x0, other arithmetic: 5.4 us -> none  [the longest x1 1.69 us: local(): jnp.concatenate([in_one, in_two], axis=2).astype(jnp.float32)]
where the time goes in v4:
time: 308 us; the launch traced here: 303 us
  Pallas kernels  296 us (96%)
  local copies, waits for them, and re-layouts  5.22 us (2%)
    pallas_call x1, Pallas kernels, run_ffn(): pl.pallas_call(functools.partial(ffn_kernel, cap), out_shape=(shape((tok,...  114 us
    pallas_call x1, Pallas kernels, run_last(): pl.pallas_call(last_kernel, out_shape=(shape((tok, width), BF16), shape((...  74.6 us
    pallas_call x1, Pallas kernels, run_attend_back(): pl.pallas_call(attend_back_kernel, out_shape=(shape((tok, width), F32), s...  60.9 us
    pallas_call x1, Pallas kernels, run_front(): pl.pallas_call(functools.partial(front_kernel, cap), out_shape=(shape((to...  44.1 us

profile of v4, /device:TPU:0, one launch (start us, length us, event | category | flops | bytes accessed | tf_op | source)
XLA Modules:
  0.0 302.6 jit_solution(10627681853345348505)
XLA Ops:
  0.6 44.1 %shard_map.196 = (bf16[256,1536]{1,0:T(8,128)(2,1)}, bf16[256,1536]{1,0:T(8,128)(2,1)}, bf16[1024,512]{1,0:T(8,128)(2,1)}, f32[16,256]{1,0:T(8,128)}, bf16[256,1...) custom-call(s32[1,8]{1,0:T(1,128)} %span.3, ...), custom_call_target="tpu_custom_call" | custom-call | flops 5000000000 | bytes 20000000 | tf_op jit(solution)/shard_map/pallas_call | solution.py:595
  44.8 114.1 %shard_map.197 = (bf16[256,1536]{1,0:T(8,128)(2,1)}, f32[256,1536]{1,0:T(8,128)}, f32[8,256]{1,0:T(8,128)}, bf16[1536,1536]{1,0:T(8,128)(2,1)}, bf16[4,96,768]{2,1,0:T(8,128)(2,1)}) custom-call(bf16[256,1536]{1,0:T(8,128)(2,1)} %get-tuple-element.41.ffn.ffn_in, f32[256,1536]{1,0:T(8,128)} %get-tuple-element.42.resid, ...), custom_call_target="tpu_custom_call" | custom-call | flops 24999999488 | bytes 50000000 | tf_op jit(solution)/shard_map/pallas_call | solution.py:823
  158.9 60.9 %shard_map.198 = (f32[256,1536]{1,0:T(8,128)}, bf16[256,2048]{1,0:T(8,128)(2,1)}, bf16[192,1536]{1,0:T(8,128)(2,1)}, bf16[1536,128]{1,0:T(8,128)(2,1)}, bf16[4,96,768]{2,1,0:T(8,128)(2,1)}) custom-call(s32[1,8]{1,0:T(1,128)} %span.3, f32[256,1536]{1,0:T(8,128)} %get-tuple-element.42.resid, bf16[256,1536]{1,0:T(8,128)(2,1)} %bitcast.21, ...), custom_call_target="tpu_custom_call" | custom-call | flops 8000000000 | bytes 40000000 | tf_op jit(solution)/shard_map/pallas_call | solution.py:1060
  219.9 0.0 copy-start
  219.9 0.0 copy-start.2
  219.9 0.0 copy-start.3
  219.9 74.6 %shard_map.199 = (bf16[256,1536]{1,0:T(8,128)(2,1)}, bf16[48,2176]{1,0:T(8,128)(2,1)}, bf16[48,1536]{1,0:T(8,128)(2,1)}, bf16[4,96,768]{2,1,0:T(8,128)(2,1)}) custom-call(bf16[256,1536]{1,0:T(8,128)(2,1)} %get-tuple-element.46.normed, bf16[256,2048]{1,0:T(8,128)(2,1)} %get-tuple-element.55.mixed_grad, bf16[256,1536]{1,0:T(8,128)(2,1)} %bitcast.19, ...), custom_call_target="tpu_custom_call" | custom-call | flops 4000000000 | bytes 40000000 | tf_op jit(solution)/shard_map/pallas_call | solution.py:1214
  294.6 0.0 copy-done
  294.6 0.0 copy-done.2
  294.6 0.0 copy-done.3
  294.6 0.0 copy-start.1
  294.6 1.1 copy-done.1
  295.7 0.0 copy-start.4
  295.7 1.1 copy-done.4
  296.8 0.0 copy-start.5
  296.8 0.9 copy-done.5
  297.7 0.0 copy-start.6
  297.7 0.9 copy-done.6
  298.6 2.6 shard_map.200
  301.2 0.5 slice_bitcast_fusion
  301.7 0.7 copy.22
Async XLA Ops:
  219.9 74.7 %copy-start = (bf16[256,1536]{1,0:T(8,128)(2,1)S(1)}, bf16[256,1536]{1,0:T(8,128)(2,1)}, u32[]{:S(2)}) copy-start(bf16[256,1536]{1,0:T(8,128)(2,1)} %get-tuple-element.45.output_low) | copy-start | bytes 2359300
  219.9 74.7 %copy-start.2 = (bf16[4,96,768]{2,1,0:T(8,128)(2,1)S(1)}, bf16[4,96,768]{2,1,0:T(8,128)(2,1)}, u32[]{:S(2)}) copy-start(bf16[4,96,768]{2,1,0:T(8,128)(2,1)} %get-tuple-element.64.down_low) | copy-start | bytes 1769476
  219.9 74.7 %copy-start.3 = (bf16[4,96,768]{2,1,0:T(8,128)(2,1)S(1)}, bf16[4,96,768]{2,1,0:T(8,128)(2,1)}, u32[]{:S(2)}) copy-start(bf16[4,96,768]{2,1,0:T(8,128)(2,1)} %get-tuple-element.62.one) | copy-start | bytes 1769476
  294.6 1.1 copy-start.1
  295.7 1.1 copy-start.4
  296.8 0.9 copy-start.5
  297.7 0.9 copy-start.6

commit v5 on v4

--- a/solution.py
+++ b/solution.py
@@ -140,11 +140,12 @@
 
 
 class Plane:
-    def __init__(self, spot, zcr, zk, rx, ry, s, r):
+    def __init__(self, spot, zcr, zk, rx, ry, s, r, zcr_there=None):
+        self.zcr_there = zcr_there or zcr
         self.spot, self.zcr, self.zk, self.rx, self.ry, self.s, self.r = spot, zcr, zk, rx, ry, s, r
         half = zk[0].shape[0] // 2
         self.lo, self.hi = pl.ds(0, half), pl.ds(half, half)
-        self.sent = []
+        self.sent, self.gives = [], []
 
     def push(self, src, dst, i, dev):
         copy = remote(src, dst, self.s.at[i], self.r.at[i], dev)
@@ -154,8 +155,14 @@
     def arrive(self, dst, i):
         remote(dst, dst, self.s.at[i], self.r.at[i], self.spot.kp).wait_recv()
 
+    def given(self):
+        for copy in self.gives:
+            copy.wait_send()
+        self.gives = []
+
     def give(self, q, src):
-        self.push(src, self.zcr[q], q, self.spot.kp)
+        self.gives.append(remote(src, self.zcr_there[q], self.s.at[q], self.r.at[q], self.spot.kp))
+        self.gives[-1].start()
 
     def fold(self, q, own=None):
         self.arrive(self.zcr[q], q)
@@ -189,6 +196,7 @@
         )
 
     def done(self):
+        self.given()
         for copy in self.sent:
             copy.wait_send()
 
@@ -627,7 +635,7 @@
 
 
 def ffn_kernel(cap, ffn, resid, cot_h, meta, win_h, wdn_h, output, pg_out, gg_out, gwin_h, ex_out, *scratch):
-    agb, metas, cotb, win, wdn, xs, ds, hid, igs, pgs, ggs, ggr, stage, gwdn, pgt = scratch[:15]
+    agb, metas, cotb, win, wdn, xs, ds, hid, igs, pgs, ggs, ggr, wint, gwdn, pgt = scratch[:15]
     load_sem, ag_s, ag_r, me_s, me_r, gg_s, gg_r, out_s, out_r = scratch[15:24]
     plane_refs, line_refs = scratch[24:30], scratch[30:]
     spot = Spot()
@@ -651,12 +659,13 @@
     lo, hi = plane.lo, plane.hi
     outs = Plane(
         spot,
-        [agb.at[q] for q in range(4)],
+        [agb.at[2 * i + k] for i in range(4)],
         [cotb.at[base + k] for base in chips],
-        [agb.at[4, lo], agb.at[4, hi], agb.at[5, lo]],
-        [agb.at[6, lo], agb.at[6, hi], agb.at[5, hi]],
+        [agb.at[1 - k, lo], agb.at[1 - k, hi], agb.at[3 - k, lo]],
+        [agb.at[3 - k, hi], agb.at[5 - k, lo], agb.at[5 - k, hi]],
         out_s,
         out_r,
+        [agb.at[2 * i + 1 - k] for i in range(4)],
     )
     line = ExpertLine(spot, gwdn, 0, ff, *line_refs)
     gather = Gather(spot, ffn, agb, ag_s, ag_r)
@@ -675,16 +684,17 @@
     def gate_of(p, hot):
         return jnp.sum(hot * metas[p, 1:2, :], axis=1, keepdims=True)
 
-    def group(q):
-        base = chips[q]
-        rows = pl.ds(q * 2 * cap, 2 * cap)
+    def dispatch(q):
         for kk in range(2):
-            p = base + kk
+            p = chips[q] + kk
             hot = spots(p)
             low = hot.astype(BF16)
             part = pl.ds(q * 2 * cap + kk * cap, cap)
             xs[part, :] = dot(low, agb[p]).astype(BF16)
             ds[part, :] = (dot(low, cotb[p]) * gate_of(p, hot)).astype(BF16)
+
+    def work(q, count):
+        rows = pl.ds(q * 2 * cap, count * 2 * cap)
 
         @pl.loop(0, ff // step)
         def _(n):
@@ -702,35 +712,51 @@
         @pl.loop(0, width // step)
         def _(n):
             cols = lanes(n * step, step)
-            pgs[:, cols] = dot_nt(igs[rows, :], win[cols, :]).astype(BF16)
-
-        mine, theirs = rows_at(k * cap, cap), rows_at((1 - k) * cap, cap)
-        zcs = stage.at[q]
-        zcs[...] = dot_tn(spots(base + 1 - k).astype(BF16), pgs[theirs, :]).astype(BF16)
-        plane.give(q, zcs)
+            pgs[pl.ds(0, count * 2 * cap), cols] = dot(igs[rows, :], wint[:, cols]).astype(BF16)
+
+    def back(q, at):
+        base = chips[q]
+        mine, theirs = rows_at(at * 2 * cap + k * cap, cap), rows_at(at * 2 * cap + (1 - k) * cap, cap)
+        given = agb.at[base + 1 - k]
+        given[...] = dot_tn(spots(base + 1 - k).astype(BF16), pgs[theirs, :]).astype(BF16)
+        plane.give(q, given)
         plane.zk[q][...] = dot_tn(spots(base + k).astype(BF16), pgs[mine, :]).astype(BF16)
 
     for load in loads:
         load.wait()
+
+    @pl.loop(0, width // step)
+    def _(n):
+        cols = lanes(n * step, step)
+        wint[:, cols] = win[cols, :].T
+
     for n in range(planes - 1):
         source = lax.rem(me + planes - 1 - n, planes)
         remote(metas.at[source], metas.at[source], me_s.at[n], me_r.at[n], kp).wait_recv()
     gather.other_core(0)
-    group(0)
+    dispatch(0)
+    work(0, 1)
+    back(0, 0)
     gather.first()
     gather.second()
     gather.other_core(1)
-    group(1)
+    dispatch(1)
+    gather.other_core(2)
+    dispatch(2)
+    work(1, 2)
     gather.third()
-    gather.other_core(2)
-    group(2)
+    back(1, 0)
+    back(2, 1)
+    gather.other_core(3)
+    gather.done()
+    dispatch(3)
     plane.fold(1)
     plane.fold(2)
     plane.near()
-    gather.other_core(3)
-    gather.done()
-    group(3)
+    work(3, 1)
+    back(3, 0)
     plane.fold(3)
+    plane.given()
     plane.across()
 
     tall = width // ctx
@@ -743,33 +769,37 @@
 
     line.step(1)
     plane.fold(0)
-    plane.turn()
-
-    for q in (1, 2, 3, 0):
+
+    @pl.loop(0, width // step)
+    def _(n):
+        cols = lanes(n * step, step)
+        ds[:, cols] = dot_nt(hid[...], wdn[cols, :]).astype(BF16)
+
+    def returned(q):
         base = chips[q]
-
-        @pl.loop(0, width // step)
-        def _(n):
-            cols = lanes(n * step, step)
-            pgs[:, cols] = dot_nt(hid[pl.ds(q * 2 * cap, 2 * cap), :], wdn[cols, :]).astype(BF16)
-
         for kk in range(2):
             p = base + kk
             hot = spots(p)
-            rows = pgs[pl.ds(kk * cap, cap), :]
+            rows = ds[pl.ds(q * 2 * cap + kk * cap, cap), :]
             ggs[p, 0:1, :] = jnp.sum(hot * dot_nt(rows, cotb[p]), axis=0, keepdims=True)
             scaled = (rows.astype(F32) * gate_of(p, hot)).astype(BF16)
             cotb[p] = dot_tn(hot.astype(BF16), scaled).astype(BF16)
         outs.give(q, cotb.at[base + 1 - k])
-    ggr[me] = ggs[me]
-    for n, (other, dev) in enumerate(others):
-        remote(ggs.at[other], ggr.at[me], gg_s.at[n], gg_r.at[n], dev).start()
-    line.step(2)
+
+    returned(1)
+    returned(2)
+    plane.turn()
+    returned(3)
+    returned(0)
     outs.fold(1)
     outs.fold(2)
     outs.near()
     outs.fold(3)
     outs.across()
+    ggr[me] = ggs[me]
+    for n, (other, dev) in enumerate(others):
+        remote(ggs.at[other], ggr.at[me], gg_s.at[n], gg_r.at[n], dev).start()
+    line.step(2)
     outs.fold(0)
     half_wide = ff
 
@@ -790,8 +820,8 @@
 
     for slot in range(2):
         pltpu.make_async_copy(pgt.at[slot], gwin_h.at[pl.ds(0, tall), pl.ds(0, half_wide)], load_sem.at[slot]).wait()
+    line.step(3)
     outs.turn()
-    line.step(3)
     for rows, terms in plane.total():
         pg_out[rows, :] = summed(terms)
     for n in range(planes - 1):
@@ -841,10 +871,10 @@
             pltpu.VMEM((rows, width), BF16),
             pltpu.VMEM((rows, ff), BF16),
             pltpu.VMEM((rows, 2 * ff), BF16),
-            pltpu.VMEM((2 * cap, width), BF16),
+            pltpu.VMEM((4 * cap, width), BF16),
             pltpu.VMEM((planes, 8, tok), F32),
             pltpu.VMEM((planes, 8, tok), F32),
-            pltpu.VMEM((4, tok, width), BF16),
+            pltpu.VMEM((2 * ff, width), BF16),
             pltpu.VMEM((ctx, parts, piece, ff), BF16),
             pltpu.VMEM((2, width // ctx, ff), BF16),
             dma((3,)),
@@ -860,94 +890,149 @@
         + plane_scratch(tok, width)
         + expert_scratch(ctx, parts, piece, ff),
         compiler_params=pltpu.CompilerParams(
-            collective_id=1, has_side_effects=True, vmem_limit_bytes=62 * 2**20
+            collective_id=1, has_side_effects=True, vmem_limit_bytes=63 * 2**20
         ),
         cost_estimate=pl.CostEstimate(flops=25 * 10**9, bytes_accessed=50 * 10**6, transcendentals=10**6),
     )(ffn, resid, cot_all, meta, win, wdn)
 
 
-def attend_back_kernel(
+def back_kernel(
     span,
-    resid,
-    cot,
-    pg,
+    meta,
     gg,
-    meta,
-    attended,
-    ffn_in,
-    queries,
-    kv,
     lse,
     trig,
-    wout,
+    kv,
+    queries,
+    attended,
+    normed,
     router_t,
-    gain,
+    gain_two,
+    gain_one,
+    resid_h,
+    cot_h,
+    pg_h,
+    ffn_in_h,
+    hidden_h,
+    wout_h,
+    wqkv_h,
     gwin_h,
-    resid_grad,
-    mixed_grad,
-    out_red,
-    small,
-    ex_out,
+    input_grad,
+    qkv_out,
+    proj_out,
+    one_out,
+    two_out,
     *scratch,
 ):
-    gwin, osend, low, attg, mask, delta, kt, dk, dv, dq, kvs, kvr = scratch[:12]
-    load_sem, kv_s, kv_r = scratch[12:15]
-    out_refs, line_refs = scratch[15:21], scratch[21:]
+    wide_f, back, low, attg, mixed, weights, gwin, send, bsend, smalls, total, out_red = scratch[:12]
+    mask, delta, kt, dk, dv, kvs, kvr = scratch[12:19]
+    load_sem, kv_s, kv_r = scratch[19:22]
+    p_zcr, p_zk, p_rx, p_ry, p_s, p_r = scratch[22:28]
+    a_rx, a_ry, a_s, a_r = scratch[28:32]
+    b_refs, qkv_refs, proj_refs = scratch[32:38], scratch[38:41], scratch[41:44]
+    one_refs, two_refs = scratch[44:51], scratch[51:58]
     spot = Spot()
     c, k, z, ctx = spot.c, spot.k, spot.z, spot.ctx
-    tok, width = cot.shape
-    cols = ex_out.shape[2]
-    block = out_red.shape[0]
+    tok, width = attended.shape
+    cols = one_out.shape[2]
+    block, piece = out_red.shape[0], proj_out.shape[0]
     heads_kv = KV_HEADS
-    group = HEADS // KV_HEADS
     half_head = HEAD // 2
-    gwin_load = pltpu.make_async_copy(gwin_h.at[:, :, :, pl.ds(0, cols)], gwin, load_sem.at[0])
-    gwin_load.start()
+    n_experts = meta.shape[0]
+    kv_wide = mixed.shape[1] - width
+    step = 256
+
+    def load(src, dst, i):
+        copy = pltpu.make_async_copy(src, dst, load_sem.at[i])
+        copy.start()
+        return copy
+
+    gwin_load = load(gwin_h, gwin, 0)
+    early = [
+        load(resid_h, wide_f, 1),
+        load(pg_h, back, 2),
+        load(cot_h, input_grad, 3),
+        load(ffn_in_h, attg, 4),
+    ]
+    wout_load = load(wout_h, weights.at[:, pl.ds(0, width)], 5)
     greet([spot.xp, spot.yp, spot.kp, spot.yk], spot.along())
-    weights = plane_of(spot, *out_refs)
-    line = ExpertLine(spot, gwin, 0, cols, *line_refs)
+    one = ExpertLine(spot, gwin, 0, cols, *one_refs)
+    two = ExpertLine(spot, gwin, cols, cols, *two_refs)
+    proj_plane = plane_of(spot, p_zcr, p_zk, p_rx, p_ry, p_s, p_r)
+    qkv_plane = plane_of(spot, p_zcr, p_zk, a_rx, a_ry, a_s, a_r)
+    rest_plane = plane_of(spot, *b_refs)
+
+    def shared_line(ref, refs):
+        def own(d):
+            return ref.at[rows_at(d * piece, piece)]
+
+        def adder(came, d):
+            came[...] = plus(came[...], own(d)[...])
+
+        return Line(spot, own, adder, *refs)
+
+    qkv_line, proj_line = shared_line(total, qkv_refs), shared_line(out_red, proj_refs)
+
+    def put_shared(to, ref, came):
+        to[...] = plus(ref[rows_at(z * piece, piece)], *(x[...] for x in came))
+
+    mine, theirs = rows_at(k * block, block), rows_at((1 - k) * block, block)
     gwin_load.wait()
-    line.step(1)
-
-    gate = jnp.concatenate([meta[g, 1:2, :] for g in range(meta.shape[0])], axis=0)
+    one.step(1)
+
+    for copy in early:
+        copy.wait()
+    gate = jnp.concatenate([meta[g, 1:2, :] for g in range(n_experts)], axis=0)
     seen = gate * gg[...]
     mix = seen - gate * jnp.sum(seen, axis=0, keepdims=True)
-    mix = jnp.concatenate([mix, jnp.zeros((HEAD - mix.shape[0], tok), F32)], axis=0)
+    mix = jnp.concatenate([mix, jnp.zeros((HEAD - n_experts, tok), F32)], axis=0)
     logit_t = mix.astype(BF16)
-    r = resid[...]
+    r = wide_f[...]
     inv = lax.rsqrt(jnp.mean(r * r, axis=-1, keepdims=True) + NORM_EPS)
     plain = r * inv
-    ffn_grad = pg[...] + dot_tn(logit_t[: router_t.shape[0]], router_t[...])
+    ffn_grad = back[...] + dot_tn(logit_t[:n_experts], router_t[...])
     gain_row = jnp.sum(ffn_grad * plain, axis=0, keepdims=True)
-    scaled = ffn_grad * gain[...]
-    back = cot[...].astype(F32) + inv * (
+    scaled = ffn_grad * gain_two[...]
+    grad = input_grad[...].astype(F32) + inv * (
         scaled - plain * jnp.mean(scaled * plain, axis=-1, keepdims=True)
     )
-    resid_grad[...] = back
-    low[...] = back.astype(BF16)
+    back[...] = grad
+    low[...] = grad.astype(BF16)
     lane = lax.broadcasted_iota(jnp.int32, (width, HEAD), 1)
+    routed = dot_tn(attg[...], logit_t.T)
     gain_col = jnp.broadcast_to(gain_row, (HEAD, width)).T
-    routed = dot_tn(ffn_in[...], logit_t.T)
-    small[...] = jnp.where(lane == gate.shape[0], gain_col, routed).astype(BF16)
+    smalls[...] = jnp.where(lane == n_experts, gain_col, routed).astype(BF16)
 
     for q in (1, 2, 3, 0):
         at = lanes(spot.chips[q] * block, 2 * block)
-        osend[q] = dot_tn(low[:, at], attended[...]).astype(BF16)
-        weights.give(q, osend.at[q, rows_at((1 - k) * block, block)])
-
-    step = 256
+        send[q] = dot_tn(low[:, at], attended[...]).astype(BF16)
+        proj_plane.give(q, send.at[q, theirs])
+    wout_load.wait()
 
     @pl.loop(0, width // step)
     def _(n):
         at = lanes(n * step, step)
-        attg[:, at] = dot(low[...], wout[:, at]).astype(BF16)
+        attg[:, at] = dot(low[...], weights[:, at]).astype(BF16)
+
+    wqkv_load = load(wqkv_h, weights, 5)
+    hidden_load = load(hidden_h, low, 1)
+
+    def start_plane(plane):
+        plane.fold(1, send[1, mine])
+        plane.fold(2, send[2, mine])
+        plane.near()
+        plane.fold(3, send[3, mine])
+        plane.across()
+        plane.fold(0, send[0, mine])
+
+    start_plane(proj_plane)
 
     seq = kv.shape[0]
     spans = span.shape[1]
     size = seq // spans
-    mine = spans // ctx
+    per = spans // ctx
     along_q = lax.broadcasted_iota(jnp.int32, (size, tok), 1)
-    q_pos = jnp.where(along_q < size, span[0, c * mine] * size, (span[0, c * mine + 1] - 1) * size) + along_q
+    q_pos = jnp.where(along_q < size, span[0, c * per] * size, (span[0, c * per + 1] - 1) * size) + along_q
     for s in range(spans):
         k_pos = span[0, s] * size + lax.broadcasted_iota(jnp.int32, (size, tok), 0)
         mask[s * size : (s + 1) * size, :] = jnp.where(k_pos <= q_pos, 0.0, MASKED)
@@ -962,6 +1047,11 @@
     for g in range(heads_kv):
         kt[g] = kv[:, g * HEAD : (g + 1) * HEAD].astype(F32).T.astype(BF16)
 
+    cosine, sine = trig[0], trig[1]
+
+    def unrotate(w):
+        return w * cosine - pltpu.roll(w, half_head, 1) * sine
+
     def head(g, h):
         at = lanes(h * HEAD, HEAD)
         k_at = slice(g * HEAD, (g + 1) * HEAD)
@@ -970,276 +1060,197 @@
         soft = jnp.exp(dot_nt(kv[:, k_at], q) + mask[...] - lse[pl.ds(h, 1), :])
         prob = dot_nt(kv[:, v_at], a)
         score = (soft * (prob - delta[pl.ds(h, 1), :])).astype(BF16)
-        dq[:, at] = dot(kt[g], score).T
+        mixed[:, at] = (unrotate(dot(kt[g], score).T) * HEAD**-0.5).astype(BF16)
         dk[...] += dot(score, q)
         dv[...] += dot(soft.astype(BF16), a)
+
+    def heads(g, first, count):
+        @pl.loop(first, first + count)
+        def _(h):
+            head(g, h)
+
+    def clear():
+        dk[...] = jnp.zeros(dk.shape, F32)
+        dv[...] = jnp.zeros(dv.shape, F32)
+
+    flip_c = lax.rem(c + 2, ctx)
+    near_c = c + 1 - 2 * k
+    across_c = lax.rem(near_c + 2, ctx)
+
+    def kv_copy(g, src, i, dev):
+        return remote(src, kvr.at[g, i], kv_s.at[g, i], kv_r.at[g, i], dev)
 
     def send_kv(g):
         for cc in range(ctx):
             rows = slice(cc * tok, (cc + 1) * tok)
             kvs[g, cc, :, :HEAD] = dk[rows, :].astype(BF16)
             kvs[g, cc, :, HEAD:] = dv[rows, :].astype(BF16)
-        for n in range(1, ctx):
-            cc = lax.rem(c + n, ctx)
-            remote(kvs.at[g, cc], kvr.at[g, c], kv_s.at[g, n - 1], kv_r.at[g, n - 1], (spot.e, cc, z)).start()
-
-    def heads(g, first, count):
-        @pl.loop(first, first + count)
-        def _(h):
-            head(g, h)
-
-    def clear():
-        dk[...] = jnp.zeros(dk.shape, F32)
-        dv[...] = jnp.zeros(dv.shape, F32)
-
-    def own_part(q):
-        return osend[q, rows_at(k * block, block)]
+        kv_copy(g, kvs.at[g, across_c], 1, spot.kp).start()
+        kv_copy(g, kvs.at[g, near_c], 0, spot.kp).start()
+
+    def pass_kv(g):
+        kv_copy(g, kvs.at[g, across_c], 1, spot.kp).wait_recv()
+        kvs[g, flip_c] = plus(kvs[g, flip_c], kvr[g, 1])
+        kv_copy(g, kvs.at[g, flip_c], 2, spot.yp).start()
 
     clear()
     heads(0, 0, 2)
-    for q in (1, 2):
-        weights.fold(q, own_part(q))
-    weights.near()
-    weights.fold(3, own_part(3))
-    weights.across()
-    weights.fold(0, own_part(0))
-    heads(0, 2, 2)
-    line.step(2)
-    heads(0, 4, 2)
+    one.step(2)
+    heads(0, 2, 4)
     send_kv(0)
-    weights.turn()
     clear()
-    heads(1, 6, 2)
-    line.step(3)
-    heads(1, 8, 2)
-    heads(1, 10, 2)
+    proj_plane.turn()
+    heads(1, 6, 3)
+    pass_kv(0)
+    one.step(3)
+    two.step(1)
+    heads(1, 9, 3)
     send_kv(1)
-    cosine, sine = trig[0], trig[1]
-
-    def unrotate(w):
-        return w * cosine - pltpu.roll(w, half_head, 1) * sine
-
-    for h in range(HEADS):
-        at = slice(h * HEAD, (h + 1) * HEAD)
-        mixed_grad[:, at] = (unrotate(dq[:, at]) * HEAD**-0.5).astype(BF16)
-    line.final()
-    for rows, terms in weights.total():
+    pass_kv(1)
+    for rows, terms in proj_plane.total():
         out_red[rows, :] = summed(terms).astype(BF16)
+    proj_line.step(1)
+    proj_plane.done()
     for g in range(heads_kv):
-        own = kvs[g, c].astype(F32)
-        for n in range(1, ctx):
-            cc = lax.rem(c + ctx - n, ctx)
-            got = remote(kvr.at[g, cc], kvr.at[g, cc], kv_s.at[g, n - 1], kv_r.at[g, n - 1], spot.kp)
-            got.wait_recv()
-            own = own + kvr[g, cc].astype(F32)
+        kv_copy(g, kvs.at[g, near_c], 0, spot.kp).wait_recv()
+        kv_copy(g, kvs.at[g, flip_c], 2, spot.yp).wait_recv()
+        own = kvs[g, c].astype(F32) + kvr[g, 0].astype(F32) + kvr[g, 2].astype(F32)
         at = width + g * HEAD
-        mixed_grad[:, at : at + HEAD] = unrotate(own[:, :HEAD]).astype(BF16)
+        mixed[:, at : at + HEAD] = unrotate(own[:, :HEAD]).astype(BF16)
         at = width + (heads_kv + g) * HEAD
-        mixed_grad[:, at : at + HEAD] = own[:, HEAD:].astype(BF16)
+        mixed[:, at : at + HEAD] = own[:, HEAD:].astype(BF16)
+
+    for q in (1, 2, 3, 0):
+        at = lanes(spot.chips[q] * block, 2 * block)
+        send[q] = dot_tn(normed[:, at], mixed[:, :width]).astype(BF16)
+        qkv_plane.give(q, send.at[q, theirs])
+    start_plane(qkv_plane)
+    one.final()
+    proj_line.step(2)
+    wqkv_load.wait()
+
+    @pl.loop(0, width // step)
+    def _(n):
+        at = lanes(n * step, step)
+        wide_f[:, at] = dot_nt(mixed[...], weights[at, :])
+
+    hidden_load.wait()
+    x = low[...].astype(F32)
+    inv = lax.rsqrt(jnp.mean(x * x, axis=-1, keepdims=True) + NORM_EPS)
+    plain = x * inv
+    ng = wide_f[...]
+    gain_row = jnp.sum(ng * plain, axis=0, keepdims=True)
+    scaled = ng * gain_one[...]
+    input_grad[...] = (
+        back[...] + inv * (scaled - plain * jnp.mean(scaled * plain, axis=-1, keepdims=True))
+    ).astype(BF16)
+    lane = lax.broadcasted_iota(jnp.int32, (width, HEAD), 1)
+    gain_col = jnp.broadcast_to(gain_row, (HEAD, width)).T
+    smalls[...] = jnp.where(lane == HEAD - 1, gain_col, smalls[...].astype(F32)).astype(BF16)
+    for q in (1, 2, 3, 0):
+        at = lanes(spot.chips[q] * block, 2 * block)
+        bsend[q, :, :kv_wide] = dot_tn(normed[:, at], mixed[:, width:]).astype(BF16)
+        bsend[q, :, kv_wide:] = smalls[rows_at(spot.chips[q] * block, 2 * block), :]
+        rest_plane.give(q, bsend.at[q, theirs])
+    rest_plane.fold(1, bsend[1, mine])
+    rest_plane.fold(2, bsend[2, mine])
+    rest_plane.near()
+    rest_plane.fold(3, bsend[3, mine])
+    rest_plane.across()
+    rest_plane.fold(0, bsend[0, mine])
+    two.step(2)
+    qkv_plane.turn()
+    rest_plane.turn()
+    proj_line.step(3)
+    for rows, terms in qkv_plane.total():
+        total[rows, :width] = summed(terms).astype(BF16)
+    for rows, terms in rest_plane.total():
+        total[rows, width:] = summed(terms).astype(BF16)
+    qkv_line.step(1)
+    one.done(one_out)
+    two.step(3)
+    qkv_line.step(2)
+    proj_line.final(lambda *came: put_shared(proj_out, out_red, came))
+    qkv_line.step(3)
+    two.final()
+    proj_line.done()
+    qkv_plane.done()
+    rest_plane.done()
     for g in range(heads_kv):
-        for n in range(1, ctx):
-            cc = lax.rem(c + n, ctx)
-            remote(kvs.at[g, cc], kvr.at[g, cc], kv_s.at[g, n - 1], kv_r.at[g, n - 1], spot.kp).wait_send()
-    weights.done()
-    line.done(ex_out)
-
-
-def run_attend_back(
-    span, resid, cot, pg, gg, meta, attended, ffn_in, queries, kv, lse, trig, wout, router_t, gain, gwin
+        kv_copy(g, kvs.at[g, near_c], 0, spot.kp).wait_send()
+        kv_copy(g, kvs.at[g, across_c], 1, spot.kp).wait_send()
+        kv_copy(g, kvs.at[g, flip_c], 2, spot.yp).wait_send()
+    qkv_line.final(lambda *came: put_shared(qkv_out, total, came))
+    qkv_line.done()
+    two.done(two_out)
+
+
+def run_back(
+    span, meta, gg, lse, trig, kv, queries, attended, normed, router_t, gain_two, gain_one,
+    resid, cot, pg, ffn_in, hidden, wout, wqkv, gwin,
 ):
-    tok, width = cot.shape
-    ctx, parts, piece, wide = gwin.shape
+    tok, width = attended.shape
+    seq, kv_cols = kv.shape
     planes = meta.shape[0]
+    ctx, parts, rows, wide = gwin.shape
     cols = wide // 2
     block = width // planes
-    seq, kv_cols = kv.shape
+    piece = block // parts
+    rest = kv_cols + HEAD
     vm, anyspace = pl.BlockSpec(memory_space=pltpu.VMEM), pl.BlockSpec(memory_space=pl.ANY)
     sm = pl.BlockSpec(memory_space=pltpu.SMEM)
     shape = jax.ShapeDtypeStruct
     dma = pltpu.SemaphoreType.DMA
     return pl.pallas_call(
-        attend_back_kernel,
+        back_kernel,
         out_shape=(
-            shape((tok, width), F32),
-            shape((tok, width + kv_cols), BF16),
-            shape((block, width), BF16),
-            shape((width, HEAD), BF16),
-            shape((ctx, piece, cols), BF16),
+            shape((tok, width), BF16),
+            shape((piece, width + rest), BF16),
+            shape((piece, width), BF16),
+            shape((ctx, rows, cols), BF16),
+            shape((ctx, rows, cols), BF16),
         ),
-        in_specs=[sm] + [vm] * 14 + [anyspace],
+        in_specs=[sm] + [vm] * 11 + [anyspace] * 8,
         out_specs=(vm,) * 5,
         scratch_shapes=[
-            pltpu.VMEM((ctx, parts, piece, cols), BF16),
-            pltpu.VMEM((4, 2 * block, width), BF16),
+            pltpu.VMEM((tok, width), F32),
+            pltpu.VMEM((tok, width), F32),
             pltpu.VMEM((tok, width), BF16),
             pltpu.VMEM((tok, width), BF16),
+            pltpu.VMEM((tok, width + kv_cols), BF16),
+            pltpu.VMEM(wqkv.shape, BF16),
+            pltpu.VMEM(gwin.shape, BF16),
+            pltpu.VMEM((4, 2 * block, width), BF16),
+            pltpu.VMEM((4, 2 * block, rest), BF16),
+            pltpu.VMEM((width, HEAD), BF16),
+            pltpu.VMEM((block, width + rest), BF16),
+            pltpu.VMEM((block, width), BF16),
             pltpu.VMEM((seq, tok), F32),
             pltpu.VMEM((HEAD, tok), F32),
             pltpu.VMEM((KV_HEADS, HEAD, seq), BF16),
             pltpu.VMEM((seq, HEAD), F32),
             pltpu.VMEM((seq, HEAD), F32),
-            pltpu.VMEM((tok, width), F32),
             pltpu.VMEM((KV_HEADS, ctx, tok, 2 * HEAD), BF16),
-            pltpu.VMEM((KV_HEADS, ctx, tok, 2 * HEAD), BF16),
-            dma((1,)),
-            dma((KV_HEADS, ctx - 1)),
-            dma((KV_HEADS, ctx - 1)),
+            pltpu.VMEM((KV_HEADS, 3, tok, 2 * HEAD), BF16),
+            dma((6,)),
+            dma((KV_HEADS, 3)),
+            dma((KV_HEADS, 3)),
         ]
         + plane_scratch(block, width)
-        + expert_scratch(ctx, parts, piece, cols),
-        compiler_params=pltpu.CompilerParams(
-            collective_id=2, has_side_effects=True, vmem_limit_bytes=62 * 2**20
-        ),
-        cost_estimate=pl.CostEstimate(flops=8 * 10**9, bytes_accessed=40 * 10**6, transcendentals=10**6),
-    )(
-        span, resid, cot, pg, gg, meta, attended, ffn_in, queries, kv, lse, trig, wout, router_t, gain, gwin
-    )
-
-
-def last_kernel(
-    normed, mixed_grad, hidden, resid_grad, wqkv, gain, small, out_red, gwin_h, input_grad, qkv_out, proj_out, ex_out, *scratch
-):
-    gwin, asend, bsend, norm_grad, smalls, total, load_sem = scratch[:7]
-    a_refs, b_refs, qkv_refs, proj_refs, line_refs = (
-        scratch[7:13],
-        scratch[13:19],
-        scratch[19:22],
-        scratch[22:25],
-        scratch[25:],
-    )
-    spot = Spot()
-    k, z = spot.k, spot.z
-    tok, width = normed.shape
-    cols = ex_out.shape[2]
-    block = out_red.shape[0]
-    piece = proj_out.shape[0]
-    kv_wide = mixed_grad.shape[1] - width
-    load = pltpu.make_async_copy(gwin_h.at[:, :, :, pl.ds(cols, cols)], gwin, load_sem.at[0])
-    load.start()
-    greet([spot.xp, spot.yp, spot.kp, spot.yk], spot.along())
-    first, second = plane_of(spot, *a_refs), plane_of(spot, *b_refs)
-    line = ExpertLine(spot, gwin, 0, cols, *line_refs)
-
-    def shared_line(ref, refs):
-        def own(d):
-            return ref.at[rows_at(d * piece, piece)]
-
-        def adder(came, d):
-            came[...] = plus(came[...], own(d)[...])
-
-        return Line(spot, own, adder, *refs)
-
-    qkv, proj = shared_line(total, qkv_refs), shared_line(out_red, proj_refs)
-    def put_shared(to, ref, came):
-        to[...] = plus(ref[rows_at(z * piece, piece)], *(x[...] for x in came))
-
-    mine, theirs = rows_at(k * block, block), rows_at((1 - k) * block, block)
-    load.wait()
-    line.step(1)
-    proj.step(1)
-    for q in (1, 2, 3, 0):
-        at = lanes(spot.chips[q] * block, 2 * block)
-        asend[q] = dot_tn(normed[:, at], mixed_grad[:, :width]).astype(BF16)
-        first.give(q, asend.at[q, theirs])
-    first.fold(1, asend[1, mine])
-    first.fold(2, asend[2, mine])
-    first.near()
-    first.fold(3, asend[3, mine])
-    first.across()
-    first.fold(0, asend[0, mine])
-
-    step = 256
-
-    @pl.loop(0, width // step)
-    def _(n):
-        at = lanes(n * step, step)
-        norm_grad[:, at] = dot_nt(mixed_grad[...], wqkv[at, :])
-
-    x = hidden[...].astype(F32)
-    inv = lax.rsqrt(jnp.mean(x * x, axis=-1, keepdims=True) + NORM_EPS)
-    plain = x * inv
-    ng = norm_grad[...]
-    gain_row = jnp.sum(ng * plain, axis=0, keepdims=True)
-    scaled = ng * gain[...]
-    input_grad[...] = (
-        resid_grad[...]
-        + inv * (scaled - plain * jnp.mean(scaled * plain, axis=-1, keepdims=True))
-    ).astype(BF16)
-    lane = lax.broadcasted_iota(jnp.int32, (width, HEAD), 1)
-    gain_col = jnp.broadcast_to(gain_row, (HEAD, width)).T
-    smalls[...] = jnp.where(lane == HEAD - 1, gain_col, small[...].astype(F32)).astype(BF16)
-    for q in (1, 2, 3, 0):
-        at = lanes(spot.chips[q] * block, 2 * block)
-        bsend[q, :, :kv_wide] = dot_tn(normed[:, at], mixed_grad[:, width:]).astype(BF16)
-        bsend[q, :, kv_wide:] = smalls[rows_at(spot.chips[q] * block, 2 * block), :]
-        second.give(q, bsend.at[q, theirs])
-    first.turn()
-    second.fold(1, bsend[1, mine])
-    second.fold(2, bsend[2, mine])
-    second.near()
-    second.fold(3, bsend[3, mine])
-    second.across()
-    second.fold(0, bsend[0, mine])
-    line.step(2)
-    proj.step(2)
-    for rows, terms in first.total():
-        total[rows, :width] = summed(terms).astype(BF16)
-    second.turn()
-    line.step(3)
-    proj.step(3)
-    for rows, terms in second.total():
-        total[rows, width:] = summed(terms).astype(BF16)
-    qkv.step(1)
-    proj.final(lambda *came: put_shared(proj_out, out_red, came))
-    line.final()
-    qkv.step(2)
-    line.done(ex_out)
-    qkv.step(3)
-    proj.done()
-    first.done()
-    second.done()
-    qkv.final(lambda *came: put_shared(qkv_out, total, came))
-    qkv.done()
-
-
-def run_last(normed, mixed_grad, hidden, resid_grad, wqkv, gain, small, out_red, gwin):
-    tok, width = normed.shape
-    block = out_red.shape[0]
-    ctx, parts, rows, wide = gwin.shape
-    cols = wide // 2
-    piece = block // parts
-    rest = mixed_grad.shape[1] - width + HEAD
-    vm, anyspace = pl.BlockSpec(memory_space=pltpu.VMEM), pl.BlockSpec(memory_space=pl.ANY)
-    shape = jax.ShapeDtypeStruct
-    return pl.pallas_call(
-        last_kernel,
-        out_shape=(
-            shape((tok, width), BF16),
-            shape((piece, width + rest), BF16),
-            shape((piece, width), BF16),
-            shape((ctx, rows, cols), BF16),
-        ),
-        in_specs=[vm] * 8 + [anyspace],
-        out_specs=(vm,) * 4,
-        scratch_shapes=[
-            pltpu.VMEM((ctx, parts, rows, cols), BF16),
-            pltpu.VMEM((4, 2 * block, width), BF16),
-            pltpu.VMEM((4, 2 * block, rest), BF16),
-            pltpu.VMEM((tok, width), F32),
-            pltpu.VMEM((width, HEAD), BF16),
-            pltpu.VMEM((block, width + rest), BF16),
-            pltpu.SemaphoreType.DMA((1,)),
-        ]
-        + plane_scratch(block, width)
+        + plane_scratch(block, width)[2:]
         + plane_scratch(block, rest)
         + line_scratch(parts, (piece, width + rest))
         + line_scratch(parts, (piece, width))
+        + expert_scratch(ctx, parts, rows, cols)
         + expert_scratch(ctx, parts, rows, cols),
         compiler_params=pltpu.CompilerParams(
-            collective_id=3, has_side_effects=True, vmem_limit_bytes=62 * 2**20
+            collective_id=2, has_side_effects=True, vmem_limit_bytes=63 * 2**20
         ),
-        cost_estimate=pl.CostEstimate(flops=4 * 10**9, bytes_accessed=40 * 10**6, transcendentals=0),
-    )(normed, mixed_grad, hidden, resid_grad, wqkv, gain, small, out_red, gwin)
+        cost_estimate=pl.CostEstimate(flops=12 * 10**9, bytes_accessed=60 * 10**6, transcendentals=4 * 10**6),
+    )(
+        span, meta, gg, lse, trig, kv, queries, attended, normed, router_t, gain_two, gain_one,
+        resid, cot, pg, ffn_in, hidden, wout, wqkv, gwin,
+    )
 
 
 def finish_kernel(
@@ -1332,26 +1343,27 @@
         capacity, ffn_in, resid, cot_all, meta, in_weight, down_weight, parts
     )
     gwin = gwin.reshape(ctx, parts, width // (ctx * parts), 2 * ff)
-    resid_grad, mixed_grad, out_red, small, in_one = run_attend_back(
+    input_grad, qkv_sum, proj_sum, in_one, in_two = run_back(
         span_order,
+        meta,
+        gate_grad,
+        lse,
+        trig,
+        kv,
+        queries,
+        attended,
+        normed,
+        router_t,
+        gain_ffn,
+        gain_attn,
         resid,
         cot,
         pair_sum,
-        gate_grad,
-        meta,
-        attended,
         ffn_in,
-        queries,
-        kv,
-        lse,
-        trig,
+        hidden,
         out_weight,
-        router_t,
-        gain_ffn,
+        qkv_weight,
         gwin,
-    )
-    input_grad, qkv_sum, proj_sum, in_two = run_last(
-        normed, mixed_grad, hidden, resid_grad, qkv_weight, gain_attn, small, out_red, gwin
     )
     output, input_grad, gains, qkv_grad, proj_grad, router_grad, inner_grad, down_grad = run_finish(
         n_experts, output, input_grad, qkv_sum, proj_sum, in_one, in_two, down

time: 308 us -> 276 us (0.90)
  Pallas kernels: 296 us -> 263 us
    pallas_call x2 -> x1, Pallas kernels: 136 us -> 112 us  [run_back(): pl.pallas_call(back_kernel, out_shape=(shape((tok, width), BF16), shape((...]
    pallas_call x1, Pallas kernels: 114 us -> 104 us  [run_ffn(): pl.pallas_call(functools.partial(ffn_kernel, cap), out_shape=(shape((tok,...]
where the time goes in v5:
time: 276 us; the launch traced here: 271 us
  Pallas kernels  263 us (95%)
  local copies, waits for them, and re-layouts  7.34 us (3%)
    pallas_call x1, Pallas kernels, run_back(): pl.pallas_call(back_kernel, out_shape=(shape((tok, width), BF16), shape((...  112 us
    pallas_call x1, Pallas kernels, run_ffn(): pl.pallas_call(functools.partial(ffn_kernel, cap), out_shape=(shape((tok,...  104 us
    pallas_call x1, Pallas kernels, run_front(): pl.pallas_call(functools.partial(front_kernel, cap), out_shape=(shape((to...  44.1 us
    unnamed x15, local copies, waits for them, and re-layouts  6.82 us

profile of v5, /device:TPU:0, one launch (start us, length us, event | category | flops | bytes accessed | tf_op | source)
XLA Modules:
  0.0 271.1 jit_solution(2174366532161889349)
XLA Ops:
  0.6 44.1 %shard_map.196 = (bf16[256,1536]{1,0:T(8,128)(2,1)}, bf16[256,1536]{1,0:T(8,128)(2,1)}, bf16[1024,512]{1,0:T(8,128)(2,1)}, f32[16,256]{1,0:T(8,128)}, bf16[256,1...) custom-call(s32[1,8]{1,0:T(1,128)} %span.3, ...), custom_call_target="tpu_custom_call" | custom-call | flops 5000000000 | bytes 20000000 | tf_op jit(solution)/shard_map/pallas_call | solution.py:603
  44.8 103.8 %shard_map.197 = (bf16[256,1536]{1,0:T(8,128)(2,1)}, f32[256,1536]{1,0:T(8,128)}, f32[8,256]{1,0:T(8,128)}, bf16[1536,1536]{1,0:T(8,128)(2,1)}, bf16[4,96,768]{2,1,0:T(8,128)(2,1)}) custom-call(bf16[256,1536]{1,0:T(8,128)(2,1)} %get-tuple-element.37.ffn.ffn_in_h, f32[256,1536]{1,0:T(8,128)} %get-tuple-element.38.resid.resid_h, ...), custom_call_target="tpu_custom_call" | custom-call | flops 24999999488 | bytes 50000000 | tf_op jit(solution)/shard_map/pallas_call | solution.py:853
  148.5 0.0 copy-start
  148.6 112.4 %shard_map.198 = (bf16[256,1536]{1,0:T(8,128)(2,1)}, bf16[48,2176]{1,0:T(8,128)(2,1)}, bf16[48,1536]{1,0:T(8,128)(2,1)}, bf16[4,96,768]{2,1,0:T(8,128)(2,1)}, bf16[4,96,768]{2,1,0:T(8,128)(2,1)}) custom-call(s32[1,8]{1,0:T(1,128)} %span.3, f32[8,8,256]{2,1,0:T(8,128)} %get-tuple-element.40.meta, f32[8,256]{1,0:T(8,128)} %get-tuple-element.42.gg, ...), custom_call_target="tpu_custom_call" | custom-call | flops 12000000000 | bytes 60000000 | tf_op jit(solution)/shard_map/pallas_call | solution.py:1204
  260.9 0.0 copy-done
  260.9 0.0 copy-start.1
  261.0 1.1 copy-done.1
  262.1 0.0 copy-start.2
  262.1 1.1 copy-done.2
  263.1 0.0 copy-start.3
  263.1 1.1 copy-done.3
  264.2 0.0 copy-start.4
  264.2 1.1 copy-done.4
  265.3 0.0 copy-start.5
  265.3 0.9 copy-done.5
  266.2 0.0 copy-start.6
  266.2 0.9 copy-done.6
  267.1 2.6 shard_map.199
  269.7 0.5 slice_bitcast_fusion
  270.2 0.7 copy.22
Async XLA Ops:
  148.5 112.4 %copy-start = (bf16[256,1536]{1,0:T(8,128)(2,1)S(1)}, bf16[256,1536]{1,0:T(8,128)(2,1)}, u32[]{:S(2)}) copy-start(bf16[256,1536]{1,0:T(8,128)(2,1)} %get-tuple-element.41.output_low) | copy-start | bytes 2359300
  260.9 1.1 copy-start.1
  262.1 1.1 copy-start.2
  263.1 1.1 copy-start.3
  264.2 1.1 copy-start.4
  265.3 0.9 copy-start.5
  266.2 0.9 copy-start.6

commit v6 on v5

--- a/solution.py
+++ b/solution.py
@@ -61,6 +61,9 @@
 MESH = pl.DeviceIdType.MESH
 F32 = jnp.float32
 BF16 = jnp.bfloat16
+BACK_LOW = 96
+OUT_LOW = 128
+FRONT_LOW = 96
 
 
 def dot(a, b):
@@ -140,11 +143,11 @@
 
 
 class Plane:
-    def __init__(self, spot, zcr, zk, rx, ry, s, r, zcr_there=None):
+    def __init__(self, spot, zcr, zk, rx, ry, s, r, zcr_there=None, low=None):
         self.zcr_there = zcr_there or zcr
         self.spot, self.zcr, self.zk, self.rx, self.ry, self.s, self.r = spot, zcr, zk, rx, ry, s, r
-        half = zk[0].shape[0] // 2
-        self.lo, self.hi = pl.ds(0, half), pl.ds(half, half)
+        low = low or zk[0].shape[0] // 2
+        self.lo, self.hi = pl.ds(0, low), pl.ds(low, zk[0].shape[0] - low)
         self.sent, self.gives = [], []
 
     def push(self, src, dst, i, dev):
@@ -201,19 +204,28 @@
             copy.wait_send()
 
 
-def plane_of(spot, zcr, zk, rx, ry, s, r):
-    four, three = range(4), range(3)
+def plane_of(spot, zcr, zk, rx, ry, s, r, low=None):
+    four, block = range(4), zk.shape[1]
+    lo, hi = pl.ds(0, low or block // 2), pl.ds(0, block - (low or block // 2))
     return Plane(
-        spot, [zcr.at[q] for q in four], [zk.at[q] for q in four], [rx.at[i] for i in three], [ry.at[i] for i in three], s, r
-    )
-
-
-def plane_scratch(block, wide):
+        spot,
+        [zcr.at[q] for q in four],
+        [zk.at[q] for q in four],
+        [rx.at[0, lo], rx.at[1, lo], rx.at[2, hi]],
+        [ry.at[0, hi], ry.at[1, hi], ry.at[2, lo]],
+        s,
+        r,
+        low=low,
+    )
+
+
+def plane_scratch(block, wide, low=None):
+    most = max(low or block // 2, block - (low or block // 2))
     return [
         pltpu.VMEM((4, block, wide), BF16),
         pltpu.VMEM((4, block, wide), BF16),
-        pltpu.VMEM((3, block // 2, wide), BF16),
-        pltpu.VMEM((3, block // 2, wide), BF16),
+        pltpu.VMEM((3, most, wide), BF16),
+        pltpu.VMEM((3, most, wide), BF16),
         pltpu.SemaphoreType.DMA((10,)),
         pltpu.SemaphoreType.DMA((10,)),
     ]
@@ -346,10 +358,10 @@
 
 
 class Gather:
-    def __init__(self, spot, own, buf, s, r):
+    def __init__(self, spot, own, buf, s, r, low=None):
         self.spot, self.own, self.buf, self.s, self.r = spot, own, buf, s, r
-        half = own.shape[0] // 2
-        self.lo, self.hi = pl.ds(0, half), pl.ds(half, half)
+        low = low or own.shape[0] // 2
+        self.lo, self.hi = pl.ds(0, low), pl.ds(low, own.shape[0] - low)
         self.x_me, self.y_me, self.d_me = (base + spot.k for base in spot.chips[1:])
         self.side = 1 - 2 * spot.k
         self.sent = []
@@ -466,7 +478,7 @@
     for load in loads:
         load.start()
     greet([spot.xp, spot.yp, spot.kp])
-    gather = Gather(spot, cot, cot_all, co_s, co_r)
+    gather = Gather(spot, cot, cot_all, co_s, co_r, low=FRONT_LOW)
     gather.start()
 
     x = hidden[...].astype(F32)
@@ -634,14 +646,14 @@
     )(span, hidden, cot, gain_one, freqs, gain_two, router_t, ids_t, turn_t, wqkv, wout)
 
 
-def ffn_kernel(cap, ffn, resid, cot_h, meta, win_h, wdn_h, output, pg_out, gg_out, gwin_h, ex_out, *scratch):
-    agb, metas, cotb, win, wdn, xs, ds, hid, igs, pgs, ggs, ggr, wint, gwdn, pgt = scratch[:15]
-    load_sem, ag_s, ag_r, me_s, me_r, gg_s, gg_r, out_s, out_r = scratch[15:24]
-    plane_refs, line_refs = scratch[24:30], scratch[30:]
+def ffn_kernel(cap, ffn_h, resid_h, cot_h, meta, win_h, wdn_h, output, pg_out, gg_out, gwin_h, ex_out, first_out, *scratch):
+    agb, metas, cotb, win, wdn, xs, ds, hid, igs, pgs, ggs, ggr, wint, gwdn = scratch[:14]
+    load_sem, ag_s, ag_r, me_s, me_r, gg_s, gg_r, out_s, out_r = scratch[14:23]
+    plane_refs, line_refs, first_refs = scratch[23:29], scratch[29:36], scratch[36:]
     spot = Spot()
     c, k, me = spot.c, spot.k, spot.me
     kp = spot.kp
-    tok, width = ffn.shape
+    tok, width = output.shape
     ff = wdn.shape[1]
     planes, ctx = spot.planes, spot.ctx
     chips = spot.chips
@@ -650,30 +662,36 @@
         pltpu.make_async_copy(win_h.at[c], win, load_sem.at[0]),
         pltpu.make_async_copy(wdn_h.at[c], wdn, load_sem.at[1]),
         pltpu.make_async_copy(cot_h, cotb, load_sem.at[2]),
+        pltpu.make_async_copy(resid_h, pg_out, load_sem.at[3]),
     ]
+    own_load = pltpu.make_async_copy(ffn_h, agb.at[me], load_sem.at[4])
+    own_load.start()
     for load in loads:
         load.start()
     others = spot.others()
     greet([dev for _, dev in others], spot.along())
     plane = plane_of(spot, *plane_refs)
-    lo, hi = plane.lo, plane.hi
+    o_lo, o_hi = pl.ds(0, OUT_LOW), pl.ds(OUT_LOW, tok - OUT_LOW)
     outs = Plane(
         spot,
         [agb.at[2 * i + k] for i in range(4)],
         [cotb.at[base + k] for base in chips],
-        [agb.at[1 - k, lo], agb.at[1 - k, hi], agb.at[3 - k, lo]],
-        [agb.at[3 - k, hi], agb.at[5 - k, lo], agb.at[5 - k, hi]],
+        [agb.at[1 - k, o_lo], agb.at[3 - k, o_lo], agb.at[1 - k, o_hi]],
+        [agb.at[3 - k, o_hi], agb.at[5 - k, o_hi], agb.at[5 - k, o_lo]],
         out_s,
         out_r,
         [agb.at[2 * i + 1 - k] for i in range(4)],
+        low=OUT_LOW,
     )
     line = ExpertLine(spot, gwdn, 0, ff, *line_refs)
-    gather = Gather(spot, ffn, agb, ag_s, ag_r)
+    some = first_out.shape[2]
+    first_line = ExpertLine(spot, win, 0, some, *first_refs)
+    gather = Gather(spot, agb.at[me], agb, ag_s, ag_r)
     for step, (other, dev) in enumerate(others):
         remote(meta.at[other], metas.at[me], me_s.at[step], me_r.at[step], dev).start()
+    own_load.wait()
     gather.start()
     gather.start_y()
-    agb[me] = ffn[...]
     metas[me] = meta[me]
     slot_rows = lax.broadcasted_iota(jnp.int32, (cap, tok), 0).astype(F32)
     step = 256
@@ -700,8 +718,8 @@
         def _(n):
             gate_cols, up_cols = lanes(n * step, step), lanes(ff + n * step, step)
             x = xs[rows, :]
-            g = dot(x, win[:, gate_cols])
-            u = dot(x, win[:, up_cols])
+            g = dot(x, win[:, :, :, gate_cols].reshape(width, step))
+            u = dot(x, win[:, :, :, up_cols].reshape(width, step))
             s = 1.0 / (1.0 + jnp.exp(-g))
             act = g * s
             hid[rows, gate_cols] = (act * u).astype(BF16)
@@ -725,10 +743,11 @@
     for load in loads:
         load.wait()
 
-    @pl.loop(0, width // step)
+    tall = width // ctx
+
+    @pl.loop(0, ctx)
     def _(n):
-        cols = lanes(n * step, step)
-        wint[:, cols] = win[cols, :].T
+        wint[:, lanes(n * tall, tall)] = win[n].reshape(tall, 2 * ff).T
 
     for n in range(planes - 1):
         source = lax.rem(me + planes - 1 - n, planes)
@@ -759,7 +778,6 @@
     plane.given()
     plane.across()
 
-    tall = width // ctx
 
     @pl.loop(0, ctx)
     def _(n):
@@ -801,27 +819,26 @@
         remote(ggs.at[other], ggr.at[me], gg_s.at[n], gg_r.at[n], dev).start()
     line.step(2)
     outs.fold(0)
-    half_wide = ff
-
-    @pl.loop(0, 2 * ctx)
-    def _(n):
-        slot = lax.rem(n, 2)
-        rows = lanes(lax.div(n, 2) * tall, tall)
-        cols = lanes(slot * half_wide, half_wide)
-        tile = pgt.at[slot]
-        to = pltpu.make_async_copy(tile, gwin_h.at[rows, cols], load_sem.at[slot])
-
-        @pl.when(n >= 2)
-        def _():
-            to.wait()
-
-        tile[...] = dot_tn(xs[:, rows], igs[:, cols]).astype(BF16)
-        to.start()
-
-    for slot in range(2):
-        pltpu.make_async_copy(pgt.at[slot], gwin_h.at[pl.ds(0, tall), pl.ds(0, half_wide)], load_sem.at[slot]).wait()
+
+    def gate_up(at, size):
+        @pl.loop(0, ctx)
+        def _(n):
+            tile = dot_tn(xs[:, lanes(n * tall, tall)], igs[:, pl.ds(at, size)]).astype(BF16)
+            win[n, :, :, pl.ds(at, size)] = tile.reshape(gwdn.shape[1], gwdn.shape[2], size)
+
+    gate_up(0, some)
+    rest = 2 * ff - some
+    gate_up(some, rest // 2)
+    gate_up(some + rest // 2, rest // 2)
+    gwin_copy = pltpu.make_async_copy(win.at[:, :, :, pl.ds(some, rest)], gwin_h, load_sem.at[0])
+    gwin_copy.start()
     line.step(3)
+    first_line.step(1)
     outs.turn()
+    first_line.step(2)
+    line.final()
+    for rows, terms in outs.total():
+        output[rows, :] = (pg_out[rows, :] + summed(terms)).astype(BF16)
     for rows, terms in plane.total():
         pg_out[rows, :] = summed(terms)
     for n in range(planes - 1):
@@ -829,24 +846,26 @@
         remote(ggr.at[source], ggr.at[source], gg_s.at[n], gg_r.at[n], kp).wait_recv()
     for p in range(planes):
         gg_out[p : p + 1, :] = ggr[p, 0:1, :]
-    line.final()
-    for rows, terms in outs.total():
-        output[rows, :] = (resid[rows, :] + summed(terms)).astype(BF16)
+    first_line.step(3)
+    first_line.final()
+    gwin_copy.wait()
     for n, (other, dev) in enumerate(others):
         remote(meta.at[other], metas.at[other], me_s.at[n], me_r.at[n], dev).wait_send()
         remote(ggs.at[other], ggr.at[other], gg_s.at[n], gg_r.at[n], dev).wait_send()
     plane.done()
     outs.done()
     line.done(ex_out)
-
-
-def run_ffn(cap, ffn, resid, cot_all, meta, win, wdn, parts):
+    first_line.done(first_out)
+
+
+def run_ffn(cap, ffn, resid, cot_all, meta, win, wdn, parts, some):
     tok, width = ffn.shape
     ff = wdn.shape[2]
     planes = cot_all.shape[0]
     ctx = win.shape[0]
     rows = planes * cap
     piece = width // (ctx * parts)
+    win = win.reshape(ctx, ctx, parts, piece, 2 * ff)
     vm, anyspace = pl.BlockSpec(memory_space=pltpu.VMEM), pl.BlockSpec(memory_space=pl.ANY)
     shape = jax.ShapeDtypeStruct
     dma = pltpu.SemaphoreType.DMA
@@ -856,16 +875,17 @@
             shape((tok, width), BF16),
             shape((tok, width), F32),
             shape((planes, tok), F32),
-            shape((width, 2 * ff), BF16),
+            shape((ctx, parts, piece, 2 * ff - some), BF16),
             shape((ctx, piece, ff), BF16),
+            shape((ctx, piece, some), BF16),
         ),
-        in_specs=[vm, vm, anyspace, vm, anyspace, anyspace],
-        out_specs=(vm, vm, vm, anyspace, vm),
+        in_specs=[anyspace, anyspace, anyspace, vm, anyspace, anyspace],
+        out_specs=(vm, vm, vm, anyspace, vm, vm),
         scratch_shapes=[
             pltpu.VMEM((planes, tok, width), BF16),
             pltpu.VMEM((planes, 8, tok), F32),
             pltpu.VMEM((planes, tok, width), BF16),
-            pltpu.VMEM((width, 2 * ff), BF16),
+            pltpu.VMEM((ctx, parts, piece, 2 * ff), BF16),
             pltpu.VMEM((width, ff), BF16),
             pltpu.VMEM((rows, width), BF16),
             pltpu.VMEM((rows, width), BF16),
@@ -876,8 +896,7 @@
             pltpu.VMEM((planes, 8, tok), F32),
             pltpu.VMEM((2 * ff, width), BF16),
             pltpu.VMEM((ctx, parts, piece, ff), BF16),
-            pltpu.VMEM((2, width // ctx, ff), BF16),
-            dma((3,)),
+            dma((5,)),
             dma((GATHER_COPIES,)),
             dma((GATHER_COPIES,)),
             dma((planes - 1,)),
@@ -888,7 +907,8 @@
             dma((10,)),
         ]
         + plane_scratch(tok, width)
-        + expert_scratch(ctx, parts, piece, ff),
+        + expert_scratch(ctx, parts, piece, ff)
+        + expert_scratch(ctx, parts, piece, some),
         compiler_params=pltpu.CompilerParams(
             collective_id=1, has_side_effects=True, vmem_limit_bytes=63 * 2**20
         ),
@@ -958,9 +978,9 @@
     greet([spot.xp, spot.yp, spot.kp, spot.yk], spot.along())
     one = ExpertLine(spot, gwin, 0, cols, *one_refs)
     two = ExpertLine(spot, gwin, cols, cols, *two_refs)
-    proj_plane = plane_of(spot, p_zcr, p_zk, p_rx, p_ry, p_s, p_r)
-    qkv_plane = plane_of(spot, p_zcr, p_zk, a_rx, a_ry, a_s, a_r)
-    rest_plane = plane_of(spot, *b_refs)
+    proj_plane = plane_of(spot, p_zcr, p_zk, p_rx, p_ry, p_s, p_r, low=BACK_LOW)
+    qkv_plane = plane_of(spot, p_zcr, p_zk, a_rx, a_ry, a_s, a_r, low=BACK_LOW)
+    rest_plane = plane_of(spot, *b_refs, low=BACK_LOW)
 
     def shared_line(ref, refs):
         def own(d):
@@ -1125,7 +1145,6 @@
         send[q] = dot_tn(normed[:, at], mixed[:, :width]).astype(BF16)
         qkv_plane.give(q, send.at[q, theirs])
     start_plane(qkv_plane)
-    one.final()
     proj_line.step(2)
     wqkv_load.wait()
 
@@ -1134,6 +1153,7 @@
         at = lanes(n * step, step)
         wide_f[:, at] = dot_nt(mixed[...], weights[at, :])
 
+    two.step(2)
     hidden_load.wait()
     x = low[...].astype(F32)
     inv = lax.rsqrt(jnp.mean(x * x, axis=-1, keepdims=True) + NORM_EPS)
@@ -1158,9 +1178,10 @@
     rest_plane.fold(3, bsend[3, mine])
     rest_plane.across()
     rest_plane.fold(0, bsend[0, mine])
-    two.step(2)
     qkv_plane.turn()
     rest_plane.turn()
+    two.step(3)
+    one.final()
     proj_line.step(3)
     for rows, terms in qkv_plane.total():
         total[rows, :width] = summed(terms).astype(BF16)
@@ -1168,7 +1189,6 @@
         total[rows, width:] = summed(terms).astype(BF16)
     qkv_line.step(1)
     one.done(one_out)
-    two.step(3)
     qkv_line.step(2)
     proj_line.final(lambda *came: put_shared(proj_out, out_red, came))
     qkv_line.step(3)
@@ -1236,9 +1256,9 @@
             dma((KV_HEADS, 3)),
             dma((KV_HEADS, 3)),
         ]
-        + plane_scratch(block, width)
-        + plane_scratch(block, width)[2:]
-        + plane_scratch(block, rest)
+        + plane_scratch(block, width, BACK_LOW)
+        + plane_scratch(block, width, BACK_LOW)[2:]
+        + plane_scratch(block, rest, BACK_LOW)
         + line_scratch(parts, (piece, width + rest))
         + line_scratch(parts, (piece, width))
         + expert_scratch(ctx, parts, rows, cols)
@@ -1254,18 +1274,68 @@
 
 
 def finish_kernel(
-    n_experts, output_low, input_low, qkv_low, proj_low, one, two, down_low, output, input_grad, gains, qkv, proj, router, inner, down
+    n_experts,
+    output_h,
+    input_h,
+    qkv_h,
+    proj_h,
+    first_h,
+    one_h,
+    two_h,
+    down_h,
+    output,
+    input_grad,
+    gains,
+    qkv,
+    proj,
+    router,
+    inner,
+    down,
+    low_qkv,
+    low_proj,
+    low_first,
+    low_one,
+    low_two,
+    low_down,
+    inner_full,
+    down_full,
+    sem,
+    out_sem,
 ):
-    output[...] = output_low[...]
-    input_grad[...] = input_low[...]
+    whole = [pltpu.make_async_copy(output_h, output, out_sem.at[0]), pltpu.make_async_copy(input_h, input_grad, out_sem.at[1])]
+    loads = [
+        pltpu.make_async_copy(src, dst, sem.at[i])
+        for i, (src, dst) in enumerate(
+            (
+                (down_h, low_down),
+                (first_h, low_first),
+                (one_h, low_one),
+                (two_h, low_two),
+                (qkv_h, low_qkv),
+                (proj_h, low_proj),
+            )
+        )
+    ]
+    for copy in loads + whole:
+        copy.start()
+    loads[0].wait()
+    down_full[...] = low_down[...].astype(F32)
+    whole.append(pltpu.make_async_copy(down_full, down, out_sem.at[2]))
+    whole[-1].start()
+    at = 0
+    for load, low in zip(loads[1:4], (low_first, low_one, low_two)):
+        load.wait()
+        size = low.shape[2]
+        inner_full[:, :, at : at + size] = low[...].astype(F32)
+        at += size
+    whole.append(pltpu.make_async_copy(inner_full, inner, out_sem.at[3]))
+    whole[-1].start()
+    for load in loads[4:]:
+        load.wait()
     wide = qkv.shape[1]
-    qkv[...] = qkv_low[:, :wide].astype(F32)
-    proj[...] = proj_low[...].astype(F32)
-    ff = one.shape[2]
-    inner[:, :, :ff] = one[...].astype(F32)
-    inner[:, :, ff:] = two[...].astype(F32)
-    down[...] = down_low[...].astype(F32)
-    small = qkv_low[:, wide:].astype(F32)
+    qkv[...] = low_qkv[:, :wide].astype(F32)
+    proj[...] = low_proj[...].astype(F32)
+    small = low_qkv[:, wide:].astype(F32)
     router[...] = small[:, :n_experts]
     piece = small.shape[0]
     same = lax.broadcasted_iota(jnp.int32, (piece, piece), 0) == lax.broadcasted_iota(
@@ -1273,13 +1343,15 @@
     )
     for row, col in ((0, HEAD - 1), (1, n_experts)):
         gains[row : row + 1, :] = jnp.sum(jnp.where(same, small[:, col : col + 1], 0.0), axis=0, keepdims=True)
-
-
-def run_finish(n_experts, output, input_grad, qkv, proj, one, two, down):
+    for copy in whole:
+        copy.wait()
+
+
+def run_finish(n_experts, output, input_grad, qkv, proj, first, one, two, down):
     piece, width = proj.shape
-    ctx, rows, ff = one.shape
+    ctx, rows, ff = down.shape
     shape = jax.ShapeDtypeStruct
-    vm = pl.BlockSpec(memory_space=pltpu.VMEM)
+    vm, anyspace = pl.BlockSpec(memory_space=pltpu.VMEM), pl.BlockSpec(memory_space=pl.ANY)
     return pl.pallas_call(
         functools.partial(finish_kernel, n_experts),
         out_shape=(
@@ -1292,10 +1364,17 @@
             shape((ctx, rows, 2 * ff), F32),
             shape((ctx, rows, ff), F32),
         ),
-        in_specs=[vm] * 7,
-        out_specs=(vm,) * 8,
-        compiler_params=pltpu.CompilerParams(vmem_limit_bytes=40 * 2**20),
-    )(output, input_grad, qkv, proj, one, two, down)
+        in_specs=[anyspace] * 8,
+        out_specs=(anyspace, anyspace, vm, vm, vm, vm, anyspace, anyspace),
+        scratch_shapes=[pltpu.VMEM(x.shape, BF16) for x in (qkv, proj, first, one, two, down)]
+        + [
+            pltpu.VMEM((ctx, rows, 2 * ff), F32),
+            pltpu.VMEM((ctx, rows, ff), F32),
+            pltpu.SemaphoreType.DMA((6,)),
+            pltpu.SemaphoreType.DMA((4,)),
+        ],
+        compiler_params=pltpu.CompilerParams(vmem_limit_bytes=56 * 2**20),
+    )(output, input_grad, qkv, proj, first, one, two, down)
 
 
 def local(
@@ -1339,10 +1418,9 @@
         ctx,
         planes,
     )
-    output, pair_sum, gate_grad, gwin, down = run_ffn(
-        capacity, ffn_in, resid, cot_all, meta, in_weight, down_weight, parts
-    )
-    gwin = gwin.reshape(ctx, parts, width // (ctx * parts), 2 * ff)
+    output, pair_sum, gate_grad, gwin, down, in_first = run_ffn(
+        capacity, ffn_in, resid, cot_all, meta, in_weight, down_weight, parts, ff // 3
+    )
     input_grad, qkv_sum, proj_sum, in_one, in_two = run_back(
         span_order,
         meta,
@@ -1366,7 +1444,7 @@
         gwin,
     )
     output, input_grad, gains, qkv_grad, proj_grad, router_grad, inner_grad, down_grad = run_finish(
-        n_experts, output, input_grad, qkv_sum, proj_sum, in_one, in_two, down
+        n_experts, output, input_grad, qkv_sum, proj_sum, in_first, in_one, in_two, down
     )
     return (
         output[None],

time: 276 us -> 314 us (1.14)
  Pallas kernels: 263 us -> 306 us
  local copies, waits for them, and re-layouts: 7.34 us -> 2.67 us
    pallas_call x1, Pallas kernels: 2.59 us -> 49.7 us  [run_finish(): pl.pallas_call(functools.partial(finish_kernel, n_experts), out_shape=(sh...]
    pallas_call x1, Pallas kernels: 112 us -> 100 us  [run_back(): pl.pallas_call(back_kernel, out_shape=(shape((tok, width), BF16), shape((...]
    pallas_call x1, Pallas kernels: 104 us -> 113 us  [run_ffn(): pl.pallas_call(functools.partial(ffn_kernel, cap), out_shape=(shape((tok,...]
    unnamed x15 -> x1, local copies, waits for them, and re-layouts: 6.82 us -> 1.4 us
where the time goes in v6:
time: 314 us; the launch traced here: 309 us
  Pallas kernels  306 us (97%)
    pallas_call x1, Pallas kernels, run_ffn(): pl.pallas_call(functools.partial(ffn_kernel, cap), out_shape=(shape((tok,...  113 us
    pallas_call x1, Pallas kernels, run_back(): pl.pallas_call(back_kernel, out_shape=(shape((tok, width), BF16), shape((...  100 us
    pallas_call x1, Pallas kernels, run_finish(): pl.pallas_call(functools.partial(finish_kernel, n_experts), out_shape=(sh...  49.7 us
    pallas_call x1, Pallas kernels, run_front(): pl.pallas_call(functools.partial(front_kernel, cap), out_shape=(shape((to...  42.4 us

profile of v6, /device:TPU:0, one launch (start us, length us, event | category | flops | bytes accessed | tf_op | source)
XLA Modules:
  0.0 309.1 jit_solution(3004208945824259183)
XLA Ops:
  0.6 42.4 %shard_map.196 = (bf16[256,1536]{1,0:T(8,128)(2,1)}, bf16[256,1536]{1,0:T(8,128)(2,1)}, bf16[1024,512]{1,0:T(8,128)(2,1)}, f32[16,256]{1,0:T(8,128)}, bf16[256,1...) custom-call(s32[1,8]{1,0:T(1,128)} %span.3, ...), custom_call_target="tpu_custom_call" | custom-call | flops 5000000000 | bytes 20000000 | tf_op jit(solution)/shard_map/pallas_call | solution.py:615
  43.0 113.4 %shard_map.197 = (bf16[256,1536]{1,0:T(8,128)(2,1)}, f32[256,1536]{1,0:T(8,128)}, f32[8,256]{1,0:T(8,128)}, bf16[4,4,96,1280]{3,2,1,0:T(8,128)(2,1)}, bf16[4,96,...) custom-call(bf16[256,1536]{1,0:T(8,128)(2,1)} %get-tuple-element.38.ffn_h.ffn_in_h, ...), custom_call_target="tpu_custom_call" | custom-call | flops 24999999488 | bytes 50000000 | tf_op jit(solution)/shard_map/pallas_call | solution.py:872
  156.4 100.1 %shard_map.198 = (bf16[256,1536]{1,0:T(8,128)(2,1)}, bf16[48,2176]{1,0:T(8,128)(2,1)}, bf16[48,1536]{1,0:T(8,128)(2,1)}, bf16[4,96,640]{2,1,0:T(8,128)(2,1)}, bf16[4,96,640]{2,1,0:T(8,128)(2,1)}) custom-call(s32[1,8]{1,0:T(1,128)} %span.3, f32[8,8,256]{2,1,0:T(8,128)} %get-tuple-element.41.meta, f32[8,256]{1,0:T(8,128)} %get-tuple-element.43.gg, ...), custom_call_target="tpu_custom_call" | custom-call | flops 12000000000 | bytes 60000000 | tf_op jit(solution)/shard_map/pallas_call | solution.py:1224
  256.5 49.7 %shard_map.199 = (bf16[256,1536]{1,0:T(8,128)(2,1)}, bf16[256,1536]{1,0:T(8,128)(2,1)}, f32[2,48]{1,0:T(2,128)}, f32[48,2048]{1,0:T(8,128)}, f32[48,1536]{1,0:T(...) custom-call(bf16[256,1536]{1,0:T(8,128)(2,1)} %get-tuple-element.42.output_h, ...), custom_call_target="tpu_custom_call" | custom-call | tf_op jit(solution)/shard_map/pallas_call | solution.py:1355
  306.2 1.3 slice_bitcast_fusion
  307.5 1.4 copy.22

commit v7 on v6

--- a/solution.py
+++ b/solution.py
@@ -1297,12 +1297,14 @@
     low_one,
     low_two,
     low_down,
+    low_out,
+    low_in,
     inner_full,
     down_full,
     sem,
     out_sem,
 ):
-    whole = [pltpu.make_async_copy(output_h, output, out_sem.at[0]), pltpu.make_async_copy(input_h, input_grad, out_sem.at[1])]
+    whole = []
     loads = [
         pltpu.make_async_copy(src, dst, sem.at[i])
         for i, (src, dst) in enumerate(
@@ -1313,10 +1315,12 @@
                 (two_h, low_two),
                 (qkv_h, low_qkv),
                 (proj_h, low_proj),
+                (output_h, low_out),
+                (input_h, low_in),
             )
         )
     ]
-    for copy in loads + whole:
+    for copy in loads:
         copy.start()
     loads[0].wait()
     down_full[...] = low_down[...].astype(F32)
@@ -1330,7 +1334,11 @@
         at += size
     whole.append(pltpu.make_async_copy(inner_full, inner, out_sem.at[3]))
     whole[-1].start()
-    for load in loads[4:]:
+    for i, (low, to) in enumerate(((low_out, output), (low_in, input_grad))):
+        loads[6 + i].wait()
+        whole.append(pltpu.make_async_copy(low, to, out_sem.at[i]))
+        whole[-1].start()
+    for load in loads[4:6]:
         load.wait()
     wide = qkv.shape[1]
     qkv[...] = low_qkv[:, :wide].astype(F32)
@@ -1366,11 +1374,11 @@
         ),
         in_specs=[anyspace] * 8,
         out_specs=(anyspace, anyspace, vm, vm, vm, vm, anyspace, anyspace),
-        scratch_shapes=[pltpu.VMEM(x.shape, BF16) for x in (qkv, proj, first, one, two, down)]
+        scratch_shapes=[pltpu.VMEM(x.shape, BF16) for x in (qkv, proj, first, one, two, down, output, input_grad)]
         + [
             pltpu.VMEM((ctx, rows, 2 * ff), F32),
             pltpu.VMEM((ctx, rows, ff), F32),
-            pltpu.SemaphoreType.DMA((6,)),
+            pltpu.SemaphoreType.DMA((8,)),
             pltpu.SemaphoreType.DMA((4,)),
         ],
         compiler_params=pltpu.CompilerParams(vmem_limit_bytes=56 * 2**20),

time: 314 us -> 269 us (0.86)
  Pallas kernels: 306 us -> 260 us
    pallas_call x1, Pallas kernels: 49.7 us -> 4.4 us  [run_finish(): pl.pallas_call(functools.partial(finish_kernel, n_experts), out_shape=(sh...]
where the time goes in v7:
time: 269 us; the launch traced here: 264 us
  Pallas kernels  260 us (97%)
    pallas_call x1, Pallas kernels, run_ffn(): pl.pallas_call(functools.partial(ffn_kernel, cap), out_shape=(shape((tok,...  113 us
    pallas_call x1, Pallas kernels, run_back(): pl.pallas_call(back_kernel, out_shape=(shape((tok, width), BF16), shape((...  100 us
    pallas_call x1, Pallas kernels, run_front(): pl.pallas_call(functools.partial(front_kernel, cap), out_shape=(shape((to...  42.4 us

profile of v7, /device:TPU:0, one launch (start us, length us, event | category | flops | bytes accessed | tf_op | source)
XLA Modules:
  0.0 263.8 jit_solution(5077157653219825943)
XLA Ops:
  0.6 42.4 %shard_map.196 = (bf16[256,1536]{1,0:T(8,128)(2,1)}, bf16[256,1536]{1,0:T(8,128)(2,1)}, bf16[1024,512]{1,0:T(8,128)(2,1)}, f32[16,256]{1,0:T(8,128)}, bf16[256,1...) custom-call(s32[1,8]{1,0:T(1,128)} %span.3, ...), custom_call_target="tpu_custom_call" | custom-call | flops 5000000000 | bytes 20000000 | tf_op jit(solution)/shard_map/pallas_call | solution.py:615
  43.0 113.4 %shard_map.197 = (bf16[256,1536]{1,0:T(8,128)(2,1)}, f32[256,1536]{1,0:T(8,128)}, f32[8,256]{1,0:T(8,128)}, bf16[4,4,96,1280]{3,2,1,0:T(8,128)(2,1)}, bf16[4,96,...) custom-call(bf16[256,1536]{1,0:T(8,128)(2,1)} %get-tuple-element.38.ffn_h.ffn_in_h, ...), custom_call_target="tpu_custom_call" | custom-call | flops 24999999488 | bytes 50000000 | tf_op jit(solution)/shard_map/pallas_call | solution.py:872
  156.4 100.1 %shard_map.198 = (bf16[256,1536]{1,0:T(8,128)(2,1)}, bf16[48,2176]{1,0:T(8,128)(2,1)}, bf16[48,1536]{1,0:T(8,128)(2,1)}, bf16[4,96,640]{2,1,0:T(8,128)(2,1)}, bf16[4,96,640]{2,1,0:T(8,128)(2,1)}) custom-call(s32[1,8]{1,0:T(1,128)} %span.3, f32[8,8,256]{2,1,0:T(8,128)} %get-tuple-element.41.meta, f32[8,256]{1,0:T(8,128)} %get-tuple-element.43.gg, ...), custom_call_target="tpu_custom_call" | custom-call | flops 12000000000 | bytes 60000000 | tf_op jit(solution)/shard_map/pallas_call | solution.py:1224
  256.5 4.4 %shard_map.199 = (bf16[256,1536]{1,0:T(8,128)(2,1)}, bf16[256,1536]{1,0:T(8,128)(2,1)}, f32[2,48]{1,0:T(2,128)}, f32[48,2048]{1,0:T(8,128)}, f32[48,1536]{1,0:T(...) custom-call(bf16[256,1536]{1,0:T(8,128)(2,1)} %get-tuple-element.42.output_h, ...), custom_call_target="tpu_custom_call" | custom-call | tf_op jit(solution)/shard_map/pallas_call | solution.py:1363
  260.9 1.3 slice_bitcast_fusion
  262.2 1.4 copy.22

commit v8 on v7

--- a/solution.py
+++ b/solution.py
@@ -827,13 +827,13 @@
             win[n, :, :, pl.ds(at, size)] = tile.reshape(gwdn.shape[1], gwdn.shape[2], size)
 
     gate_up(0, some)
+    first_line.step(1)
     rest = 2 * ff - some
     gate_up(some, rest // 2)
     gate_up(some + rest // 2, rest // 2)
     gwin_copy = pltpu.make_async_copy(win.at[:, :, :, pl.ds(some, rest)], gwin_h, load_sem.at[0])
     gwin_copy.start()
     line.step(3)
-    first_line.step(1)
     outs.turn()
     first_line.step(2)
     line.final()
@@ -949,8 +949,9 @@
     load_sem, kv_s, kv_r = scratch[19:22]
     p_zcr, p_zk, p_rx, p_ry, p_s, p_r = scratch[22:28]
     a_rx, a_ry, a_s, a_r = scratch[28:32]
-    b_refs, qkv_refs, proj_refs = scratch[32:38], scratch[38:41], scratch[41:44]
-    one_refs, two_refs = scratch[44:51], scratch[51:58]
+    e_refs, b_refs = scratch[32:38], scratch[38:44]
+    qkv_refs, proj_refs = scratch[44:47], scratch[47:50]
+    one_refs, two_refs = scratch[50:57], scratch[57:64]
     spot = Spot()
     c, k, z, ctx = spot.c, spot.k, spot.z, spot.ctx
     tok, width = attended.shape
@@ -979,7 +980,12 @@
     one = ExpertLine(spot, gwin, 0, cols, *one_refs)
     two = ExpertLine(spot, gwin, cols, cols, *two_refs)
     proj_plane = plane_of(spot, p_zcr, p_zk, p_rx, p_ry, p_s, p_r, low=BACK_LOW)
-    qkv_plane = plane_of(spot, p_zcr, p_zk, a_rx, a_ry, a_s, a_r, low=BACK_LOW)
+    half_wide = width // 2
+    cut = pl.ds(0, half_wide)
+    early_plane = plane_of(spot, *e_refs, low=BACK_LOW)
+    late_plane = plane_of(
+        spot, p_zcr.at[:, :, cut], p_zk.at[:, :, cut], a_rx, a_ry, a_s, a_r, low=BACK_LOW
+    )
     rest_plane = plane_of(spot, *b_refs, low=BACK_LOW)
 
     def shared_line(ref, refs):
@@ -1023,7 +1029,7 @@
     gain_col = jnp.broadcast_to(gain_row, (HEAD, width)).T
     smalls[...] = jnp.where(lane == n_experts, gain_col, routed).astype(BF16)
 
-    for q in (1, 2, 3, 0):
+    for q in (3, 1, 2, 0):
         at = lanes(spot.chips[q] * block, 2 * block)
         send[q] = dot_tn(low[:, at], attended[...]).astype(BF16)
         proj_plane.give(q, send.at[q, theirs])
@@ -1037,15 +1043,21 @@
     wqkv_load = load(wqkv_h, weights, 5)
     hidden_load = load(hidden_h, low, 1)
 
-    def start_plane(plane):
-        plane.fold(1, send[1, mine])
-        plane.fold(2, send[2, mine])
+    def start_plane(plane, at):
+        plane.fold(3, send[3, mine, at])
+        plane.across()
+        plane.fold(1, send[1, mine, at])
+        plane.fold(2, send[2, mine, at])
         plane.near()
-        plane.fold(3, send[3, mine])
-        plane.across()
-        plane.fold(0, send[0, mine])
-
-    start_plane(proj_plane)
+        plane.fold(0, send[0, mine, at])
+
+    def qkv_tiles(plane, at):
+        for q in (3, 1, 2, 0):
+            rows = lanes(spot.chips[q] * block, 2 * block)
+            send[q, :, at] = dot_tn(normed[:, rows], mixed[:, at]).astype(BF16)
+            plane.give(q, send.at[q, theirs, at])
+
+    start_plane(proj_plane, pl.ds(0, width))
 
     seq = kv.shape[0]
     spans = span.shape[1]
@@ -1120,13 +1132,18 @@
     send_kv(0)
     clear()
     proj_plane.turn()
-    heads(1, 6, 3)
+    proj_plane.given()
+    qkv_tiles(early_plane, pl.ds(0, half_wide))
+    heads(1, 6, 1)
+    start_plane(early_plane, pl.ds(0, half_wide))
     pass_kv(0)
     one.step(3)
     two.step(1)
+    heads(1, 7, 2)
     heads(1, 9, 3)
     send_kv(1)
     pass_kv(1)
+    early_plane.turn()
     for rows, terms in proj_plane.total():
         out_red[rows, :] = summed(terms).astype(BF16)
     proj_line.step(1)
@@ -1140,11 +1157,8 @@
         at = width + (heads_kv + g) * HEAD
         mixed[:, at : at + HEAD] = own[:, HEAD:].astype(BF16)
 
-    for q in (1, 2, 3, 0):
-        at = lanes(spot.chips[q] * block, 2 * block)
-        send[q] = dot_tn(normed[:, at], mixed[:, :width]).astype(BF16)
-        qkv_plane.give(q, send.at[q, theirs])
-    start_plane(qkv_plane)
+    qkv_tiles(late_plane, pl.ds(half_wide, half_wide))
+    start_plane(late_plane, pl.ds(half_wide, half_wide))
     proj_line.step(2)
     wqkv_load.wait()
 
@@ -1167,34 +1181,37 @@
     lane = lax.broadcasted_iota(jnp.int32, (width, HEAD), 1)
     gain_col = jnp.broadcast_to(gain_row, (HEAD, width)).T
     smalls[...] = jnp.where(lane == HEAD - 1, gain_col, smalls[...].astype(F32)).astype(BF16)
-    for q in (1, 2, 3, 0):
+    for q in (3, 1, 2, 0):
         at = lanes(spot.chips[q] * block, 2 * block)
         bsend[q, :, :kv_wide] = dot_tn(normed[:, at], mixed[:, width:]).astype(BF16)
         bsend[q, :, kv_wide:] = smalls[rows_at(spot.chips[q] * block, 2 * block), :]
         rest_plane.give(q, bsend.at[q, theirs])
+    rest_plane.fold(3, bsend[3, mine])
+    rest_plane.across()
     rest_plane.fold(1, bsend[1, mine])
     rest_plane.fold(2, bsend[2, mine])
     rest_plane.near()
-    rest_plane.fold(3, bsend[3, mine])
-    rest_plane.across()
     rest_plane.fold(0, bsend[0, mine])
-    qkv_plane.turn()
+    late_plane.turn()
     rest_plane.turn()
     two.step(3)
     one.final()
     proj_line.step(3)
-    for rows, terms in qkv_plane.total():
-        total[rows, :width] = summed(terms).astype(BF16)
+    for rows, terms in early_plane.total():
+        total[rows, :half_wide] = summed(terms).astype(BF16)
+    for rows, terms in late_plane.total():
+        total[rows, half_wide:width] = summed(terms).astype(BF16)
     for rows, terms in rest_plane.total():
         total[rows, width:] = summed(terms).astype(BF16)
     qkv_line.step(1)
     one.done(one_out)
     qkv_line.step(2)
+    two.final()
     proj_line.final(lambda *came: put_shared(proj_out, out_red, came))
     qkv_line.step(3)
-    two.final()
     proj_line.done()
-    qkv_plane.done()
+    early_plane.done()
+    late_plane.done()
     rest_plane.done()
     for g in range(heads_kv):
         kv_copy(g, kvs.at[g, near_c], 0, spot.kp).wait_send()
@@ -1257,7 +1274,8 @@
             dma((KV_HEADS, 3)),
         ]
         + plane_scratch(block, width, BACK_LOW)
-        + plane_scratch(block, width, BACK_LOW)[2:]
+        + plane_scratch(block, width // 2, BACK_LOW)[2:]
+        + plane_scratch(block, width // 2, BACK_LOW)
         + plane_scratch(block, rest, BACK_LOW)
         + line_scratch(parts, (piece, width + rest))
         + line_scratch(parts, (piece, width))
@@ -1285,7 +1303,8 @@
     down_h,
     output,
     input_grad,
-    gains,
+    gain_one,
+    gain_two,
     qkv,
     proj,
     router,
@@ -1344,13 +1363,18 @@
     qkv[...] = low_qkv[:, :wide].astype(F32)
     proj[...] = low_proj[...].astype(F32)
     small = low_qkv[:, wide:].astype(F32)
-    router[...] = small[:, :n_experts]
     piece = small.shape[0]
     same = lax.broadcasted_iota(jnp.int32, (piece, piece), 0) == lax.broadcasted_iota(
         jnp.int32, (piece, piece), 1
     )
-    for row, col in ((0, HEAD - 1), (1, n_experts)):
-        gains[row : row + 1, :] = jnp.sum(jnp.where(same, small[:, col : col + 1], 0.0), axis=0, keepdims=True)
+
+    def column(at):
+        return jnp.sum(jnp.where(same, small[:, at : at + 1], 0.0), axis=0, keepdims=True)
+
+    gain_one[...] = column(HEAD - 1)[0]
+    gain_two[...] = column(n_experts)[0]
+    for at in range(n_experts):
+        router[at : at + 1, :] = column(at)
     for copy in whole:
         copy.wait()
 
@@ -1365,15 +1389,16 @@
         out_shape=(
             shape(output.shape, BF16),
             shape(input_grad.shape, BF16),
-            shape((2, piece), F32),
+            shape((piece,), F32),
+            shape((piece,), F32),
             shape((piece, qkv.shape[1] - HEAD), F32),
             shape((piece, width), F32),
-            shape((piece, n_experts), F32),
+            shape((n_experts, piece), F32),
             shape((ctx, rows, 2 * ff), F32),
             shape((ctx, rows, ff), F32),
         ),
         in_specs=[anyspace] * 8,
-        out_specs=(anyspace, anyspace, vm, vm, vm, vm, anyspace, anyspace),
+        out_specs=(anyspace, anyspace, vm, vm, vm, vm, vm, anyspace, anyspace),
         scratch_shapes=[pltpu.VMEM(x.shape, BF16) for x in (qkv, proj, first, one, two, down, output, input_grad)]
         + [
             pltpu.VMEM((ctx, rows, 2 * ff), F32),
@@ -1451,17 +1476,17 @@
         qkv_weight,
         gwin,
     )
-    output, input_grad, gains, qkv_grad, proj_grad, router_grad, inner_grad, down_grad = run_finish(
+    output, input_grad, gain_one, gain_two, qkv_grad, proj_grad, router_grad, inner_grad, down_grad = run_finish(
         n_experts, output, input_grad, qkv_sum, proj_sum, in_first, in_one, in_two, down
     )
     return (
         output[None],
         input_grad[None],
-        gains[0],
+        gain_one,
         qkv_grad,
         proj_grad,
-        gains[1],
-        router_grad,
+        gain_two,
+        router_grad.T,
         inner_grad,
         down_grad,
     )

time: 269 us -> 261 us (0.970)
  Pallas kernels: 260 us -> 255 us
where the time goes in v8:
time: 261 us; the launch traced here: 256 us
  Pallas kernels  255 us (98%)
    pallas_call x1, Pallas kernels, run_ffn(): pl.pallas_call(functools.partial(ffn_kernel, cap), out_shape=(shape((tok,...  111 us
    pallas_call x1, Pallas kernels, run_back(): pl.pallas_call(back_kernel, out_shape=(shape((tok, width), BF16), shape((...  97.6 us
    pallas_call x1, Pallas kernels, run_front(): pl.pallas_call(functools.partial(front_kernel, cap), out_shape=(shape((to...  42.3 us

profile of v8, /device:TPU:0, one launch (start us, length us, event | category | flops | bytes accessed | tf_op | source)
XLA Modules:
  0.0 255.9 jit_solution(1619983342847133478)
XLA Ops:
  0.6 42.3 %shard_map.196 = (bf16[256,1536]{1,0:T(8,128)(2,1)}, bf16[256,1536]{1,0:T(8,128)(2,1)}, bf16[1024,512]{1,0:T(8,128)(2,1)}, f32[16,256]{1,0:T(8,128)}, bf16[256,1...) custom-call(s32[1,8]{1,0:T(1,128)} %span.3, ...), custom_call_target="tpu_custom_call" | custom-call | flops 5000000000 | bytes 20000000 | tf_op jit(solution)/shard_map/pallas_call | solution.py:615
  42.9 110.7 %shard_map.197 = (bf16[256,1536]{1,0:T(8,128)(2,1)}, f32[256,1536]{1,0:T(8,128)}, f32[8,256]{1,0:T(8,128)}, bf16[4,4,96,1280]{3,2,1,0:T(8,128)(2,1)}, bf16[4,96,...) custom-call(bf16[256,1536]{1,0:T(8,128)(2,1)} %get-tuple-element.39.ffn_h.ffn_in_h, ...), custom_call_target="tpu_custom_call" | custom-call | flops 24999999488 | bytes 50000000 | tf_op jit(solution)/shard_map/pallas_call | solution.py:872
  153.6 97.6 %shard_map.198 = (bf16[256,1536]{1,0:T(8,128)(2,1)}, bf16[48,2176]{1,0:T(8,128)(2,1)}, bf16[48,1536]{1,0:T(8,128)(2,1)}, bf16[4,96,640]{2,1,0:T(8,128)(2,1)}, bf16[4,96,640]{2,1,0:T(8,128)(2,1)}) custom-call(s32[1,8]{1,0:T(1,128)} %span.3, f32[8,8,256]{2,1,0:T(8,128)} %get-tuple-element.42.meta, f32[8,256]{1,0:T(8,128)} %get-tuple-element.44.gg, ...), custom_call_target="tpu_custom_call" | custom-call | flops 12000000000 | bytes 60000000 | tf_op jit(solution)/shard_map/pallas_call | solution.py:1241
  251.2 4.4 %shard_map.199 = (bf16[256,1536]{1,0:T(8,128)(2,1)}, bf16[256,1536]{1,0:T(8,128)(2,1)}, f32[48]{0:T(128)}, f32[48]{0:T(128)}, f32[48,2048]{1,0:T(8,128)}, /*inde...) custom-call(bf16[256,1536]{1,0:T(8,128)(2,1)} %get-tuple-element.43.output_h, ...), custom_call_target="tpu_custom_call" | custom-call | tf_op jit(solution)/shard_map/pallas_call | solution.py:1387

commit v9 on v8

--- a/solution.py
+++ b/solution.py
@@ -64,6 +64,7 @@
 BACK_LOW = 96
 OUT_LOW = 128
 FRONT_LOW = 96
+FRONT_AHEAD = 64
 
 
 def dot(a, b):
@@ -358,10 +359,11 @@
 
 
 class Gather:
-    def __init__(self, spot, own, buf, s, r, low=None):
+    def __init__(self, spot, own, buf, s, r, low=None, ahead=0):
         self.spot, self.own, self.buf, self.s, self.r = spot, own, buf, s, r
         low = low or own.shape[0] // 2
         self.lo, self.hi = pl.ds(0, low), pl.ds(low, own.shape[0] - low)
+        self.ahead, self.rest = ahead and pl.ds(low, ahead), pl.ds(low + ahead, own.shape[0] - low - ahead)
         self.x_me, self.y_me, self.d_me = (base + spot.k for base in spot.chips[1:])
         self.side = 1 - 2 * spot.k
         self.sent = []
@@ -381,13 +383,15 @@
     def start(self):
         me, own, lo, hi = self.spot.me, self.own, self.lo, self.hi
         self.push(own.at[lo], self.buf.at[me, lo], 0, self.spot.xp)
+        if self.ahead:
+            self.push(own.at[self.ahead], self.buf.at[me, self.ahead], 14, self.spot.yp)
         self.push(own.at[lo], self.buf.at[me, lo], 6, self.spot.kp)
         self.push(own.at[hi], self.buf.at[me, hi], 13, self.spot.kp)
         self.push(own.at[hi], self.buf.at[me, hi], 1, self.spot.xp)
 
     def start_y(self):
-        me, own, lo, hi = self.spot.me, self.own, self.lo, self.hi
-        self.push(own.at[hi], self.buf.at[me, hi], 3, self.spot.yp)
+        me, own, lo, rest = self.spot.me, self.own, self.lo, self.rest
+        self.push(own.at[rest], self.buf.at[me, rest], 3, self.spot.yp)
         self.push(own.at[lo], self.buf.at[me, lo], 2, self.spot.yp)
 
     def first(self):
@@ -395,7 +399,9 @@
         self.got(self.x_me, self.lo, 0)
         self.move(self.x_me, self.lo, 4, spot.yp)
         self.move(self.x_me, self.lo, 7, spot.kp)
-        self.got(self.y_me, self.hi, 3)
+        if self.ahead:
+            self.got(self.y_me, self.ahead, 14)
+        self.got(self.y_me, self.rest, 3)
         self.move(self.y_me, self.hi, 5, spot.xp)
         self.move(self.y_me, self.hi, 10, spot.kp)
 
@@ -422,7 +428,7 @@
             copy.wait_send()
 
 
-GATHER_COPIES = 14
+GATHER_COPIES = 15
 
 
 def front_kernel(
@@ -438,9 +444,9 @@
     turn_t,
     wqkv_h,
     wout_h,
-    normed,
-    queries,
-    kv,
+    normed_h,
+    queries_h,
+    kv_h,
     lse,
     attended,
     resid,
@@ -452,7 +458,11 @@
     wout,
     mask,
     vt,
+    normed,
+    queries,
+    kv,
     load_sem,
+    out_sem,
     kv_s,
     kv_r,
     co_s,
@@ -478,7 +488,7 @@
     for load in loads:
         load.start()
     greet([spot.xp, spot.yp, spot.kp])
-    gather = Gather(spot, cot, cot_all, co_s, co_r, low=FRONT_LOW)
+    gather = Gather(spot, cot, cot_all, co_s, co_r, low=FRONT_LOW, ahead=FRONT_AHEAD)
     gather.start()
 
     x = hidden[...].astype(F32)
@@ -517,6 +527,8 @@
         copy.start()
     gather.start_y()
 
+    outs = [pltpu.make_async_copy(normed, normed_h, out_sem.at[0])]
+    outs[0].start()
     loads[1].wait()
     step = 256
 
@@ -527,6 +539,9 @@
         for i in range(step // HEAD):
             w = raw[:, i * HEAD : (i + 1) * HEAD]
             queries[:, lanes(n * step + i * HEAD, HEAD)] = (rotate_in(w) * HEAD**-0.5).astype(BF16)
+
+    outs.append(pltpu.make_async_copy(queries, queries_h, out_sem.at[1]))
+    outs[1].start()
 
     flip = rows_at(flip_c * tok, tok)
     kv_copy(flip, 1, spot.kp).wait_recv()
@@ -555,6 +570,8 @@
     near, across = rows_at(near_c * tok, tok), rows_at(across_c * tok, tok)
     kv_copy(near, 0, spot.kp).wait_recv()
     kv_copy(across, 2, spot.kp).wait_recv()
+    outs.append(pltpu.make_async_copy(kv, kv_h, out_sem.at[2]))
+    outs[2].start()
     for g in range(KV_HEADS):
         vt[g] = kv[:, kv_cols + g * HEAD : kv_cols + (g + 1) * HEAD].astype(F32).T.astype(BF16)
     lse[...] = jnp.zeros(lse.shape, F32)
@@ -599,6 +616,8 @@
         gather.other_core(q)
     loads[3].wait()
     gather.done()
+    for copy in outs:
+        copy.wait()
     for copy in sent:
         copy.wait_send()
 
@@ -627,13 +646,17 @@
             shape((planes, tok, width), BF16),
         ),
         in_specs=[sm] + [vm] * 8 + [anyspace] * 2,
-        out_specs=(vm,) * 9 + (anyspace,),
+        out_specs=(anyspace,) * 3 + (vm,) * 6 + (anyspace,),
         scratch_shapes=[
             pltpu.VMEM(wqkv.shape, BF16),
             pltpu.VMEM(wout.shape, BF16),
             pltpu.VMEM((seq, tok), F32),
             pltpu.VMEM((KV_HEADS, HEAD, seq), BF16),
+            pltpu.VMEM((tok, width), BF16),
+            pltpu.VMEM((tok, width), BF16),
+            pltpu.VMEM((seq, kv_cols), BF16),
             dma((4,)),
+            dma((3,)),
             dma((3,)),
             dma((3,)),
             dma((GATHER_COPIES,)),
@@ -666,8 +689,6 @@
     ]
     own_load = pltpu.make_async_copy(ffn_h, agb.at[me], load_sem.at[4])
     own_load.start()
-    for load in loads:
-        load.start()
     others = spot.others()
     greet([dev for _, dev in others], spot.along())
     plane = plane_of(spot, *plane_refs)
@@ -692,6 +713,8 @@
     own_load.wait()
     gather.start()
     gather.start_y()
+    for load in loads:
+        load.start()
     metas[me] = meta[me]
     slot_rows = lax.broadcasted_iota(jnp.int32, (cap, tok), 0).astype(F32)
     step = 256
@@ -740,9 +763,7 @@
         plane.give(q, given)
         plane.zk[q][...] = dot_tn(spots(base + k).astype(BF16), pgs[mine, :]).astype(BF16)
 
-    for load in loads:
-        load.wait()
-
+    loads[0].wait()
     tall = width // ctx
 
     @pl.loop(0, ctx)
@@ -752,6 +773,8 @@
     for n in range(planes - 1):
         source = lax.rem(me + planes - 1 - n, planes)
         remote(metas.at[source], metas.at[source], me_s.at[n], me_r.at[n], kp).wait_recv()
+    for load in loads[1:]:
+        load.wait()
     gather.other_core(0)
     dispatch(0)
     work(0, 1)

time: 261 us -> 258 us (0.989)
  no operation moved by 1% of the time
where the time goes in v9:
time: 258 us; the launch traced here: 254 us
  Pallas kernels  253 us (98%)
    pallas_call x1, Pallas kernels, run_ffn(): pl.pallas_call(functools.partial(ffn_kernel, cap), out_shape=(shape((tok,...  111 us
    pallas_call x1, Pallas kernels, run_back(): pl.pallas_call(back_kernel, out_shape=(shape((tok, width), BF16), shape((...  97.7 us
    pallas_call x1, Pallas kernels, run_front(): pl.pallas_call(functools.partial(front_kernel, cap), out_shape=(shape((to...  40 us

profile of v9, /device:TPU:0, one launch (start us, length us, event | category | flops | bytes accessed | tf_op | source)
XLA Modules:
  0.0 253.7 jit_solution(2896972154942271681)
XLA Ops:
  0.6 40.0 %shard_map.196 = (bf16[256,1536]{1,0:T(8,128)(2,1)}, bf16[256,1536]{1,0:T(8,128)(2,1)}, bf16[1024,512]{1,0:T(8,128)(2,1)}, f32[16,256]{1,0:T(8,128)}, bf16[256,1...) custom-call(s32[1,8]{1,0:T(1,128)} %span.3, ...), custom_call_target="tpu_custom_call" | custom-call | flops 5000000000 | bytes 20000000 | tf_op jit(solution)/shard_map/pallas_call | solution.py:634
  40.6 110.7 %shard_map.197 = (bf16[256,1536]{1,0:T(8,128)(2,1)}, f32[256,1536]{1,0:T(8,128)}, f32[8,256]{1,0:T(8,128)}, bf16[4,4,96,1280]{3,2,1,0:T(8,128)(2,1)}, bf16[4,96,...) custom-call(bf16[256,1536]{1,0:T(8,128)(2,1)} %get-tuple-element.39.ffn_h.ffn_in_h, ...), custom_call_target="tpu_custom_call" | custom-call | flops 24999999488 | bytes 50000000 | tf_op jit(solution)/shard_map/pallas_call | solution.py:895
  151.3 97.7 %shard_map.198 = (bf16[256,1536]{1,0:T(8,128)(2,1)}, bf16[48,2176]{1,0:T(8,128)(2,1)}, bf16[48,1536]{1,0:T(8,128)(2,1)}, bf16[4,96,640]{2,1,0:T(8,128)(2,1)}, bf16[4,96,640]{2,1,0:T(8,128)(2,1)}) custom-call(s32[1,8]{1,0:T(1,128)} %span.3, f32[8,8,256]{2,1,0:T(8,128)} %get-tuple-element.42.meta, f32[8,256]{1,0:T(8,128)} %get-tuple-element.44.gg, ...), custom_call_target="tpu_custom_call" | custom-call | flops 12000000000 | bytes 60000000 | tf_op jit(solution)/shard_map/pallas_call | solution.py:1264
  249.0 4.4 %shard_map.199 = (bf16[256,1536]{1,0:T(8,128)(2,1)}, bf16[256,1536]{1,0:T(8,128)(2,1)}, f32[48]{0:T(128)}, f32[48]{0:T(128)}, f32[48,2048]{1,0:T(8,128)}, /*inde...) custom-call(bf16[256,1536]{1,0:T(8,128)(2,1)} %get-tuple-element.43.output_h, ...), custom_call_target="tpu_custom_call" | custom-call | tf_op jit(solution)/shard_map/pallas_call | solution.py:1410

commit v10 on v9

--- a/solution.py
+++ b/solution.py
@@ -297,7 +297,7 @@
 
 
 class ExpertLine:
-    def __init__(self, spot, ref, at, cols, buf, s, r, fin, spread, a_s, a_r):
+    def __init__(self, spot, ref, at, cols, buf, s, r, fin, spread=None, a_s=None, a_r=None):
         self.spot, self.ref, self.at, self.cols = spot, ref, at, cols
         self.fin, self.spread, self.a_s, self.a_r = fin, spread, a_s, a_r
         self.line = Line(spot, self.own, self.adder, buf, s, r)
@@ -321,6 +321,8 @@
                 self.fin[cc] = plus(self.piece(cc, spot.z), *(x[cc] for x in came))
 
         self.line.final(put)
+        if self.spread is None:
+            return
         for step in range(1, spot.ctx):
             cc = lax.rem(spot.c + step, spot.ctx)
             remote(
@@ -331,8 +333,11 @@
                 (spot.e, cc, spot.z),
             ).start()
 
-    def done(self, out):
+    def done(self, out=None):
         spot = self.spot
+        if self.spread is None:
+            self.line.done()
+            return
         for step in range(1, spot.ctx):
             cc = lax.rem(spot.c + spot.ctx - step, spot.ctx)
             got = remote(
@@ -669,10 +674,10 @@
     )(span, hidden, cot, gain_one, freqs, gain_two, router_t, ids_t, turn_t, wqkv, wout)
 
 
-def ffn_kernel(cap, ffn_h, resid_h, cot_h, meta, win_h, wdn_h, output, pg_out, gg_out, gwin_h, ex_out, first_out, *scratch):
+def ffn_kernel(cap, ffn_h, resid_h, cot_h, meta, win_h, wdn_h, output, pg_out, gg_out, gwin_h, ex_out, *scratch):
     agb, metas, cotb, win, wdn, xs, ds, hid, igs, pgs, ggs, ggr, wint, gwdn = scratch[:14]
     load_sem, ag_s, ag_r, me_s, me_r, gg_s, gg_r, out_s, out_r = scratch[14:23]
-    plane_refs, line_refs, first_refs = scratch[23:29], scratch[29:36], scratch[36:]
+    plane_refs, line_refs, first_refs = scratch[23:29], scratch[29:32], scratch[32:]
     spot = Spot()
     c, k, me = spot.c, spot.k, spot.me
     kp = spot.kp
@@ -704,9 +709,9 @@
         [agb.at[2 * i + 1 - k] for i in range(4)],
         low=OUT_LOW,
     )
-    line = ExpertLine(spot, gwdn, 0, ff, *line_refs)
-    some = first_out.shape[2]
-    first_line = ExpertLine(spot, win, 0, some, *first_refs)
+    line = ExpertLine(spot, gwdn, 0, ff, *line_refs, ex_out.at[:, :, pl.ds(0, ff)])
+    some = ex_out.shape[2] - ff
+    first_line = ExpertLine(spot, win, 0, some, *first_refs, ex_out.at[:, :, pl.ds(ff, some)])
     gather = Gather(spot, agb.at[me], agb, ag_s, ag_r)
     for step, (other, dev) in enumerate(others):
         remote(meta.at[other], metas.at[me], me_s.at[step], me_r.at[step], dev).start()
@@ -877,8 +882,8 @@
         remote(ggs.at[other], ggr.at[other], gg_s.at[n], gg_r.at[n], dev).wait_send()
     plane.done()
     outs.done()
-    line.done(ex_out)
-    first_line.done(first_out)
+    line.done()
+    first_line.done()
 
 
 def run_ffn(cap, ffn, resid, cot_all, meta, win, wdn, parts, some):
@@ -899,11 +904,10 @@
             shape((tok, width), F32),
             shape((planes, tok), F32),
             shape((ctx, parts, piece, 2 * ff - some), BF16),
-            shape((ctx, piece, ff), BF16),
-            shape((ctx, piece, some), BF16),
+            shape((ctx, piece, ff + some), BF16),
         ),
         in_specs=[anyspace, anyspace, anyspace, vm, anyspace, anyspace],
-        out_specs=(vm, vm, vm, anyspace, vm, vm),
+        out_specs=(vm, vm, vm, anyspace, vm),
         scratch_shapes=[
             pltpu.VMEM((planes, tok, width), BF16),
             pltpu.VMEM((planes, 8, tok), F32),
@@ -930,8 +934,8 @@
             dma((10,)),
         ]
         + plane_scratch(tok, width)
-        + expert_scratch(ctx, parts, piece, ff)
-        + expert_scratch(ctx, parts, piece, some),
+        + line_scratch(parts, (ctx, piece, ff))
+        + line_scratch(parts, (ctx, piece, some)),
         compiler_params=pltpu.CompilerParams(
             collective_id=1, has_side_effects=True, vmem_limit_bytes=63 * 2**20
         ),
@@ -952,6 +956,7 @@
     router_t,
     gain_two,
     gain_one,
+    reduced,
     resid_h,
     cot_h,
     pg_h,
@@ -965,6 +970,7 @@
     proj_out,
     one_out,
     two_out,
+    ffn_out,
     *scratch,
 ):
     wide_f, back, low, attg, mixed, weights, gwin, send, bsend, smalls, total, out_red = scratch[:12]
@@ -975,6 +981,7 @@
     e_refs, b_refs = scratch[32:38], scratch[38:44]
     qkv_refs, proj_refs = scratch[44:47], scratch[47:50]
     one_refs, two_refs = scratch[50:57], scratch[57:64]
+    f_s, f_r = scratch[64:]
     spot = Spot()
     c, k, z, ctx = spot.c, spot.k, spot.z, spot.ctx
     tok, width = attended.shape
@@ -1000,6 +1007,10 @@
     ]
     wout_load = load(wout_h, weights.at[:, pl.ds(0, width)], 5)
     greet([spot.xp, spot.yp, spot.kp, spot.yk], spot.along())
+    for n in range(1, ctx):
+        cc = lax.rem(c + n, ctx)
+        remote(reduced.at[cc], ffn_out.at[c], f_s.at[n - 1], f_r.at[n - 1], (spot.e, cc, z)).start()
+    ffn_out[c] = reduced[c]
     one = ExpertLine(spot, gwin, 0, cols, *one_refs)
     two = ExpertLine(spot, gwin, cols, cols, *two_refs)
     proj_plane = plane_of(spot, p_zcr, p_zk, p_rx, p_ry, p_s, p_r, low=BACK_LOW)
@@ -1242,12 +1253,17 @@
         kv_copy(g, kvs.at[g, flip_c], 2, spot.yp).wait_send()
     qkv_line.final(lambda *came: put_shared(qkv_out, total, came))
     qkv_line.done()
+    for n in range(1, ctx):
+        cc = lax.rem(c + ctx - n, ctx)
+        got = remote(ffn_out.at[cc], ffn_out.at[cc], f_s.at[n - 1], f_r.at[n - 1], spot.kp)
+        got.wait_recv()
+        got.wait_send()
     two.done(two_out)
 
 
 def run_back(
     span, meta, gg, lse, trig, kv, queries, attended, normed, router_t, gain_two, gain_one,
-    resid, cot, pg, ffn_in, hidden, wout, wqkv, gwin,
+    reduced, resid, cot, pg, ffn_in, hidden, wout, wqkv, gwin,
 ):
     tok, width = attended.shape
     seq, kv_cols = kv.shape
@@ -1269,9 +1285,10 @@
             shape((piece, width), BF16),
             shape((ctx, rows, cols), BF16),
             shape((ctx, rows, cols), BF16),
+            shape(reduced.shape, BF16),
         ),
-        in_specs=[sm] + [vm] * 11 + [anyspace] * 8,
-        out_specs=(vm,) * 5,
+        in_specs=[sm] + [vm] * 12 + [anyspace] * 8,
+        out_specs=(vm,) * 6,
         scratch_shapes=[
             pltpu.VMEM((tok, width), F32),
             pltpu.VMEM((tok, width), F32),
@@ -1303,14 +1320,15 @@
         + line_scratch(parts, (piece, width + rest))
         + line_scratch(parts, (piece, width))
         + expert_scratch(ctx, parts, rows, cols)
-        + expert_scratch(ctx, parts, rows, cols),
+        + expert_scratch(ctx, parts, rows, cols)
+        + [dma((ctx - 1,)), dma((ctx - 1,))],
         compiler_params=pltpu.CompilerParams(
             collective_id=2, has_side_effects=True, vmem_limit_bytes=63 * 2**20
         ),
         cost_estimate=pl.CostEstimate(flops=12 * 10**9, bytes_accessed=60 * 10**6, transcendentals=4 * 10**6),
     )(
         span, meta, gg, lse, trig, kv, queries, attended, normed, router_t, gain_two, gain_one,
-        resid, cot, pg, ffn_in, hidden, wout, wqkv, gwin,
+        reduced, resid, cot, pg, ffn_in, hidden, wout, wqkv, gwin,
     )
 
 
@@ -1320,7 +1338,6 @@
     input_h,
     qkv_h,
     proj_h,
-    first_h,
     one_h,
     two_h,
     down_h,
@@ -1335,7 +1352,6 @@
     down,
     low_qkv,
     low_proj,
-    low_first,
     low_one,
     low_two,
     low_down,
@@ -1352,7 +1368,6 @@
         for i, (src, dst) in enumerate(
             (
                 (down_h, low_down),
-                (first_h, low_first),
                 (one_h, low_one),
                 (two_h, low_two),
                 (qkv_h, low_qkv),
@@ -1365,11 +1380,13 @@
     for copy in loads:
         copy.start()
     loads[0].wait()
-    down_full[...] = low_down[...].astype(F32)
+    ff = down.shape[2]
+    down_full[...] = low_down[:, :, :ff].astype(F32)
+    at = low_down.shape[2] - ff
+    inner_full[:, :, :at] = low_down[:, :, ff:].astype(F32)
     whole.append(pltpu.make_async_copy(down_full, down, out_sem.at[2]))
     whole[-1].start()
-    at = 0
-    for load, low in zip(loads[1:4], (low_first, low_one, low_two)):
+    for load, low in zip(loads[1:3], (low_one, low_two)):
         load.wait()
         size = low.shape[2]
         inner_full[:, :, at : at + size] = low[...].astype(F32)
@@ -1377,10 +1394,10 @@
     whole.append(pltpu.make_async_copy(inner_full, inner, out_sem.at[3]))
     whole[-1].start()
     for i, (low, to) in enumerate(((low_out, output), (low_in, input_grad))):
-        loads[6 + i].wait()
+        loads[5 + i].wait()
         whole.append(pltpu.make_async_copy(low, to, out_sem.at[i]))
         whole[-1].start()
-    for load in loads[4:6]:
+    for load in loads[3:5]:
         load.wait()
     wide = qkv.shape[1]
     qkv[...] = low_qkv[:, :wide].astype(F32)
@@ -1402,9 +1419,10 @@
         copy.wait()
 
 
-def run_finish(n_experts, output, input_grad, qkv, proj, first, one, two, down):
+def run_finish(n_experts, output, input_grad, qkv, proj, one, two, down):
     piece, width = proj.shape
-    ctx, rows, ff = down.shape
+    ctx, rows, cols = one.shape
+    ff = (down.shape[2] + 2 * cols) // 3
     shape = jax.ShapeDtypeStruct
     vm, anyspace = pl.BlockSpec(memory_space=pltpu.VMEM), pl.BlockSpec(memory_space=pl.ANY)
     return pl.pallas_call(
@@ -1420,17 +1438,17 @@
             shape((ctx, rows, 2 * ff), F32),
             shape((ctx, rows, ff), F32),
         ),
-        in_specs=[anyspace] * 8,
+        in_specs=[anyspace] * 7,
         out_specs=(anyspace, anyspace, vm, vm, vm, vm, vm, anyspace, anyspace),
-        scratch_shapes=[pltpu.VMEM(x.shape, BF16) for x in (qkv, proj, first, one, two, down, output, input_grad)]
+        scratch_shapes=[pltpu.VMEM(x.shape, BF16) for x in (qkv, proj, one, two, down, output, input_grad)]
         + [
             pltpu.VMEM((ctx, rows, 2 * ff), F32),
             pltpu.VMEM((ctx, rows, ff), F32),
-            pltpu.SemaphoreType.DMA((8,)),
+            pltpu.SemaphoreType.DMA((7,)),
             pltpu.SemaphoreType.DMA((4,)),
         ],
         compiler_params=pltpu.CompilerParams(vmem_limit_bytes=56 * 2**20),
-    )(output, input_grad, qkv, proj, first, one, two, down)
+    )(output, input_grad, qkv, proj, one, two, down)
 
 
 def local(
@@ -1474,10 +1492,10 @@
         ctx,
         planes,
     )
-    output, pair_sum, gate_grad, gwin, down, in_first = run_ffn(
+    output, pair_sum, gate_grad, gwin, reduced = run_ffn(
         capacity, ffn_in, resid, cot_all, meta, in_weight, down_weight, parts, ff // 3
     )
-    input_grad, qkv_sum, proj_sum, in_one, in_two = run_back(
+    input_grad, qkv_sum, proj_sum, in_one, in_two, ffn_sums = run_back(
         span_order,
         meta,
         gate_grad,
@@ -1490,6 +1508,7 @@
         router_t,
         gain_ffn,
         gain_attn,
+        reduced,
         resid,
         cot,
         pair_sum,
@@ -1500,7 +1519,7 @@
         gwin,
     )
     output, input_grad, gain_one, gain_two, qkv_grad, proj_grad, router_grad, inner_grad, down_grad = run_finish(
-        n_experts, output, input_grad, qkv_sum, proj_sum, in_first, in_one, in_two, down
+        n_experts, output, input_grad, qkv_sum, proj_sum, in_one, in_two, ffn_sums
     )
     return (
         output[None],

time: 258 us -> 256 us (level)
    pallas_call x1, Pallas kernels: 111 us -> 107 us  [run_ffn(): pl.pallas_call(functools.partial(ffn_kernel, cap), out_shape=(shape((tok,...]
where the time goes in v10:
time: 256 us; the launch traced here: 252 us
  Pallas kernels  251 us (98%)
    pallas_call x1, Pallas kernels, run_ffn(): pl.pallas_call(functools.partial(ffn_kernel, cap), out_shape=(shape((tok,...  107 us
    pallas_call x1, Pallas kernels, run_back(): pl.pallas_call(back_kernel, out_shape=(shape((tok, width), BF16), shape((...  98.9 us
    pallas_call x1, Pallas kernels, run_front(): pl.pallas_call(functools.partial(front_kernel, cap), out_shape=(shape((to...  40 us

profile of v10, /device:TPU:0, one launch (start us, length us, event | category | flops | bytes accessed | tf_op | source)
XLA Modules:
  0.0 251.5 jit_solution(3323916493065429180)
XLA Ops:
  0.6 40.0 %shard_map.196 = (bf16[256,1536]{1,0:T(8,128)(2,1)}, bf16[256,1536]{1,0:T(8,128)(2,1)}, bf16[1024,512]{1,0:T(8,128)(2,1)}, f32[16,256]{1,0:T(8,128)}, bf16[256,1...) custom-call(s32[1,8]{1,0:T(1,128)} %span.3, ...), custom_call_target="tpu_custom_call" | custom-call | flops 5000000000 | bytes 20000000 | tf_op jit(solution)/shard_map/pallas_call | solution.py:639
  40.6 107.3 %shard_map.197 = (bf16[256,1536]{1,0:T(8,128)(2,1)}, f32[256,1536]{1,0:T(8,128)}, f32[8,256]{1,0:T(8,128)}, bf16[4,4,96,1280]{3,2,1,0:T(8,128)(2,1)}, bf16[4,96,1024]{2,1,0:T(8,128)(2,1)}) custom-call(bf16[256,1536]{1,0:T(8,128)(2,1)} %get-tuple-element.39.ffn_h.ffn_in_h, f32[256,1536]{1,0:T(8,128)} %get-tuple-element.40.resid_h, ...), custom_call_target="tpu_custom_call" | custom-call | flops 24999999488 | bytes 50000000 | tf_op jit(solution)/shard_map/pallas_call | solution.py:900
  147.9 98.9 %shard_map.198 = (bf16[256,1536]{1,0:T(8,128)(2,1)}, bf16[48,2176]{1,0:T(8,128)(2,1)}, bf16[48,1536]{1,0:T(8,128)(2,1)}, bf16[4,96,640]{2,1,0:T(8,128)(2,1)}, bf...) custom-call(s32[1,8]{1,0:T(1,128)} %span.3, f32[8,8,256]{2,1,0:T(8,128)} %get-tuple-element.42.meta, ...), custom_call_target="tpu_custom_call" | custom-call | flops 12000000000 | bytes 60000000 | tf_op jit(solution)/shard_map/pallas_call | solution.py:1280
  246.8 4.5 %shard_map.199 = (bf16[256,1536]{1,0:T(8,128)(2,1)}, bf16[256,1536]{1,0:T(8,128)(2,1)}, f32[48]{0:T(128)}, f32[48]{0:T(128)}, f32[48,2048]{1,0:T(8,128)}, /*inde...) custom-call(bf16[256,1536]{1,0:T(8,128)(2,1)} %get-tuple-element.43.output_h, ...), custom_call_target="tpu_custom_call" | custom-call | tf_op jit(solution)/shard_map/pallas_call | solution.py:1428

commit v11 on v10

--- a/solution.py
+++ b/solution.py
@@ -864,7 +864,6 @@
     line.step(3)
     outs.turn()
     first_line.step(2)
-    line.final()
     for rows, terms in outs.total():
         output[rows, :] = (pg_out[rows, :] + summed(terms)).astype(BF16)
     for rows, terms in plane.total():
@@ -875,6 +874,7 @@
     for p in range(planes):
         gg_out[p : p + 1, :] = ggr[p, 0:1, :]
     first_line.step(3)
+    line.final()
     first_line.final()
     gwin_copy.wait()
     for n, (other, dev) in enumerate(others):
@@ -949,14 +949,14 @@
     gg,
     lse,
     trig,
-    kv,
-    queries,
     attended,
-    normed,
     router_t,
     gain_two,
     gain_one,
     reduced,
+    kv_h,
+    queries_h,
+    normed_h,
     resid_h,
     cot_h,
     pg_h,
@@ -981,7 +981,7 @@
     e_refs, b_refs = scratch[32:38], scratch[38:44]
     qkv_refs, proj_refs = scratch[44:47], scratch[47:50]
     one_refs, two_refs = scratch[50:57], scratch[57:64]
-    f_s, f_r = scratch[64:]
+    f_s, f_r, kv, queries, normed = scratch[64:]
     spot = Spot()
     c, k, z, ctx = spot.c, spot.k, spot.z, spot.ctx
     tok, width = attended.shape
@@ -1006,6 +1006,7 @@
         load(ffn_in_h, attg, 4),
     ]
     wout_load = load(wout_h, weights.at[:, pl.ds(0, width)], 5)
+    later = [load(kv_h, kv, 6), load(queries_h, queries, 7), load(normed_h, normed, 8)]
     greet([spot.xp, spot.yp, spot.kp, spot.yk], spot.along())
     for n in range(1, ctx):
         cc = lax.rem(c + n, ctx)
@@ -1092,6 +1093,9 @@
             plane.give(q, send.at[q, theirs, at])
 
     start_plane(proj_plane, pl.ds(0, width))
+
+    for copy in later:
+        copy.wait()
 
     seq = kv.shape[0]
     spans = span.shape[1]
@@ -1262,8 +1266,8 @@
 
 
 def run_back(
-    span, meta, gg, lse, trig, kv, queries, attended, normed, router_t, gain_two, gain_one,
-    reduced, resid, cot, pg, ffn_in, hidden, wout, wqkv, gwin,
+    span, meta, gg, lse, trig, attended, router_t, gain_two, gain_one, reduced, kv, queries, normed,
+    resid, cot, pg, ffn_in, hidden, wout, wqkv, gwin,
 ):
     tok, width = attended.shape
     seq, kv_cols = kv.shape
@@ -1287,7 +1291,7 @@
             shape((ctx, rows, cols), BF16),
             shape(reduced.shape, BF16),
         ),
-        in_specs=[sm] + [vm] * 12 + [anyspace] * 8,
+        in_specs=[sm] + [vm] * 9 + [anyspace] * 11,
         out_specs=(vm,) * 6,
         scratch_shapes=[
             pltpu.VMEM((tok, width), F32),
@@ -1309,7 +1313,7 @@
             pltpu.VMEM((seq, HEAD), F32),
             pltpu.VMEM((KV_HEADS, ctx, tok, 2 * HEAD), BF16),
             pltpu.VMEM((KV_HEADS, 3, tok, 2 * HEAD), BF16),
-            dma((6,)),
+            dma((9,)),
             dma((KV_HEADS, 3)),
             dma((KV_HEADS, 3)),
         ]
@@ -1321,14 +1325,15 @@
         + line_scratch(parts, (piece, width))
         + expert_scratch(ctx, parts, rows, cols)
         + expert_scratch(ctx, parts, rows, cols)
-        + [dma((ctx - 1,)), dma((ctx - 1,))],
+        + [dma((ctx - 1,)), dma((ctx - 1,))]
+        + [pltpu.VMEM(kv.shape, BF16), pltpu.VMEM(queries.shape, BF16), pltpu.VMEM(normed.shape, BF16)],
         compiler_params=pltpu.CompilerParams(
             collective_id=2, has_side_effects=True, vmem_limit_bytes=63 * 2**20
         ),
         cost_estimate=pl.CostEstimate(flops=12 * 10**9, bytes_accessed=60 * 10**6, transcendentals=4 * 10**6),
     )(
-        span, meta, gg, lse, trig, kv, queries, attended, normed, router_t, gain_two, gain_one,
-        reduced, resid, cot, pg, ffn_in, hidden, wout, wqkv, gwin,
+        span, meta, gg, lse, trig, attended, router_t, gain_two, gain_one, reduced, kv, queries, normed,
+        resid, cot, pg, ffn_in, hidden, wout, wqkv, gwin,
     )
 
 
@@ -1501,14 +1506,14 @@
         gate_grad,
         lse,
         trig,
-        kv,
-        queries,
         attended,
-        normed,
         router_t,
         gain_ffn,
         gain_attn,
         reduced,
+        kv,
+        queries,
+        normed,
         resid,
         cot,
         pair_sum,

time: 256 us -> 256 us (level)
  no operation moved by 1% of the time
where the time goes in v11:
time: 256 us; the launch traced here: 251 us
  Pallas kernels  250 us (98%)
    pallas_call x1, Pallas kernels, run_ffn(): pl.pallas_call(functools.partial(ffn_kernel, cap), out_shape=(shape((tok,...  107 us
    pallas_call x1, Pallas kernels, run_back(): pl.pallas_call(back_kernel, out_shape=(shape((tok, width), BF16), shape((...  98.1 us
    pallas_call x1, Pallas kernels, run_front(): pl.pallas_call(functools.partial(front_kernel, cap), out_shape=(shape((to...  40 us

profile of v11, /device:TPU:0, one launch (start us, length us, event | category | flops | bytes accessed | tf_op | source)
XLA Modules:
  0.0 250.8 jit_solution(15455025433634923135)
XLA Ops:
  0.6 40.0 %shard_map.196 = (bf16[256,1536]{1,0:T(8,128)(2,1)}, bf16[256,1536]{1,0:T(8,128)(2,1)}, bf16[1024,512]{1,0:T(8,128)(2,1)}, f32[16,256]{1,0:T(8,128)}, bf16[256,1...) custom-call(s32[1,8]{1,0:T(1,128)} %span.3, ...), custom_call_target="tpu_custom_call" | custom-call | flops 5000000000 | bytes 20000000 | tf_op jit(solution)/shard_map/pallas_call | solution.py:639
  40.6 107.3 %shard_map.197 = (bf16[256,1536]{1,0:T(8,128)(2,1)}, f32[256,1536]{1,0:T(8,128)}, f32[8,256]{1,0:T(8,128)}, bf16[4,4,96,1280]{3,2,1,0:T(8,128)(2,1)}, bf16[4,96,1024]{2,1,0:T(8,128)(2,1)}) custom-call(bf16[256,1536]{1,0:T(8,128)(2,1)} %get-tuple-element.39.ffn_h.ffn_in_h, f32[256,1536]{1,0:T(8,128)} %get-tuple-element.40.resid_h, ...), custom_call_target="tpu_custom_call" | custom-call | flops 24999999488 | bytes 50000000 | tf_op jit(solution)/shard_map/pallas_call | solution.py:900
  147.9 98.1 %shard_map.198 = (bf16[256,1536]{1,0:T(8,128)(2,1)}, bf16[48,2176]{1,0:T(8,128)(2,1)}, bf16[48,1536]{1,0:T(8,128)(2,1)}, bf16[4,96,640]{2,1,0:T(8,128)(2,1)}, bf...) custom-call(s32[1,8]{1,0:T(1,128)} %span.3, f32[8,8,256]{2,1,0:T(8,128)} %get-tuple-element.42.meta, ...), custom_call_target="tpu_custom_call" | custom-call | flops 12000000000 | bytes 60000000 | tf_op jit(solution)/shard_map/pallas_call | solution.py:1284
  246.0 4.5 %shard_map.199 = (bf16[256,1536]{1,0:T(8,128)(2,1)}, bf16[256,1536]{1,0:T(8,128)(2,1)}, f32[48]{0:T(128)}, f32[48]{0:T(128)}, f32[48,2048]{1,0:T(8,128)}, /*inde...) custom-call(bf16[256,1536]{1,0:T(8,128)(2,1)} %get-tuple-element.43.output_h, ...), custom_call_target="tpu_custom_call" | custom-call | tf_op jit(solution)/shard_map/pallas_call | solution.py:1433

commit v12 on v11

--- a/solution.py
+++ b/solution.py
@@ -674,10 +674,11 @@
     )(span, hidden, cot, gain_one, freqs, gain_two, router_t, ids_t, turn_t, wqkv, wout)
 
 
-def ffn_kernel(cap, ffn_h, resid_h, cot_h, meta, win_h, wdn_h, output, pg_out, gg_out, gwin_h, ex_out, *scratch):
+def ffn_kernel(cap, ffn_h, resid_h, cot_h, meta, win_h, wdn_h, output_h, pg_h, gg_out, gwin_h, ex_out, *scratch):
     agb, metas, cotb, win, wdn, xs, ds, hid, igs, pgs, ggs, ggr, wint, gwdn = scratch[:14]
     load_sem, ag_s, ag_r, me_s, me_r, gg_s, gg_r, out_s, out_r = scratch[14:23]
-    plane_refs, line_refs, first_refs = scratch[23:29], scratch[29:32], scratch[32:]
+    plane_refs, line_refs, first_refs = scratch[23:29], scratch[29:32], scratch[32:35]
+    output, pg_out = scratch[35:]
     spot = Spot()
     c, k, me = spot.c, spot.k, spot.me
     kp = spot.kp
@@ -866,8 +867,12 @@
     first_line.step(2)
     for rows, terms in outs.total():
         output[rows, :] = (pg_out[rows, :] + summed(terms)).astype(BF16)
+    early = [pltpu.make_async_copy(output, output_h, load_sem.at[1])]
+    early[0].start()
     for rows, terms in plane.total():
         pg_out[rows, :] = summed(terms)
+    early.append(pltpu.make_async_copy(pg_out, pg_h, load_sem.at[2]))
+    early[1].start()
     for n in range(planes - 1):
         source = lax.rem(me + planes - 1 - n, planes)
         remote(ggr.at[source], ggr.at[source], gg_s.at[n], gg_r.at[n], kp).wait_recv()
@@ -877,6 +882,8 @@
     line.final()
     first_line.final()
     gwin_copy.wait()
+    for copy in early:
+        copy.wait()
     for n, (other, dev) in enumerate(others):
         remote(meta.at[other], metas.at[other], me_s.at[n], me_r.at[n], dev).wait_send()
         remote(ggs.at[other], ggr.at[other], gg_s.at[n], gg_r.at[n], dev).wait_send()
@@ -907,7 +914,7 @@
             shape((ctx, piece, ff + some), BF16),
         ),
         in_specs=[anyspace, anyspace, anyspace, vm, anyspace, anyspace],
-        out_specs=(vm, vm, vm, anyspace, vm),
+        out_specs=(anyspace, anyspace, vm, anyspace, vm),
         scratch_shapes=[
             pltpu.VMEM((planes, tok, width), BF16),
             pltpu.VMEM((planes, 8, tok), F32),
@@ -935,7 +942,8 @@
         ]
         + plane_scratch(tok, width)
         + line_scratch(parts, (ctx, piece, ff))
-        + line_scratch(parts, (ctx, piece, some)),
+        + line_scratch(parts, (ctx, piece, some))
+        + [pltpu.VMEM((tok, width), BF16), pltpu.VMEM((tok, width), F32)],
         compiler_params=pltpu.CompilerParams(
             collective_id=1, has_side_effects=True, vmem_limit_bytes=63 * 2**20
         ),

time: 256 us -> 255 us (level)
  no operation moved by 1% of the time
where the time goes in v12:
time: 255 us; the launch traced here: 250 us
  Pallas kernels  249 us (98%)
    pallas_call x1, Pallas kernels, run_ffn(): pl.pallas_call(functools.partial(ffn_kernel, cap), out_shape=(shape((tok,...  106 us
    pallas_call x1, Pallas kernels, run_back(): pl.pallas_call(back_kernel, out_shape=(shape((tok, width), BF16), shape((...  98.1 us
    pallas_call x1, Pallas kernels, run_front(): pl.pallas_call(functools.partial(front_kernel, cap), out_shape=(shape((to...  40 us

profile of v12, /device:TPU:0, one launch (start us, length us, event | category | flops | bytes accessed | tf_op | source)
XLA Modules:
  0.0 249.9 jit_solution(12308903963525535421)
XLA Ops:
  0.6 40.0 %shard_map.196 = (bf16[256,1536]{1,0:T(8,128)(2,1)}, bf16[256,1536]{1,0:T(8,128)(2,1)}, bf16[1024,512]{1,0:T(8,128)(2,1)}, f32[16,256]{1,0:T(8,128)}, bf16[256,1...) custom-call(s32[1,8]{1,0:T(1,128)} %span.3, ...), custom_call_target="tpu_custom_call" | custom-call | flops 5000000000 | bytes 20000000 | tf_op jit(solution)/shard_map/pallas_call | solution.py:639
  40.6 106.3 %shard_map.197 = (bf16[256,1536]{1,0:T(8,128)(2,1)}, f32[256,1536]{1,0:T(8,128)}, f32[8,256]{1,0:T(8,128)}, bf16[4,4,96,1280]{3,2,1,0:T(8,128)(2,1)}, bf16[4,96,1024]{2,1,0:T(8,128)(2,1)}) custom-call(bf16[256,1536]{1,0:T(8,128)(2,1)} %get-tuple-element.39.ffn_h.ffn_in_h, f32[256,1536]{1,0:T(8,128)} %get-tuple-element.40.resid_h, ...), custom_call_target="tpu_custom_call" | custom-call | flops 24999999488 | bytes 50000000 | tf_op jit(solution)/shard_map/pallas_call | solution.py:907
  147.0 98.1 %shard_map.198 = (bf16[256,1536]{1,0:T(8,128)(2,1)}, bf16[48,2176]{1,0:T(8,128)(2,1)}, bf16[48,1536]{1,0:T(8,128)(2,1)}, bf16[4,96,640]{2,1,0:T(8,128)(2,1)}, bf...) custom-call(s32[1,8]{1,0:T(1,128)} %span.3, f32[8,8,256]{2,1,0:T(8,128)} %get-tuple-element.42.meta, ...), custom_call_target="tpu_custom_call" | custom-call | flops 12000000000 | bytes 60000000 | tf_op jit(solution)/shard_map/pallas_call | solution.py:1292
  245.1 4.5 %shard_map.199 = (bf16[256,1536]{1,0:T(8,128)(2,1)}, bf16[256,1536]{1,0:T(8,128)(2,1)}, f32[48]{0:T(128)}, f32[48]{0:T(128)}, f32[48,2048]{1,0:T(8,128)}, /*inde...) custom-call(bf16[256,1536]{1,0:T(8,128)(2,1)} %get-tuple-element.43.output_h, ...), custom_call_target="tpu_custom_call" | custom-call | tf_op jit(solution)/shard_map/pallas_call | solution.py:1441
